TPU v7x, 32 devices: a whole 2x2x4 slice. The times are simulated.
32 devices in a mesh: snap: 8 (over z, x), mesh: 4 (over y, core).
Axes of the slice: x: 2, y: 2, z: 4, core: 2. Of those that a mesh axis runs over, the one named last changes fastest.
Arguments:
- snapshots: float32 [12288, 1024], P('mesh', 'snap'), may hold values from -6 to 6
- region_ids: int32 [24, 512], P('mesh'), may hold values from 0 to 7
- conductivity: float32 [8], replicated, may hold values from 0.2 to 5
Outputs:
- gram: float32 [1024, 1024], P('snap', 'mesh')
All inputs are finite; a program needn't handle non-finite values.
Results may differ from a plain program's by a relative error of at most 0.0003.
Values sent between devices are 32-bit elements; how exact they have to be, the bound alone decides.
No kernel may reach another device: no remote copies, remote signals or barrier semaphores. Data moves between devices by JAX's collectives and lax.ppermute only.
A program may use at most 128 MiB of HBM per device.

v0:
```python
import math

import jax
import jax.numpy as jnp
from jax import lax
from jax.sharding import PartitionSpec as P


def passed_along(value, axis, steps):
    count = lax.axis_size(axis)
    first, last = (max(0, -steps), min(count, count - steps))
    return lax.ppermute(value, axis, [(source, source + steps) for source in range(first, last)])


def from_behind(block, axis, distance):
    devices = range(lax.axis_size(axis))
    route = [((i - distance) % len(devices), i) for i in devices]
    return lax.ppermute(block, axis, route)


def weights_of(region_ids, conductivity):
    table = jnp.arange(conductivity.shape[0], dtype=jnp.int32)
    picked = jnp.where(
        region_ids[:, :, None] == table[None, None, :],
        conductivity[None, None, :],
        jnp.zeros((), conductivity.dtype),
    )
    return jnp.sum(picked, axis=-1) / 36.0


def element_terms(field, below, weight):
    lower = jnp.concatenate([field, below[None]], 0)
    padded = jnp.pad(lower, ((0, 0), (0, 1), (0, 0)))
    corner_a = padded[:-1, :-1]
    corner_b = padded[:-1, 1:]
    corner_e = padded[1:, :-1]
    corner_d = padded[1:, 1:]
    scaled = weight[:, :, None]
    to_a = scaled * (4.0 * corner_a + 2.0 * corner_b + 2.0 * corner_e + corner_d)
    to_b = scaled * (2.0 * corner_a + 4.0 * corner_b + corner_e + 2.0 * corner_d)
    to_e = scaled * (2.0 * corner_a + corner_b + 4.0 * corner_e + 2.0 * corner_d)
    to_d = scaled * (corner_a + 2.0 * corner_b + 2.0 * corner_e + 4.0 * corner_d)
    total = jnp.pad(to_a, ((0, 1), (0, 1), (0, 0))) + jnp.pad(to_b, ((0, 1), (1, 0), (0, 0)))
    total = (
        total + jnp.pad(to_e, ((1, 0), (0, 1), (0, 0))) + jnp.pad(to_d, ((1, 0), (1, 0), (0, 0)))
    )
    return total


def contract(left, right):
    return lax.dot_general(
        left,
        right,
        (((0,), (0,)), ((), ())),
        precision=lax.Precision.HIGHEST,
        preferred_element_type=jnp.float32,
    )


def local(snapshots, region_ids, conductivity):
    strip, width = region_ids.shape
    node_rows, group_cols = snapshots.shape
    field = snapshots.reshape(strip, width, group_cols)
    weight = weights_of(region_ids, conductivity)
    below = passed_along(field[0], "mesh", -1)
    total = element_terms(field, below, weight)
    carried = passed_along(total[strip, :width], "mesh", 1)
    inner = total[:strip, :width]
    panel = jnp.concatenate([inner[:1] + carried[None], inner[1:]], 0).reshape(
        node_rows, group_cols
    )
    count = lax.axis_size("snap")
    group = lax.axis_index("snap")
    reach = count // 2

    def place(partial_value, moving, step):
        tile = contract(snapshots, moving)
        source = (group - step) % count * group_cols
        return lax.dynamic_update_slice(partial_value, tile, (jnp.int32(0), source))

    partial_value = place(jnp.zeros((group_cols, group_cols * count), jnp.float32), panel, 0)

    def turn(step, carry):
        moving, partial_value = carry
        moving = from_behind(moving, "snap", 1)
        return (moving, place(partial_value, moving, step))

    _, partial_value = lax.fori_loop(1, reach + 1, turn, (panel, partial_value))
    blocks = jnp.transpose(partial_value.reshape(group_cols, count, group_cols), (1, 2, 0))
    target = jnp.arange(count, dtype=jnp.int32)
    offset = (group - target) % count
    valid = (offset >= 1) & (offset <= count - 1 - reach)
    outgoing = jnp.where(valid[:, None, None], blocks, jnp.zeros((), jnp.float32))
    incoming = lax.all_to_all(outgoing, "snap", split_axis=0, concat_axis=0, tiled=True)
    partial_value = partial_value + jnp.transpose(incoming, (1, 0, 2)).reshape(
        group_cols, count * group_cols
    )
    summed = lax.psum_scatter(partial_value, "mesh", scatter_dimension=1, tiled=True)
    total_nodes = node_rows * lax.axis_size("mesh")
    return summed / math.sqrt(total_nodes)


def solution(mesh):
    return jax.shard_map(
        local,
        mesh=mesh,
        in_specs=(P("mesh", "snap"), P("mesh", None), P()),
        out_specs=P("snap", "mesh"),
        check_vma=False,
    )
```

profile of v0, /device:TPU:8, one launch (start us, length us, event | category | flops | bytes accessed | tf_op | source)
XLA Modules:
  0.0 243.2 jit_solution(4092860514584894099)
XLA Ops:
  6.5 0.0 reduce-scatter.2.cloned.1.call-start
  6.5 1.0 slice.28
  7.5 1.3 collective-permute-start.1
  8.8 0.8 select_reduce_fusion
  9.7 1.3 collective-permute-done.1
  10.9 0.0 copy-start
  10.9 1.6 pad_maximum_fusion
  12.6 0.2 copy-done
  12.8 0.6 add_multiply_fusion.3
  13.5 0.0 copy-start.5
  13.5 1.3 add_multiply_fusion.2
  14.7 0.0 copy-start.1
  14.7 0.0 copy-start.3
  14.7 0.0 copy-done.5
  14.8 1.1 copy-done.1
  15.9 0.5 copy-done.3
  16.4 6.8 %collective-permute-start.2 = (f32[512,128]{1,0:T(8,128)S(1)}, f32[512,128]{1,0:T(8,128)}, u32[]{:S(2)}, u32[]{:S(2)}) collective-permute-start(f32[512,128]{1,0:T(8,128)S(1)} %add_bitcast_fusion), channel_id=1, source_target_pairs={{0,1},{1,2},{2,3},{4,5},{5,6},{6,7},{8,9},{9,10},{10,11},{12,13},{... | collective-permute-start | bytes 786440 | tf_op jit(solution)/shard_map/ppermute | solution.py:12
  23.2 0.0 copy-start.2
  23.2 0.0 copy-start.4
  23.2 0.0 copy-start.6
  23.2 2.6 %pad_add_fusion = f32[5,512,128]{2,1,0:T(8,128)S(1)} fusion(f32[6,512,128]{2,1,0:T(8,128)} %copy-done.3, f32[6,512,128]{2,1,0:T(8,128)} %copy-done.1, f32[6,512,128]{2,1,0:T(8,128)S(1)} %get-tuple-element.151, f32[6,512,128]{2,1,0:T(8,128)} %copy-done.5), kind=kLoop, calls=%fused_computation.12 | loop fusion | flops 983040 | bytes 7602176 | tf_op jit(solution)/shard_map/add | solution.py:45
  25.8 0.0 collective-permute-done.2
  25.8 0.0 copy-done.2
  25.8 0.5 copy-done.4
  26.2 0.5 copy-done.6
  26.7 1.0 add_add_fusion
  27.7 0.1 pad_maximum_fusion.1
  27.8 0.0 copy-start.7
  27.8 1.2 copy-done.7
  29.0 2.7 %convolution_bitcast_fusion = f32[128,128]{0,1:T(8,128)S(1)} fusion(f32[3072,128]{1,0:T(8,128)S(1)} %bitcast.27, f32[3072,128]{1,0:T(8,128)S(1)} %copy-done), kind=kOutput, calls=%fused_computation.15 | convolution fusion | flops 603979776 | bytes 3211264 | tf_op jit(solution)/shard_map/dot_general | solution.py:51
  31.7 0.1 copy.13
  31.9 0.0 copy-start.8
  31.9 0.8 copy-done.8
  32.7 160.0 %while.17 = (s32[]{:T(128)}, f32[3072,128]{1,0:T(8,128)}, f32[128,1024]{1,0:T(8,128)}, f32[3072,128]{1,0:T(8,128)S(1)}, s32[]{:T(128)}, /*index=5*/s32[]{:T(128)...) while((s32[]{:T(128)}, f32[3072,128]{1,0:T(8,128)}, f32[128,1024]{1,0:T(8,128)}, ...), condition=%wide.region_2.3_spmd, body=%wide.region_1.2_spmd.sunk | while | flops 603979776 | bytes 12648768 | solution.py:88
  32.7 1.5 collective-permute-start
  34.2 35.2 %collective-permute-done = f32[3072,128]{1,0:T(8,128)S(1)} collective-permute-done((f32[3072,128]{1,0:T(8,128)}, f32[3072,128]{1,0:T(8,128)S(1)}, u32[]{:S(2)}, u32[]{:S(2)}) %collective-permute-start) | collective-permute-done | bytes 1572896 | tf_op jit(solution)/shard_map/while/body/eval_jaxpr/ppermute | solution.py:18
  69.4 1.2 copy.27
  70.6 3.3 %convolution_dynamic-update-slice_fusion.2 = f32[128,1024]{1,0:T(8,128)} fusion(f32[128,1024]{1,0:T(8,128)} %get-tuple-element.198, s32[]{:T(128)S(6)} %select_n.72, f32[3072,128]{1,0:T(8,128)S(1)} %get-tuple-element.210, f32[3072,128]{1,0:T(8,128)S(1)} %collective-permute-done), kind=kOutput, calls=%fused_computation.clone.1 | convolution fusion | flops 603979776 | bytes 3211268 | tf_op jit(solution)/shard_map/while/body/eval_jaxpr/dot_general | solution.py:51
  73.8 0.6 collective-permute-start
  74.4 35.2 %collective-permute-done = f32[3072,128]{1,0:T(8,128)S(1)} collective-permute-done((f32[3072,128]{1,0:T(8,128)}, f32[3072,128]{1,0:T(8,128)S(1)}, u32[]{:S(2)}, u32[]{:S(2)}) %collective-permute-start) | collective-permute-done | bytes 1572896 | tf_op jit(solution)/shard_map/while/body/eval_jaxpr/ppermute | solution.py:18
  109.6 1.2 copy.27
  110.8 3.3 %convolution_dynamic-update-slice_fusion.2 = f32[128,1024]{1,0:T(8,128)} fusion(f32[128,1024]{1,0:T(8,128)} %get-tuple-element.198, s32[]{:T(128)S(6)} %select_n.72, f32[3072,128]{1,0:T(8,128)S(1)} %get-tuple-element.210, f32[3072,128]{1,0:T(8,128)S(1)} %collective-permute-done), kind=kOutput, calls=%fused_computation.clone.1 | convolution fusion | flops 603979776 | bytes 3211268 | tf_op jit(solution)/shard_map/while/body/eval_jaxpr/dot_general | solution.py:51
  114.1 0.0 collective-permute-start
  114.1 34.9 %collective-permute-done = f32[3072,128]{1,0:T(8,128)S(1)} collective-permute-done((f32[3072,128]{1,0:T(8,128)}, f32[3072,128]{1,0:T(8,128)S(1)}, u32[]{:S(2)}, u32[]{:S(2)}) %collective-permute-start) | collective-permute-done | bytes 1572896 | tf_op jit(solution)/shard_map/while/body/eval_jaxpr/ppermute | solution.py:18
  149.0 1.2 copy.27
  150.1 3.3 %convolution_dynamic-update-slice_fusion.2 = f32[128,1024]{1,0:T(8,128)} fusion(f32[128,1024]{1,0:T(8,128)} %get-tuple-element.198, s32[]{:T(128)S(6)} %select_n.72, f32[3072,128]{1,0:T(8,128)S(1)} %get-tuple-element.210, f32[3072,128]{1,0:T(8,128)S(1)} %collective-permute-done), kind=kOutput, calls=%fused_computation.clone.1 | convolution fusion | flops 603979776 | bytes 3211268 | tf_op jit(solution)/shard_map/while/body/eval_jaxpr/dot_general | solution.py:51
  153.4 0.0 collective-permute-start
  153.4 34.8 %collective-permute-done = f32[3072,128]{1,0:T(8,128)S(1)} collective-permute-done((f32[3072,128]{1,0:T(8,128)}, f32[3072,128]{1,0:T(8,128)S(1)}, u32[]{:S(2)}, u32[]{:S(2)}) %collective-permute-start) | collective-permute-done | bytes 1572896 | tf_op jit(solution)/shard_map/while/body/eval_jaxpr/ppermute | solution.py:18
  188.2 1.2 copy.27
  189.4 3.3 %convolution_dynamic-update-slice_fusion.2 = f32[128,1024]{1,0:T(8,128)} fusion(f32[128,1024]{1,0:T(8,128)} %get-tuple-element.198, s32[]{:T(128)S(6)} %select_n.72, f32[3072,128]{1,0:T(8,128)S(1)} %get-tuple-element.210, f32[3072,128]{1,0:T(8,128)S(1)} %collective-permute-done), kind=kOutput, calls=%fused_computation.clone.1 | convolution fusion | flops 603979776 | bytes 3211268 | tf_op jit(solution)/shard_map/while/body/eval_jaxpr/dot_general | solution.py:51
  192.6 1.2 copy.16
  193.9 0.1 select_bitcast_fusion
  194.0 19.3 %all_to_all.5 = f32[8,128,128]{2,1,0:T(8,128)S(1)} all-to-all(f32[8,128,128]{2,1,0:T(8,128)S(1)} %select_bitcast_fusion), channel_id=1, replica_groups=mesh['snap'=8,'mesh'=4] {'snap'}, dimensions={0} | all-to-all | bytes 1048576 | tf_op jit(solution)/shard_map/all_to_all | solution.py:94
  213.3 0.2 copy.15
  213.5 0.9 bitcast_add_fusion
  214.3 0.0 reduce-scatter.2.cloned.1.call-update
  214.4 20.3 %reduce-scatter.2.cloned.1.call-done = f32[128,256]{0,1:T(8,128)} async-done(((f32[128,1024]{0,1:T(8,128)}), f32[128,256]{0,1:T(8,128)}) %reduce-scatter.2.cloned.1.call-update) | async-done | bytes 131088 | tf_op jit(solution)/shard_map/reduce_scatter | solution.py:98
  234.7 0.9 broadcast_multiply_fusion
  235.6 0.8 copy.17
  (5 shorter events, 0.1 us)
Async XLA Ops:
  6.5 228.1 %reduce-scatter.2.cloned.1.call-start = ((), (), s32[]{:S(2)}) async-start(), calls=%async_computation.2 | async-start | bytes 655360 | tf_op jit(solution)/shard_map/reduce_scatter | solution.py:98
  7.5 3.4 %collective-permute-start.1 = (f32[512,128]{1,0:T(8,128)S(1)}, f32[512,128]{1,0:T(8,128)S(1)}, u32[]{:S(2)}, u32[]{:S(2)}) collective-permute-start(f32[512,128]{1,0:T(8,128)S(1)} %slice.28), channel_id=1, source_target_pairs={{1,0},{2,1},{3,2},{5,4},{6,5},{7,6},{9,8},{10,9},{11,10},{13,12},{... | collective-permute-start | bytes 786440 | tf_op jit(solution)/shard_map/ppermute | solution.py:12
  10.9 1.9 copy-start
  13.5 1.3 copy-start.5
  14.7 1.1 copy-start.1
  14.7 1.6 copy-start.3
  16.4 9.4 %collective-permute-start.2 = (f32[512,128]{1,0:T(8,128)S(1)}, f32[512,128]{1,0:T(8,128)}, u32[]{:S(2)}, u32[]{:S(2)}) collective-permute-start(f32[512,128]{1,0:T(8,128)S(1)} %add_bitcast_fusion), channel_id=1, source_target_pairs={{0,1},{1,2},{2,3},{4,5},{5,6},{6,7},{8,9},{9,10},{10,11},{12,13},{... | collective-permute-start | bytes 786440 | tf_op jit(solution)/shard_map/ppermute | solution.py:12
  23.2 2.6 %copy-start.2 = (f32[6,512,128]{2,1,0:T(8,128)S(1)}, f32[6,512,128]{2,1,0:T(8,128)}, u32[]{:S(2)}) copy-start(f32[6,512,128]{2,1,0:T(8,128)} %copy-done.1) | copy-start | bytes 4718596
  23.2 3.1 %copy-start.4 = (f32[6,512,128]{2,1,0:T(8,128)S(1)}, f32[6,512,128]{2,1,0:T(8,128)}, u32[]{:S(2)}) copy-start(f32[6,512,128]{2,1,0:T(8,128)} %copy-done.3) | copy-start | bytes 4718596
  23.2 3.5 %copy-start.6 = (f32[6,512,128]{2,1,0:T(8,128)S(1)}, f32[6,512,128]{2,1,0:T(8,128)}, u32[]{:S(2)}) copy-start(f32[6,512,128]{2,1,0:T(8,128)} %copy-done.5) | copy-start | bytes 4718596
  27.8 1.2 copy-start.7
  31.9 0.8 copy-start.8
  32.7 36.7 %collective-permute-start = (f32[3072,128]{1,0:T(8,128)}, f32[3072,128]{1,0:T(8,128)S(1)}, u32[]{:S(2)}, u32[]{:S(2)}) collective-permute-start(f32[3072,128]{1,0:T(8,128)} %get-tuple-element.197), channel_id=1, source_target_pairs={{28,0},{0,4},{4,8},{8,12},{12,16},{16,20},{20,24},{24,28},{29,1},{... | collective-permute-start | bytes 4718600 | tf_op jit(solution)/shard_map/while/body/eval_jaxpr/ppermute | solution.py:18
  73.8 35.8 %collective-permute-start = (f32[3072,128]{1,0:T(8,128)}, f32[3072,128]{1,0:T(8,128)S(1)}, u32[]{:S(2)}, u32[]{:S(2)}) collective-permute-start(f32[3072,128]{1,0:T(8,128)} %get-tuple-element.197), channel_id=1, source_target_pairs={{28,0},{0,4},{4,8},{8,12},{12,16},{16,20},{20,24},{24,28},{29,1},{... | collective-permute-start | bytes 4718600 | tf_op jit(solution)/shard_map/while/body/eval_jaxpr/ppermute | solution.py:18
  114.1 34.9 %collective-permute-start = (f32[3072,128]{1,0:T(8,128)}, f32[3072,128]{1,0:T(8,128)S(1)}, u32[]{:S(2)}, u32[]{:S(2)}) collective-permute-start(f32[3072,128]{1,0:T(8,128)} %get-tuple-element.197), channel_id=1, source_target_pairs={{28,0},{0,4},{4,8},{8,12},{12,16},{16,20},{20,24},{24,28},{29,1},{... | collective-permute-start | bytes 4718600 | tf_op jit(solution)/shard_map/while/body/eval_jaxpr/ppermute | solution.py:18
  153.4 34.8 %collective-permute-start = (f32[3072,128]{1,0:T(8,128)}, f32[3072,128]{1,0:T(8,128)S(1)}, u32[]{:S(2)}, u32[]{:S(2)}) collective-permute-start(f32[3072,128]{1,0:T(8,128)} %get-tuple-element.197), channel_id=1, source_target_pairs={{28,0},{0,4},{4,8},{8,12},{12,16},{16,20},{20,24},{24,28},{29,1},{... | collective-permute-start | bytes 4718600 | tf_op jit(solution)/shard_map/while/body/eval_jaxpr/ppermute | solution.py:18
Sparse Core Ops, SparseCore 0:
  214.5 20.1 reduce-scatter.1
where the time goes:
time: 245 us; the launch traced here: 243 us
  waiting for transfers between devices  162 us (66%)
  blocking collectives  19.3 us (8%)
  matrix products  15.8 us (6%)
  between operations  13.6 us (6%)
  local copies, waits for them, and re-layouts  12.7 us (5%)
  starting transfers between devices  10.2 us (4%)
  other arithmetic  9.95 us (4%)
    ppermute x4, waiting for transfers between devices, from_behind(): return lax.ppermute(block, axis, route)  140 us
    reduce_scatter x1, waiting for transfers between devices, local(): lax.psum_scatter(partial_value, 'mesh', scatter_dimension=1, tiled=True)  20.3 us
    all_to_all x1, blocking collectives, local(): lax.all_to_all(outgoing, 'snap', split_axis=0, concat_axis=0, tiled=True)  19.3 us
    dot_general x5, matrix products, contract(): lax.dot_general(left, right, (((0,), (0,)), ((), ())), precision=lax.Prec...  15.8 us
    ppermute x2, starting transfers between devices, passed_along(): lax.ppermute(value, axis, [(source, source + steps) for source in range(f...  8.08 us
  transfers between devices with their start and end apart: 7, of which 6 were waited for; matrix products, arithmetic and copies ran while one was open for 1% of the time, Pallas kernels for 0%

commit v1 on v0

--- a/solution.py
+++ b/solution.py
@@ -3,6 +3,9 @@
 import jax
 import jax.numpy as jnp
 from jax import lax
+from jax.experimental import pallas as pl
+from jax.experimental.pallas import tpu as pltpu
+from jax.sharding import Mesh
 from jax.sharding import PartitionSpec as P
 
 
@@ -57,7 +60,7 @@
     )
 
 
-def local(snapshots, region_ids, conductivity):
+def local_ring(snapshots, region_ids, conductivity):
     strip, width = region_ids.shape
     node_rows, group_cols = snapshots.shape
     field = snapshots.reshape(strip, width, group_cols)
@@ -100,11 +103,260 @@
     return summed / math.sqrt(total_nodes)
 
 
+ALL = ("h", "l", "x", "y", "c")
+PLACE = ("l", "x")
+TILE = ("y", "c")
+GROUP = 128
+STRIP = 128
+SEAM = 16
+
+
+def flat(h, l, x, y, c):
+    return (((h * 2 + l) * 2 + x) * 2 + y) * 2 + c
+
+
+def crossing(outer, flip):
+    pairs = []
+    for h in range(2):
+        l = h if outer else 1 - h
+        for x in range(2):
+            for y in range(2):
+                for c in range(2):
+                    pairs.append((flat(h, l, x, y, c), flat(1 - h, h, x ^ flip, y, c)))
+    return pairs
+
+
+def split(value):
+    high = value.astype(jnp.bfloat16)
+    return high, (value - high.astype(jnp.float32)).astype(jnp.bfloat16)
+
+
+def product(left_high, left_low, right_high, right_low):
+    def one(a, b):
+        return lax.dot_general(
+            a, b, (((0,), (0,)), ((), ())), preferred_element_type=jnp.float32
+        )
+
+    return one(left_high, right_high) + one(left_high, right_low) + one(left_low, right_high)
+
+
+def own_kernel(
+    rows, seam_ref, field_ref, above_ref, below_ref, weight_ref, high_ref, low_ref, gram_ref, sh, sl
+):
+    wide = STRIP + 16
+    line_number = lax.broadcasted_iota(jnp.int32, (SEAM, GROUP), 0)
+
+    def line(main, left, right):
+        return jnp.concatenate(
+            [
+                jnp.broadcast_to(left, (8, GROUP)),
+                main,
+                jnp.broadcast_to(right, (8, GROUP)),
+            ],
+            0,
+        )
+
+    def halo(ref, g):
+        return line(ref[g, :STRIP], ref[g, STRIP : STRIP + 1], ref[g, STRIP + 1 : STRIP + 2])
+
+    body = rows * STRIP
+    for g in range(4):
+        columns = slice(g * GROUP, (g + 1) * GROUP)
+        before = halo(above_ref, g)
+        before_up = pltpu.roll(before, wide - 1, 0)
+        carried = carried_next = None
+        seam = jnp.zeros((SEAM, GROUP), jnp.float32)
+        for r in range(-1, rows):
+            if r + 1 < rows:
+                main = field_ref[g, (r + 1) * STRIP : (r + 2) * STRIP]
+                after = line(
+                    main,
+                    field_ref[g, body + r + 1 : body + r + 2],
+                    field_ref[g, body + 8 + r + 1 : body + 8 + r + 2],
+                )
+                high, low = split(main)
+                sh[(r + 1) * STRIP : (r + 2) * STRIP, columns] = high
+                sl[(r + 1) * STRIP : (r + 2) * STRIP, columns] = low
+            else:
+                after = halo(below_ref, g)
+            after_up = pltpu.roll(after, wide - 1, 0)
+            weight = weight_ref[r + 1]
+            top, top_up = 2.0 * before + after, 2.0 * before_up + after_up
+            to_a, to_b = weight * (2.0 * top + top_up), weight * (top + 2.0 * top_up)
+            if r >= 0:
+                from_left = pltpu.roll(to_b + carried_next, 1, 0)
+                total = to_a + carried + from_left
+                beside = (
+                    seam_ref[0] * from_left[8 + STRIP : 9 + STRIP] + seam_ref[1] * from_left[8:9]
+                )
+                seam = jnp.where(line_number == r, beside, seam)
+                high, low = split(total[8 : 8 + STRIP])
+                high_ref[r * STRIP : (r + 1) * STRIP, columns] = high
+                low_ref[r * STRIP : (r + 1) * STRIP, columns] = low
+            low_end, low_up = before + 2.0 * after, before_up + 2.0 * after_up
+            carried = weight * (2.0 * low_end + low_up)
+            carried_next = weight * (low_end + 2.0 * low_up)
+            before, before_up = after, after_up
+        high, low = split(seam)
+        high_ref[body : body + SEAM, columns] = high
+        low_ref[body : body + SEAM, columns] = low
+    for a in range(2):
+        left = slice(a * 256, (a + 1) * 256)
+        for b in range(2):
+            right = slice(b * 256, (b + 1) * 256)
+            tile = product(
+                sh[:, left], sl[:, left], high_ref[:body, right], low_ref[:body, right]
+            )
+            for i in range(2):
+                for j in range(2):
+                    gram_ref[(2 * a + i) * 4 + 2 * b + j] = tile[
+                        i * GROUP : (i + 1) * GROUP, j * GROUP : (j + 1) * GROUP
+                    ]
+
+
+def cross_kernel(place_ref, high_ref, low_ref, s0, s1, s2, s3, gram_ref):
+    for pair, (first, second) in enumerate(((s0, s1), (s2, s3))):
+        h0, l0 = split(first[...])
+        h1, l1 = split(second[...])
+        sh = jnp.concatenate([h0, h1], 1)
+        sl = jnp.concatenate([l0, l1], 1)
+        for a in range(2):
+            left = slice(a * 256, (a + 1) * 256)
+            tile = product(high_ref[:, left], low_ref[:, left], sh, sl)
+            for i in range(2):
+                for j in range(2):
+                    gram_ref[(2 * a + i) * 4 + place_ref[2 * pair + j]] = tile[
+                        i * GROUP : (i + 1) * GROUP, j * GROUP : (j + 1) * GROUP
+                    ]
+
+
+VMEM = pl.BlockSpec(memory_space=pltpu.VMEM)
+SMEM = pl.BlockSpec(memory_space=pltpu.SMEM)
+
+
+def local_strips(snapshots, region_ids, conductivity):
+    rows, width = region_ids.shape
+    nodes = rows * STRIP
+    field = snapshots.reshape(rows, width, GROUP)
+    h, l, x, y, c = (lax.axis_index(a) for a in ALL)
+
+    seam = jnp.concatenate(
+        [field[:, 2 * STRIP], jnp.zeros((SEAM - rows, GROUP), jnp.float32)], 0
+    )
+
+    def strip_at(t):
+        main = lax.dynamic_slice_in_dim(field, t * STRIP, STRIP, 1).reshape(nodes, GROUP)
+        return jnp.concatenate([main, seam], 0)
+
+    far_same = strip_at(2 * (1 - h) + x)
+    far_flip = strip_at(2 * (1 - h) + (1 - x))
+    near = [lax.ppermute(far_same, ALL, crossing(False, 0)), lax.ppermute(far_flip, ALL, crossing(False, 1))]
+
+    none = jnp.zeros((rows, GROUP), jnp.float32)
+    pad = jnp.zeros((8 - rows, GROUP), jnp.float32)
+    pieces = []
+    for t in (2, 3, 0, 1):
+        left = field[:, t * STRIP - 1] if t > 0 else none
+        right = field[:, (t + 1) * STRIP] if t < 3 else none
+        main = field[:, t * STRIP : (t + 1) * STRIP].reshape(nodes, GROUP)
+        pieces.append(jnp.concatenate([main, left, pad, right, pad], 0))
+    own = lax.all_to_all(jnp.stack(pieces), PLACE, 0, 0, tiled=True)
+
+    far_same, far_flip, own, *near = lax.optimization_barrier((far_same, far_flip, own, *near))
+    far = [lax.ppermute(far_same, ALL, crossing(True, 0)), lax.ppermute(far_flip, ALL, crossing(True, 1))]
+
+    def edge(r):
+        return jnp.concatenate(
+            [
+                own[:, r * STRIP : (r + 1) * STRIP],
+                own[:, nodes + r : nodes + r + 1],
+                own[:, nodes + 8 + r : nodes + 8 + r + 1],
+                jnp.zeros((4, 6, GROUP), jnp.float32),
+            ],
+            1,
+        )
+
+    above = lax.ppermute(edge(rows - 1), TILE, [(m, m + 1) for m in range(3)])
+    below = lax.ppermute(edge(0), TILE, [(m + 1, m) for m in range(3)])
+
+    total_nodes = snapshots.shape[0] * 4
+    weight = weights_of(region_ids, conductivity) / math.sqrt(total_nodes)
+    weight_above = lax.ppermute(weight[rows - 1 :], TILE, [(m, m + 1) for m in range(3)])
+    weight = jnp.pad(jnp.concatenate([weight_above, weight], 0), ((0, 0), (8, 8)))
+    weight = lax.dynamic_slice_in_dim(weight, (2 * (1 - l) + x) * STRIP, STRIP + 16, 1)
+    weight = jnp.broadcast_to(weight[:, :, None], (rows + 1, STRIP + 16, GROUP))
+
+    blocks = jax.ShapeDtypeStruct((16, GROUP, GROUP), jnp.float32)
+    half_float = jax.ShapeDtypeStruct((nodes + SEAM, 4 * GROUP), jnp.bfloat16)
+    seam_side = jnp.stack([(h == 0) & (x == 1), (h == 1) & (x == 0)]).astype(jnp.float32)
+    seam_side = seam_side * jnp.array([1.0, -1.0], jnp.float32)
+    high, low, own_blocks = pl.pallas_call(
+        lambda *refs: own_kernel(rows, *refs),
+        out_shape=(half_float, half_float, blocks),
+        in_specs=[SMEM] + [VMEM] * 4,
+        out_specs=(VMEM,) * 3,
+        scratch_shapes=[pltpu.VMEM((nodes, 4 * GROUP), jnp.bfloat16)] * 2,
+        compiler_params=pltpu.CompilerParams(vmem_limit_bytes=40 * 1024 * 1024),
+        cost_estimate=pl.CostEstimate(
+            flops=6 * nodes * 512 * 512, bytes_accessed=6 * 1024 * 1024, transcendentals=0
+        ),
+    )(seam_side, own, above, below, weight)
+
+    place = jnp.stack([2 * h + x, 2 * h + (1 - x), 2 * (1 - h) + x, 2 * (1 - h) + (1 - x)])
+    cross_blocks = pl.pallas_call(
+        cross_kernel,
+        out_shape=blocks,
+        in_specs=[SMEM] + [VMEM] * 6,
+        out_specs=VMEM,
+        compiler_params=pltpu.CompilerParams(vmem_limit_bytes=40 * 1024 * 1024),
+        cost_estimate=pl.CostEstimate(
+            flops=6 * nodes * 512 * 512, bytes_accessed=5 * 1024 * 1024, transcendentals=0
+        ),
+    )(place.astype(jnp.int32), high, low, *near, *far)
+
+    def gathered(parts):
+        return jnp.sum(lax.all_to_all(parts, PLACE + TILE, 0, 0, tiled=True), 0)
+
+    own_block = gathered(own_blocks)
+    cross_block = gathered(cross_blocks)
+    swap = []
+    for half in range(2):
+        for i in range(4):
+            for m in range(4):
+                swap.append((half * 16 + i * 4 + m, (1 - half) * 16 + m * 4 + i))
+    cross_block = cross_block + lax.ppermute(cross_block, ALL, swap).T
+
+    first = jnp.where(h == 0, own_block, cross_block)
+    last = jnp.where(h == 0, cross_block, own_block)
+    one = jnp.where(c == 0, first, last)
+    two = jnp.where(c == 0, last, first)
+    one = lax.ppermute(one, TILE, [(0, 0), (1, 2), (2, 1), (3, 3)])
+    two = lax.ppermute(two, TILE, [(0, 2), (1, 0), (2, 3), (3, 1)])
+    return jnp.where(
+        y == 0, jnp.concatenate([one, two], 1), jnp.concatenate([two, one], 1)
+    )
+
+
 def solution(mesh):
-    return jax.shard_map(
-        local,
-        mesh=mesh,
-        in_specs=(P("mesh", "snap"), P("mesh", None), P()),
-        out_specs=P("snap", "mesh"),
-        check_vma=False,
-    )
+    sizes = (mesh.shape["snap"], mesh.shape["mesh"])
+
+    def whole(snapshots, region_ids, conductivity):
+        width = region_ids.shape[1]
+        if sizes == (8, 4) and snapshots.shape[1] == 8 * GROUP and width == 4 * STRIP:
+            parts = Mesh(mesh.devices.reshape(2, 2, 2, 2, 2), ALL)
+            return jax.shard_map(
+                local_strips,
+                mesh=parts,
+                in_specs=(P(TILE, ("h", "l", "x")), P(TILE, None), P()),
+                out_specs=P(("h", "l", "x"), TILE),
+                check_vma=False,
+            )(snapshots, region_ids, conductivity)
+        return jax.shard_map(
+            local_ring,
+            mesh=mesh,
+            in_specs=(P("mesh", "snap"), P("mesh", None), P()),
+            out_specs=P("snap", "mesh"),
+            check_vma=False,
+        )(snapshots, region_ids, conductivity)
+
+    return whole

time: 245 us -> 111 us (0.45)
  the two profiles are of different devices: /device:TPU:8 before, /device:TPU:25 now
where the time goes in v1:
time: 111 us
  starting transfers between devices  40.7 us (37%)
  waiting for transfers between devices  33.5 us (30%)
  blocking collectives  20.6 us (19%)
  Pallas kernels  7.64 us (7%)
  other arithmetic  4.27 us (4%)
  local copies, waits for them, and re-layouts  3.77 us (3%)
    all_to_all x1, blocking collectives, gathered(): return jnp.sum(lax.all_to_all(parts, PLACE + TILE, 0, 0, tiled=True), 0)  20.6 us
    all_to_all x1, waiting for transfers between devices, local_strips(): own = lax.all_to_all(jnp.stack(pieces), PLACE, 0, 0, tiled=True)  12.9 us
    all_to_all x1, waiting for transfers between devices, gathered(): return jnp.sum(lax.all_to_all(parts, PLACE + TILE, 0, 0, tiled=True), 0)  11.6 us
    ppermute x1, starting transfers between devices, local_strips(): lax.ppermute(far_same, ALL, crossing(True, 0))  10.5 us
    all_to_all x1, starting transfers between devices, gathered(): return jnp.sum(lax.all_to_all(parts, PLACE + TILE, 0, 0, tiled=True), 0)  5.76 us
    pallas_call x1, Pallas kernels, local_strips(): pl.pallas_call(lambda *refs: own_kernel(rows, *refs), out_shape=(half_flo...  5.25 us
    ppermute x1, starting transfers between devices, local_strips(): lax.ppermute(weight[rows - 1:], TILE, [(m, m + 1) for m in range(3)])  4.21 us
    ppermute x1, starting transfers between devices, local_strips(): cross_block = cross_block + lax.ppermute(cross_block, ALL, swap).T  3.95 us
  transfers between devices with their start and end apart: 12, of which 6 were waited for; matrix products, arithmetic and copies ran while one was open for 3% of the time, Pallas kernels for 5%

profile of v1, /device:TPU:25, one launch (start us, length us, event | category | flops | bytes accessed | tf_op | source)
XLA Modules:
  0.0 110.7 jit_solution(13123807548830578033)
XLA Ops:
  0.0 0.8 fusion.10
  0.9 1.8 %fusion.11 = (f32[6,128,128]{2,1,0:T(8,128)S(1)}, f32[6,128,128]{2,1,0:T(8,128)S(1)}, f32[6,128,128]{2,1,0:T(8,128)S(1)}, f32[6,128,128]{2,1,0:T(8,128)S(1)}, f3...) fusion(f32[6,512,128]{2,1,0:T(8,128)} %bitcast.38, s32[]{:T(128)S(6)} %select_n.47, s32[]{:T(128)S(6)} %select_n.46), kind=kLoop, calls=%fused_computation.38 | loop fusion | bytes 4718600 | tf_op jit(solution)/shard_map/slice | solution.py:261
  2.7 0.2 concatenate.39
  2.9 0.1 concatenate.40
  3.0 0.1 concatenate.38
  3.2 0.1 concatenate.41
  3.3 1.3 %pad_maximum_fusion = f32[4,784,128]{2,1,0:T(8,128)} fusion(f32[1,784,128]{2,1,0:T(8,128)S(1)} %bitcast.42, f32[1,784,128]{2,1,0:T(8,128)S(1)} %bitcast.40, f32[1,784,128]{2,1,0:T(8,128)S(1)} %bitcast.39, f32[1,784,128]{2,1,0:T(8,128)S(1)} %bitcast.41), kind=kLoop, calls=%fused_computation | loop fusion | flops 1204224 | bytes 3211264 | tf_op jit(solution)/shard_map/stack | solution.py:263
  4.6 3.7 %all-to-all-start = ((f32[4,784,128]{2,1,0:T(8,128)}), f32[4,784,128]{2,1,0:T(8,128)S(1)}, u32[]{:S(2)}, u32[]{:S(2)}) async-start(f32[4,784,128]{2,1,0:T(8,128)} %pad_maximum_fusion), calls=%async_computation | async-start | bytes 3211264 | tf_op jit(solution)/shard_map/all_to_all | solution.py:263
  8.3 0.0 copy-start.1
  8.3 0.0 copy-start.2
  8.3 0.1 pad.32.clone
  8.4 0.0 copy-start.3
  8.4 0.9 fusion.1
  9.3 0.0 copy-start
  9.3 0.7 collective-permute-start.1
  10.0 0.7 collective-permute-start
  10.7 0.0 copy-done.1
  10.7 0.0 copy-done.2
  10.7 0.1 select_reduce_fusion
  10.9 4.2 %collective-permute-start.4 = (f32[1,512]{1,0:T(1,128)S(1)}, f32[1,512]{1,0:T(1,128)S(1)}, u32[]{:S(2)}, u32[]{:S(2)}) collective-permute-start(f32[1,512]{1,0:T(1,128)S(1)} %slice.79), channel_id=1, source_target_pairs={{0,1},{1,2},{2,3},{4,5},{5,6},{6,7},{8,9},{9,10},{10,11},{12,13},{... | collective-permute-start | bytes 6152 | tf_op jit(solution)/shard_map/ppermute | solution.py:284
  15.1 0.1 pad.22.clone
  15.2 0.0 collective-permute-done.1.s1
  15.2 0.0 collective-permute-done.s0
  15.2 12.9 %all-to-all-done.refs_1_ = f32[4,784,128]{2,1,0:T(8,128)S(1)} async-done(((f32[4,784,128]{2,1,0:T(8,128)}), f32[4,784,128]{2,1,0:T(8,128)S(1)}, u32[]{:S(2)}, u32[]{:S(2)}) %all-to-all-start) | async-done | bytes 1605664 | tf_op jit(solution)/shard_map/all_to_all | solution.py:263
  28.1 0.0 copy-done
  28.1 10.5 %collective-permute-start.5 = (f32[784,128]{1,0:T(8,128)}, f32[784,128]{1,0:T(8,128)S(1)}, u32[]{:S(2)}, u32[]{:S(2)}) collective-permute-start(f32[784,128]{1,0:T(8,128)} %get-tuple-element.19), channel_id=1, source_target_pairs={{0,16},{1,17},{2,18},{3,19},{4,20},{5,21},{6,22},{7,23},{24,8},{25... | collective-permute-start | bytes 1204232 | tf_op jit(solution)/shard_map/ppermute | solution.py:266
  38.6 1.3 %collective-permute-start.6 = (f32[784,128]{1,0:T(8,128)}, f32[784,128]{1,0:T(8,128)S(1)}, u32[]{:S(2)}, u32[]{:S(2)}) collective-permute-start(f32[784,128]{1,0:T(8,128)} %copy-done), channel_id=1, source_target_pairs={{0,20},{1,21},{2,22},{3,23},{4,16},{5,17},{6,18},{7,19},{24,12},{2... | collective-permute-start | bytes 1204232 | tf_op jit(solution)/shard_map/ppermute | solution.py:266
  39.9 0.9 maximum_maximum_fusion.1
  40.8 3.0 %collective-permute-start.3 = (f32[4,136,128]{2,1,0:T(8,128)}, f32[4,136,128]{2,1,0:T(8,128)S(1)}, u32[]{:S(2)}, u32[]{:S(2)}) collective-permute-start(f32[4,136,128]{2,1,0:T(8,128)} %get-tuple-element.44), channel_id=1, source_target_pairs={{1,0},{2,1},{3,2},{5,4},{6,5},{7,6},{9,8},{10,9},{11,10},{13,12},{... | collective-permute-start | bytes 835592 | tf_op jit(solution)/shard_map/ppermute | solution.py:280
  43.9 3.0 %collective-permute-start.2 = (f32[4,136,128]{2,1,0:T(8,128)}, f32[4,136,128]{2,1,0:T(8,128)}, u32[]{:S(2)}, u32[]{:S(2)}) collective-permute-start(f32[4,136,128]{2,1,0:T(8,128)} %get-tuple-element.45), channel_id=1, source_target_pairs={{0,1},{1,2},{2,3},{4,5},{5,6},{6,7},{8,9},{9,10},{10,11},{12,13},{... | collective-permute-start | bytes 835592 | tf_op jit(solution)/shard_map/ppermute | solution.py:279
  46.9 0.0 copy-done.3
  46.9 0.1 add_select_fusion.refs_0_
  47.0 0.1 pad_add_fusion.place_ref
  47.1 0.0 collective-permute-done.4
  47.1 0.1 fusion.3
  47.2 2.2 %collective-permute-done.3.refs_3_ = f32[4,136,128]{2,1,0:T(8,128)S(1)} collective-permute-done((f32[4,136,128]{2,1,0:T(8,128)}, f32[4,136,128]{2,1,0:T(8,128)S(1)}, u32[]{:S(2)}, u32[]{:S(2)}) %collective-permute-start.3) | collective-permute-done | bytes 278560 | tf_op jit(solution)/shard_map/ppermute | solution.py:280
  49.4 1.3 %collective-permute-done.2.refs_2_ = f32[4,136,128]{2,1,0:T(8,128)} collective-permute-done((f32[4,136,128]{2,1,0:T(8,128)}, f32[4,136,128]{2,1,0:T(8,128)}, u32[]{:S(2)}, u32[]{:S(2)}) %collective-permute-start.2) | collective-permute-done | bytes 278560 | tf_op jit(solution)/shard_map/ppermute | solution.py:279
  50.7 0.2 broadcast_in_dim.35.refs_4_
  50.9 5.3 %shard_map.46 = (bf16[784,512]{1,0:T(8,128)(2,1)S(1)}, bf16[784,512]{1,0:T(8,128)(2,1)S(1)}, f32[16,128,128]{2,1,0:T(8,128)}) custom-call(f32[2]{0:T(128)S(1)} %add_select_fusion.refs_0_, f32[4,784,128]{2,1,0:T(8,128)S(1)} %all-to-all-done.refs_1_, f32[4,136,128]{2,1,0:T(8,128)} %collective-permute-done.2.refs_2_, ...), custom_call_target="tpu_custom_call" | custom-call | flops 1207959552 | bytes 6291456 | tf_op jit(solution)/shard_map/pallas_call | solution.py:293
  56.1 0.0 collective-permute-done.5.s2
  56.2 0.0 collective-permute-done.6.s3
  56.2 2.4 %shard_map.47 = f32[16,128,128]{2,1,0:T(8,128)S(1)} custom-call(s32[4]{0:T(128)S(1)} %pad_add_fusion.place_ref, bf16[784,512]{1,0:T(8,128)(2,1)S(1)} %get-tuple-element.15.high_ref, bf16[784,512]{1,0:T(8,128)(2,1)S(1)} %get-tuple-element.16.low_ref, f32[784,128]{1,0:T(8,128)S(1)} %collective-permute-done.s0, f32[784,128]{1,0:T(8,128)S(1)} %collective-permute-done.1.s1, ...), custom_call_target="tpu_custom_call" | custom-call | flops 1207959552 | bytes 5242880 | tf_op jit(solution)/shard_map/pallas_call | solution.py:306
  58.5 20.6 %all_to_all.15 = f32[16,128,128]{2,1,0:T(8,128)S(1)} all-to-all(f32[16,128,128]{2,1,0:T(8,128)S(1)} %shard_map.47), channel_id=1, replica_groups=mesh['h'=2,'l'=2,'x'=2,'y'=2,'c'=2] {'l','x','y','c'}, dimensions={0} | all-to-all | bytes 2097152 | tf_op jit(solution)/shard_map/all_to_all | solution.py:318
  79.2 5.8 %all-to-all-start.1 = ((f32[16,128,128]{2,1,0:T(8,128)}), f32[16,128,128]{2,1,0:T(8,128)S(1)}, u32[]{:S(2)}, u32[]{:S(2)}) async-start(f32[16,128,128]{2,1,0:T(8,128)} %get-tuple-element.14), calls=%async_computation.1 | async-start | bytes 2097152 | tf_op jit(solution)/shard_map/all_to_all | solution.py:318
  84.9 0.1 reduce_sum.29
  85.0 0.1 copy.26
  85.1 3.9 %collective-permute-start.7 = (f32[128,128]{0,1:T(8,128)S(1)}, f32[128,128]{0,1:T(8,128)S(1)}, u32[]{:S(2)}, u32[]{:S(2)}) collective-permute-start(f32[128,128]{0,1:T(8,128)S(1)} %copy.26), channel_id=1, source_target_pairs={{0,16},{1,20},{2,24},{3,28},{4,17},{5,21},{6,25},{7,29},{8,18},{9,... | collective-permute-start | bytes 196616 | tf_op jit(solution)/shard_map/ppermute | solution.py:327
  89.0 11.6 %all-to-all-done.1 = f32[16,128,128]{2,1,0:T(8,128)S(1)} async-done(((f32[16,128,128]{2,1,0:T(8,128)}), f32[16,128,128]{2,1,0:T(8,128)S(1)}, u32[]{:S(2)}, u32[]{:S(2)}) %all-to-all-start.1) | async-done | bytes 1048608 | tf_op jit(solution)/shard_map/all_to_all | solution.py:318
  100.6 0.1 reduce_sum.28
  100.7 1.8 %collective-permute-done.7 = f32[128,128]{0,1:T(8,128)S(1)} collective-permute-done((f32[128,128]{0,1:T(8,128)S(1)}, f32[128,128]{0,1:T(8,128)S(1)}, u32[]{:S(2)}, u32[]{:S(2)}) %collective-permute-start.7) | collective-permute-done | bytes 65568 | tf_op jit(solution)/shard_map/ppermute | solution.py:327
  102.5 1.9 %collective-permute-start.9 = (f32[128,128]{1,0:T(8,128)S(1)}, f32[128,128]{1,0:T(8,128)S(1)}, u32[]{:S(2)}, u32[]{:S(2)}) collective-permute-start(f32[128,128]{1,0:T(8,128)S(1)} %broadcast_select_fusion.2), channel_id=1, source_target_pairs={{0,2},{1,0},{2,3},{3,1},{4,6},{5,4},{6,7},{7,5},{8,10},{9,8},{10,1... | collective-permute-start | bytes 196616 | tf_op jit(solution)/shard_map/ppermute | solution.py:334
  104.4 1.9 %collective-permute-start.8 = (f32[128,128]{1,0:T(8,128)S(1)}, f32[128,128]{1,0:T(8,128)S(1)}, u32[]{:S(2)}, u32[]{:S(2)}) collective-permute-start(f32[128,128]{1,0:T(8,128)S(1)} %get-tuple-element.21), channel_id=1, source_target_pairs={{0,0},{1,2},{2,1},{3,3},{4,4},{5,6},{6,5},{7,7},{8,8},{9,10},{10,9... | collective-permute-start | bytes 196616 | tf_op jit(solution)/shard_map/ppermute | solution.py:333
  106.4 0.0 collective-permute-done.9
  106.4 3.6 %collective-permute-done.8 = f32[128,128]{1,0:T(8,128)S(1)} collective-permute-done((f32[128,128]{1,0:T(8,128)S(1)}, f32[128,128]{1,0:T(8,128)S(1)}, u32[]{:S(2)}, u32[]{:S(2)}) %collective-permute-start.8) | collective-permute-done | bytes 65568 | tf_op jit(solution)/shard_map/ppermute | solution.py:333
  110.0 0.7 maximum_select_fusion
  (13 shorter events, 0.1 us)
Async XLA Ops:
  4.6 23.4 %all-to-all-start = ((f32[4,784,128]{2,1,0:T(8,128)}), f32[4,784,128]{2,1,0:T(8,128)S(1)}, u32[]{:S(2)}, u32[]{:S(2)}) async-start(f32[4,784,128]{2,1,0:T(8,128)} %pad_maximum_fusion), calls=%async_computation | async-start | bytes 3211264 | tf_op jit(solution)/shard_map/all_to_all | solution.py:263
  8.3 2.4 %copy-start.1 = (s32[6,512]{1,0:T(8,128)S(1)}, s32[6,512]{1,0:T(8,128)}, u32[]{:S(2)}) copy-start(s32[6,512]{1,0:T(8,128)} %param.5) | copy-start | bytes 36868
  8.3 2.4 %copy-start.2 = (f32[8]{0:T(128)S(1)}, f32[8]{0:T(128)}, u32[]{:S(2)}) copy-start(f32[8]{0:T(128)} %param.6) | copy-start | bytes 100
  8.4 38.5 %copy-start.3 = (f32[2]{0:T(128)S(1)}, f32[2]{0:T(128)}, u32[]{:S(2)}) copy-start(f32[2]{0:T(128)} %constant.46.clone) | copy-start | bytes 28
  9.3 18.7 %copy-start = (f32[784,128]{1,0:T(8,128)}, f32[784,128]{1,0:T(8,128)S(1)}, u32[]{:S(2)}) copy-start(f32[784,128]{1,0:T(8,128)S(1)} %get-tuple-element.20) | copy-start | bytes 1204228
  9.3 5.8 %collective-permute-start.1 = (f32[784,128]{1,0:T(8,128)S(1)}, f32[784,128]{1,0:T(8,128)S(1)}, u32[]{:S(2)}, u32[]{:S(2)}) collective-permute-start(f32[784,128]{1,0:T(8,128)S(1)} %get-tuple-element.20), channel_id=1, source_target_pairs={{8,20},{9,21},{10,22},{11,23},{12,16},{13,17},{14,18},{15,19},{16,... | collective-permute-start | bytes 1204232 | tf_op jit(solution)/shard_map/ppermute | solution.py:253
  10.0 5.2 %collective-permute-start = (f32[784,128]{1,0:T(8,128)}, f32[784,128]{1,0:T(8,128)S(1)}, u32[]{:S(2)}, u32[]{:S(2)}) collective-permute-start(f32[784,128]{1,0:T(8,128)} %get-tuple-element.19), channel_id=1, source_target_pairs={{8,16},{9,17},{10,18},{11,19},{12,20},{13,21},{14,22},{15,23},{16,... | collective-permute-start | bytes 1204232 | tf_op jit(solution)/shard_map/ppermute | solution.py:253
  10.9 36.2 %collective-permute-start.4 = (f32[1,512]{1,0:T(1,128)S(1)}, f32[1,512]{1,0:T(1,128)S(1)}, u32[]{:S(2)}, u32[]{:S(2)}) collective-permute-start(f32[1,512]{1,0:T(1,128)S(1)} %slice.79), channel_id=1, source_target_pairs={{0,1},{1,2},{2,3},{4,5},{5,6},{6,7},{8,9},{9,10},{10,11},{12,13},{... | collective-permute-start | bytes 6152 | tf_op jit(solution)/shard_map/ppermute | solution.py:284
  28.1 28.0 %collective-permute-start.5 = (f32[784,128]{1,0:T(8,128)}, f32[784,128]{1,0:T(8,128)S(1)}, u32[]{:S(2)}, u32[]{:S(2)}) collective-permute-start(f32[784,128]{1,0:T(8,128)} %get-tuple-element.19), channel_id=1, source_target_pairs={{0,16},{1,17},{2,18},{3,19},{4,20},{5,21},{6,22},{7,23},{24,8},{25... | collective-permute-start | bytes 1204232 | tf_op jit(solution)/shard_map/ppermute | solution.py:266
  38.6 17.6 %collective-permute-start.6 = (f32[784,128]{1,0:T(8,128)}, f32[784,128]{1,0:T(8,128)S(1)}, u32[]{:S(2)}, u32[]{:S(2)}) collective-permute-start(f32[784,128]{1,0:T(8,128)} %copy-done), channel_id=1, source_target_pairs={{0,20},{1,21},{2,22},{3,23},{4,16},{5,17},{6,18},{7,19},{24,12},{2... | collective-permute-start | bytes 1204232 | tf_op jit(solution)/shard_map/ppermute | solution.py:266
  40.8 8.6 %collective-permute-start.3 = (f32[4,136,128]{2,1,0:T(8,128)}, f32[4,136,128]{2,1,0:T(8,128)S(1)}, u32[]{:S(2)}, u32[]{:S(2)}) collective-permute-start(f32[4,136,128]{2,1,0:T(8,128)} %get-tuple-element.44), channel_id=1, source_target_pairs={{1,0},{2,1},{3,2},{5,4},{6,5},{7,6},{9,8},{10,9},{11,10},{13,12},{... | collective-permute-start | bytes 835592 | tf_op jit(solution)/shard_map/ppermute | solution.py:280
  43.9 6.8 %collective-permute-start.2 = (f32[4,136,128]{2,1,0:T(8,128)}, f32[4,136,128]{2,1,0:T(8,128)}, u32[]{:S(2)}, u32[]{:S(2)}) collective-permute-start(f32[4,136,128]{2,1,0:T(8,128)} %get-tuple-element.45), channel_id=1, source_target_pairs={{0,1},{1,2},{2,3},{4,5},{5,6},{6,7},{8,9},{9,10},{10,11},{12,13},{... | collective-permute-start | bytes 835592 | tf_op jit(solution)/shard_map/ppermute | solution.py:279
  79.2 21.5 %all-to-all-start.1 = ((f32[16,128,128]{2,1,0:T(8,128)}), f32[16,128,128]{2,1,0:T(8,128)S(1)}, u32[]{:S(2)}, u32[]{:S(2)}) async-start(f32[16,128,128]{2,1,0:T(8,128)} %get-tuple-element.14), calls=%async_computation.1 | async-start | bytes 2097152 | tf_op jit(solution)/shard_map/all_to_all | solution.py:318
  85.1 17.4 %collective-permute-start.7 = (f32[128,128]{0,1:T(8,128)S(1)}, f32[128,128]{0,1:T(8,128)S(1)}, u32[]{:S(2)}, u32[]{:S(2)}) collective-permute-start(f32[128,128]{0,1:T(8,128)S(1)} %copy.26), channel_id=1, source_target_pairs={{0,16},{1,20},{2,24},{3,28},{4,17},{5,21},{6,25},{7,29},{8,18},{9,... | collective-permute-start | bytes 196616 | tf_op jit(solution)/shard_map/ppermute | solution.py:327
  102.5 3.9 %collective-permute-start.9 = (f32[128,128]{1,0:T(8,128)S(1)}, f32[128,128]{1,0:T(8,128)S(1)}, u32[]{:S(2)}, u32[]{:S(2)}) collective-permute-start(f32[128,128]{1,0:T(8,128)S(1)} %broadcast_select_fusion.2), channel_id=1, source_target_pairs={{0,2},{1,0},{2,3},{3,1},{4,6},{5,4},{6,7},{7,5},{8,10},{9,8},{10,1... | collective-permute-start | bytes 196616 | tf_op jit(solution)/shard_map/ppermute | solution.py:334
  104.4 5.6 %collective-permute-start.8 = (f32[128,128]{1,0:T(8,128)S(1)}, f32[128,128]{1,0:T(8,128)S(1)}, u32[]{:S(2)}, u32[]{:S(2)}) collective-permute-start(f32[128,128]{1,0:T(8,128)S(1)} %get-tuple-element.21), channel_id=1, source_target_pairs={{0,0},{1,2},{2,1},{3,3},{4,4},{5,6},{6,5},{7,7},{8,8},{9,10},{10,9... | collective-permute-start | bytes 196616 | tf_op jit(solution)/shard_map/ppermute | solution.py:333

commit v2 on v1

--- a/solution.py
+++ b/solution.py
@@ -109,6 +109,7 @@
 GROUP = 128
 STRIP = 128
 SEAM = 16
+LAST = 3
 
 
 def flat(h, l, x, y, c):
@@ -126,6 +127,29 @@
     return pairs
 
 
+def middle_groups():
+    four = [(x, y) for x in range(2) for y in range(2)]
+    groups = [[flat(h, 1 - h, x, y, c) for h in range(2) for x, y in four] for c in range(2)]
+    groups += [[flat(h, h, x, y, c) for x, y in four for c in range(2)] for h in range(2)]
+    return groups
+
+
+def owners(turn):
+    pairs = []
+    for h in range(2):
+        for x in range(2):
+            for y in range(2):
+                for c in range(2):
+                    lower = flat(0, h, x, 1, c)
+                    upper = flat(1, c, y, 0, h)
+                    down = (x + y + turn) % 2 == 0
+                    pairs.append((flat(h, 1 - h, x, y, c), lower if down else upper))
+    return pairs
+
+
+MIDDLE_GROUPS = middle_groups()
+
+
 def split(value):
     high = value.astype(jnp.bfloat16)
     return high, (value - high.astype(jnp.float32)).astype(jnp.bfloat16)
@@ -141,10 +165,24 @@
 
 
 def own_kernel(
-    rows, seam_ref, field_ref, above_ref, below_ref, weight_ref, high_ref, low_ref, gram_ref, sh, sl
+    rows,
+    side_ref,
+    seam_ref,
+    field_ref,
+    above_ref,
+    below_ref,
+    weight_ref,
+    high_ref,
+    low_ref,
+    mine_ref,
+    other_ref,
+    sh,
+    sl,
 ):
     wide = STRIP + 16
     line_number = lax.broadcasted_iota(jnp.int32, (SEAM, GROUP), 0)
+    first_core = side_ref[0] == 0
+    x, l = side_ref[2], side_ref[3]
 
     def line(main, left, right):
         return jnp.concatenate(
@@ -157,7 +195,9 @@
         )
 
     def halo(ref, g):
-        return line(ref[g, :STRIP], ref[g, STRIP : STRIP + 1], ref[g, STRIP + 1 : STRIP + 2])
+        at = g * (STRIP + 8)
+        end = at + STRIP
+        return line(ref[at:end], ref[end : end + 1], ref[end + 1 : end + 2])
 
     body = rows * STRIP
     for g in range(4):
@@ -167,20 +207,21 @@
         carried = carried_next = None
         seam = jnp.zeros((SEAM, GROUP), jnp.float32)
         for r in range(-1, rows):
-            if r + 1 < rows:
-                main = field_ref[g, (r + 1) * STRIP : (r + 2) * STRIP]
+            n = r + 1
+            if n < rows:
+                main = field_ref[g, n * STRIP : (n + 1) * STRIP]
                 after = line(
                     main,
-                    field_ref[g, body + r + 1 : body + r + 2],
-                    field_ref[g, body + 8 + r + 1 : body + 8 + r + 2],
+                    field_ref[g, body + n : body + n + 1],
+                    field_ref[g, body + 8 + n : body + 9 + n],
                 )
                 high, low = split(main)
-                sh[(r + 1) * STRIP : (r + 2) * STRIP, columns] = high
-                sl[(r + 1) * STRIP : (r + 2) * STRIP, columns] = low
+                sh[n * STRIP : (n + 1) * STRIP, columns] = high
+                sl[n * STRIP : (n + 1) * STRIP, columns] = low
             else:
                 after = halo(below_ref, g)
             after_up = pltpu.roll(after, wide - 1, 0)
-            weight = weight_ref[r + 1]
+            weight = weight_ref[r] if r >= 0 else above_ref[4 * (STRIP + 8) :]
             top, top_up = 2.0 * before + after, 2.0 * before_up + after_up
             to_a, to_b = weight * (2.0 * top + top_up), weight * (top + 2.0 * top_up)
             if r >= 0:
@@ -202,32 +243,57 @@
         low_ref[body : body + SEAM, columns] = low
     for a in range(2):
         left = slice(a * 256, (a + 1) * 256)
-        for b in range(2):
-            right = slice(b * 256, (b + 1) * 256)
-            tile = product(
+        tiles = [
+            product(
                 sh[:, left], sl[:, left], high_ref[:body, right], low_ref[:body, right]
             )
-            for i in range(2):
-                for j in range(2):
-                    gram_ref[(2 * a + i) * 4 + 2 * b + j] = tile[
-                        i * GROUP : (i + 1) * GROUP, j * GROUP : (j + 1) * GROUP
-                    ]
-
-
-def cross_kernel(place_ref, high_ref, low_ref, s0, s1, s2, s3, gram_ref):
-    for pair, (first, second) in enumerate(((s0, s1), (s2, s3))):
-        h0, l0 = split(first[...])
-        h1, l1 = split(second[...])
-        sh = jnp.concatenate([h0, h1], 1)
-        sl = jnp.concatenate([l0, l1], 1)
+            for right in (slice(0, 256), slice(256, 512))
+        ]
+        mine = jnp.where(first_core, tiles[0], tiles[1])
+        other = jnp.where(first_core, tiles[1], tiles[0])
+        for i in range(2):
+            rows_of = slice(i * GROUP, (i + 1) * GROUP)
+            mine_ref[l ^ a, x ^ i] = mine[rows_of]
+            other_ref[l ^ a, x ^ i] = other[rows_of]
+
+
+def cross_kernel(side_ref, high_ref, low_ref, *refs):
+    *pieces, mine_ref, other_ref = refs
+    core, half, x = side_ref[0], side_ref[1], side_ref[2]
+
+    def put(to_core, slot, block):
+        @pl.when(core == to_core)
+        def _():
+            mine_ref[slot] = block
+
+        @pl.when(core != to_core)
+        def _():
+            other_ref[slot] = block
+
+    for pair in range(2):
+        first, second = (
+            jnp.concatenate([pieces[k][...], pieces[k + 1][...]], 0)
+            for k in (4 * pair, 4 * pair + 2)
+        )
+        sh, sl = split(jnp.concatenate([first, second], 1))
         for a in range(2):
-            left = slice(a * 256, (a + 1) * 256)
-            tile = product(high_ref[:, left], low_ref[:, left], sh, sl)
-            for i in range(2):
-                for j in range(2):
-                    gram_ref[(2 * a + i) * 4 + place_ref[2 * pair + j]] = tile[
-                        i * GROUP : (i + 1) * GROUP, j * GROUP : (j + 1) * GROUP
-                    ]
+            own = slice(a * 256, (a + 1) * 256)
+
+            @pl.when(half == 0)
+            def _():
+                tile = product(high_ref[:, own], low_ref[:, own], sh, sl)
+                for i in range(2):
+                    for j in range(2):
+                        block = tile[i * GROUP : (i + 1) * GROUP, j * GROUP : (j + 1) * GROUP]
+                        put(pair, (2 * a + i) * 2 + (x ^ j), block)
+
+            @pl.when(half == 1)
+            def _():
+                tile = product(sh, sl, high_ref[:, own], low_ref[:, own])
+                for i in range(2):
+                    for j in range(2):
+                        block = tile[i * GROUP : (i + 1) * GROUP, j * GROUP : (j + 1) * GROUP]
+                        put(a, (2 * (1 - pair) + (x ^ i)) * 2 + j, block)
 
 
 VMEM = pl.BlockSpec(memory_space=pltpu.VMEM)
@@ -245,13 +311,23 @@
     )
 
     def strip_at(t):
-        main = lax.dynamic_slice_in_dim(field, t * STRIP, STRIP, 1).reshape(nodes, GROUP)
-        return jnp.concatenate([main, seam], 0)
-
-    far_same = strip_at(2 * (1 - h) + x)
-    far_flip = strip_at(2 * (1 - h) + (1 - x))
-    near = [lax.ppermute(far_same, ALL, crossing(False, 0)), lax.ppermute(far_flip, ALL, crossing(False, 1))]
-
+        main = lax.dynamic_slice_in_dim(field, t * STRIP, STRIP, 1)
+        return [
+            main[: rows - LAST].reshape(-1, GROUP),
+            jnp.concatenate([main[rows - LAST :].reshape(-1, GROUP), seam], 0),
+        ]
+
+    far = [[], []]
+    for flip in range(2):
+        strip = strip_at(2 * (1 - h) + (x ^ flip))
+        done = None
+        for outer in (False, True):
+            for piece in strip:
+                if done is not None:
+                    piece, done = lax.optimization_barrier((piece, done))
+                    far[flip][-1] = done
+                done = lax.ppermute(piece, ALL, crossing(outer, flip))
+                far[flip].append(done)
     none = jnp.zeros((rows, GROUP), jnp.float32)
     pad = jnp.zeros((8 - rows, GROUP), jnp.float32)
     pieces = []
@@ -260,81 +336,86 @@
         right = field[:, (t + 1) * STRIP] if t < 3 else none
         main = field[:, t * STRIP : (t + 1) * STRIP].reshape(nodes, GROUP)
         pieces.append(jnp.concatenate([main, left, pad, right, pad], 0))
-    own = lax.all_to_all(jnp.stack(pieces), PLACE, 0, 0, tiled=True)
-
-    far_same, far_flip, own, *near = lax.optimization_barrier((far_same, far_flip, own, *near))
-    far = [lax.ppermute(far_same, ALL, crossing(True, 0)), lax.ppermute(far_flip, ALL, crossing(True, 1))]
+    strips = lax.all_to_all(jnp.stack(pieces), PLACE, 0, 0, tiled=True)
+
+    total_nodes = snapshots.shape[0] * 4
+    weight = weights_of(region_ids, conductivity) / math.sqrt(total_nodes)
+    weight = jnp.pad(weight, ((0, 0), (8, 8)))
+    weight = lax.dynamic_slice_in_dim(weight, (2 * (1 - l) + x) * STRIP, STRIP + 16, 1)
+    weight = jnp.broadcast_to(weight[:, :, None], (rows, STRIP + 16, GROUP))
 
     def edge(r):
         return jnp.concatenate(
             [
-                own[:, r * STRIP : (r + 1) * STRIP],
-                own[:, nodes + r : nodes + r + 1],
-                own[:, nodes + 8 + r : nodes + 8 + r + 1],
+                strips[:, r * STRIP : (r + 1) * STRIP],
+                strips[:, nodes + r : nodes + r + 1],
+                strips[:, nodes + 8 + r : nodes + 9 + r],
                 jnp.zeros((4, 6, GROUP), jnp.float32),
             ],
             1,
-        )
-
-    above = lax.ppermute(edge(rows - 1), TILE, [(m, m + 1) for m in range(3)])
-    below = lax.ppermute(edge(0), TILE, [(m + 1, m) for m in range(3)])
-
-    total_nodes = snapshots.shape[0] * 4
-    weight = weights_of(region_ids, conductivity) / math.sqrt(total_nodes)
-    weight_above = lax.ppermute(weight[rows - 1 :], TILE, [(m, m + 1) for m in range(3)])
-    weight = jnp.pad(jnp.concatenate([weight_above, weight], 0), ((0, 0), (8, 8)))
-    weight = lax.dynamic_slice_in_dim(weight, (2 * (1 - l) + x) * STRIP, STRIP + 16, 1)
-    weight = jnp.broadcast_to(weight[:, :, None], (rows + 1, STRIP + 16, GROUP))
-
-    blocks = jax.ShapeDtypeStruct((16, GROUP, GROUP), jnp.float32)
-    half_float = jax.ShapeDtypeStruct((nodes + SEAM, 4 * GROUP), jnp.bfloat16)
+        ).reshape(4 * (STRIP + 8), GROUP)
+
+    above = jnp.concatenate([edge(rows - 1), weight[rows - 1]], 0)
+    below = edge(0)
+    above = lax.ppermute(above, TILE, [(m, m + 1) for m in range(3)])
+    below = lax.ppermute(below, TILE, [(m + 1, m) for m in range(3)])
+    far = [far[flip][2 * outer + k] for outer in range(2) for flip in range(2) for k in range(2)]
+
+    side = jnp.stack([c, h, x, l]).astype(jnp.int32)
     seam_side = jnp.stack([(h == 0) & (x == 1), (h == 1) & (x == 0)]).astype(jnp.float32)
     seam_side = seam_side * jnp.array([1.0, -1.0], jnp.float32)
-    high, low, own_blocks = pl.pallas_call(
+    blocks = jax.ShapeDtypeStruct((8, GROUP, GROUP), jnp.float32)
+    own_blocks = jax.ShapeDtypeStruct((2, 2, GROUP, 2 * GROUP), jnp.float32)
+    half_float = jax.ShapeDtypeStruct((nodes + SEAM, 4 * GROUP), jnp.bfloat16)
+    high, low, own_mine, own_other = pl.pallas_call(
         lambda *refs: own_kernel(rows, *refs),
-        out_shape=(half_float, half_float, blocks),
-        in_specs=[SMEM] + [VMEM] * 4,
-        out_specs=(VMEM,) * 3,
+        out_shape=(half_float, half_float, own_blocks, own_blocks),
+        in_specs=[SMEM] * 2 + [VMEM] * 4,
+        out_specs=(VMEM,) * 4,
         scratch_shapes=[pltpu.VMEM((nodes, 4 * GROUP), jnp.bfloat16)] * 2,
         compiler_params=pltpu.CompilerParams(vmem_limit_bytes=40 * 1024 * 1024),
-        cost_estimate=pl.CostEstimate(
-            flops=6 * nodes * 512 * 512, bytes_accessed=6 * 1024 * 1024, transcendentals=0
-        ),
-    )(seam_side, own, above, below, weight)
-
-    place = jnp.stack([2 * h + x, 2 * h + (1 - x), 2 * (1 - h) + x, 2 * (1 - h) + (1 - x)])
-    cross_blocks = pl.pallas_call(
+        cost_estimate=pl.CostEstimate(flops=1, bytes_accessed=1, transcendentals=0),
+    )(side, seam_side, strips, above, below, weight)
+
+    def both_cores(mine, other):
+        return mine + lax.ppermute(other, "c", [(0, 1), (1, 0)])
+
+    own = both_cores(own_mine, own_other)
+    cross_mine, cross_other = pl.pallas_call(
         cross_kernel,
-        out_shape=blocks,
-        in_specs=[SMEM] + [VMEM] * 6,
-        out_specs=VMEM,
+        out_shape=(blocks, blocks),
+        in_specs=[SMEM] + [VMEM] * 10,
+        out_specs=(VMEM,) * 2,
         compiler_params=pltpu.CompilerParams(vmem_limit_bytes=40 * 1024 * 1024),
-        cost_estimate=pl.CostEstimate(
-            flops=6 * nodes * 512 * 512, bytes_accessed=5 * 1024 * 1024, transcendentals=0
-        ),
-    )(place.astype(jnp.int32), high, low, *near, *far)
-
-    def gathered(parts):
-        return jnp.sum(lax.all_to_all(parts, PLACE + TILE, 0, 0, tiled=True), 0)
-
-    own_block = gathered(own_blocks)
-    cross_block = gathered(cross_blocks)
-    swap = []
-    for half in range(2):
-        for i in range(4):
-            for m in range(4):
-                swap.append((half * 16 + i * 4 + m, (1 - half) * 16 + m * 4 + i))
-    cross_block = cross_block + lax.ppermute(cross_block, ALL, swap).T
-
-    first = jnp.where(h == 0, own_block, cross_block)
-    last = jnp.where(h == 0, cross_block, own_block)
-    one = jnp.where(c == 0, first, last)
-    two = jnp.where(c == 0, last, first)
-    one = lax.ppermute(one, TILE, [(0, 0), (1, 2), (2, 1), (3, 3)])
-    two = lax.ppermute(two, TILE, [(0, 2), (1, 0), (2, 3), (3, 1)])
-    return jnp.where(
-        y == 0, jnp.concatenate([one, two], 1), jnp.concatenate([two, one], 1)
-    )
+        cost_estimate=pl.CostEstimate(flops=10**11, bytes_accessed=1, transcendentals=0),
+    )(side, high, low, *far)
+
+    own, cross_mine, cross_other = lax.optimization_barrier((own, cross_mine, cross_other))
+    own = own[0] + lax.ppermute(own[1], "l", [(0, 1), (1, 0)])
+    own = own[0] + lax.ppermute(own[1], "x", [(0, 1), (1, 0)])
+    to_holder = [
+        (flat(i, j, k, 1 - i, n), flat(i, j, k, i, n))
+        for i in range(2)
+        for j in range(2)
+        for k in range(2)
+        for n in range(2)
+    ]
+    own = own + lax.ppermute(own, ALL, to_holder)
+
+    cross = lax.all_to_all(
+        both_cores(cross_mine, cross_other), ALL, 0, 0, tiled=True, axis_index_groups=MIDDLE_GROUPS
+    )
+    cross = jnp.sum(cross, 0)
+    even = (x + y) % 2 == 0
+    turned = cross.T
+    cross_pair = [
+        lax.ppermute(jnp.where(even, cross, turned), ALL, owners(0)),
+        lax.ppermute(jnp.where(even, turned, cross), ALL, owners(1)),
+    ]
+    swapped = (x + h) % 2 == 1
+    left = jnp.where(swapped, cross_pair[1], cross_pair[0])
+    right = jnp.where(swapped, cross_pair[0], cross_pair[1])
+    return jnp.where(y == h, own, jnp.concatenate([left, right], 1))
 
 
 def solution(mesh):

time: 111 us -> 94.2 us (0.85)
  the two profiles are of different devices: /device:TPU:25 before, /device:TPU:8 now
where the time goes in v2:
time: 94.2 us; the launch traced here: 93.5 us
  starting transfers between devices  45.3 us (48%)
  waiting for transfers between devices  31 us (33%)
  Pallas kernels  7.3 us (8%)
  other arithmetic  5.06 us (5%)
  local copies, waits for them, and re-layouts  4.5 us (5%)
    ppermute x8, starting transfers between devices, local_strips(): done = lax.ppermute(piece, ALL, crossing(outer, flip))  18.3 us
    ppermute x8, waiting for transfers between devices, local_strips(): done = lax.ppermute(piece, ALL, crossing(outer, flip))  14.9 us
    ppermute x1, waiting for transfers between devices, local_strips(): own = own[0] + lax.ppermute(own[1], 'l', [(0, 1), (1, 0)])  8.02 us
    ppermute x2, starting transfers between devices, both_cores(): return mine + lax.ppermute(other, 'c', [(0, 1), (1, 0)])  6.54 us
    ppermute x1, waiting for transfers between devices, local_strips(): own = own + lax.ppermute(own, ALL, to_holder)  5.9 us
    all_to_all x1, starting transfers between devices, local_strips(): lax.all_to_all(both_cores(cross_mine, cross_other), ALL, 0, 0, tiled=True...  5.22 us
    all_to_all x1, starting transfers between devices, local_strips(): strips = lax.all_to_all(jnp.stack(pieces), PLACE, 0, 0, tiled=True)  4.35 us
    pallas_call x1, Pallas kernels, local_strips(): pl.pallas_call(lambda *refs: own_kernel(rows, *refs), out_shape=(half_flo...  3.85 us
  transfers between devices with their start and end apart: 19, of which 9 were waited for; matrix products, arithmetic and copies ran while one was open for 4% of the time, Pallas kernels for 8%

profile of v2, /device:TPU:8, one launch (start us, length us, event | category | flops | bytes accessed | tf_op | source)
XLA Modules:
  0.0 93.5 jit_solution(2364740777818089242)
XLA Ops:
  0.0 0.9 fusion.5
  0.9 1.5 %fusion.6 = (f32[6,128,128]{2,1,0:T(8,128)S(1)}, f32[6,128,128]{2,1,0:T(8,128)S(1)}, f32[6,128,128]{2,1,0:T(8,128)S(1)}, f32[6,128,128]{2,1,0:T(8,128)S(1)}) fusion(f32[6,512,128]{2,1,0:T(8,128)} %bitcast.48), kind=kLoop, calls=%fused_computation.38 | loop fusion | bytes 3145728 | tf_op jit(solution)/shard_map/slice | solution.py:337
  2.4 0.2 concatenate.34
  2.6 0.1 concatenate.35
  2.7 0.1 concatenate.36
  2.8 0.1 concatenate.33
  3.0 1.3 %pad_maximum_fusion = f32[4,784,128]{2,1,0:T(8,128)} fusion(f32[1,784,128]{2,1,0:T(8,128)S(1)} %bitcast.52, f32[1,784,128]{2,1,0:T(8,128)S(1)} %bitcast.51, f32[1,784,128]{2,1,0:T(8,128)S(1)} %bitcast.50, f32[1,784,128]{2,1,0:T(8,128)S(1)} %bitcast.53), kind=kLoop, calls=%fused_computation | loop fusion | flops 1204224 | bytes 3211264 | tf_op jit(solution)/shard_map/stack | solution.py:339
  4.3 4.4 %all-to-all-start = ((f32[4,784,128]{2,1,0:T(8,128)}), f32[4,784,128]{2,1,0:T(8,128)S(1)}, u32[]{:S(2)}, u32[]{:S(2)}) async-start(f32[4,784,128]{2,1,0:T(8,128)} %pad_maximum_fusion), calls=%async_computation | async-start | bytes 3211264 | tf_op jit(solution)/shard_map/all_to_all | solution.py:339
  8.6 0.8 constant_dynamic-slice_fusion.2
  9.5 4.5 %collective-permute-start.5 = (f32[384,128]{1,0:T(8,128)}, f32[384,128]{1,0:T(8,128)S(1)}, u32[]{:S(2)}, u32[]{:S(2)}) collective-permute-start(f32[384,128]{1,0:T(8,128)} %bitcast.27), channel_id=1, source_target_pairs={{8,20},{9,21},{10,22},{11,23},{12,16},{13,17},{14,18},{15,19},{16,... | collective-permute-start | bytes 589832 | tf_op jit(solution)/shard_map/ppermute | solution.py:329
  13.9 2.2 %collective-permute-start.3 = (f32[384,128]{1,0:T(8,128)}, f32[384,128]{1,0:T(8,128)S(1)}, u32[]{:S(2)}, u32[]{:S(2)}) collective-permute-start(f32[384,128]{1,0:T(8,128)} %bitcast.25), channel_id=1, source_target_pairs={{8,16},{9,17},{10,18},{11,19},{12,20},{13,21},{14,22},{15,23},{16,... | collective-permute-start | bytes 589832 | tf_op jit(solution)/shard_map/ppermute | solution.py:329
  16.2 0.1 pad.12.clone
  16.3 0.1 select_reduce_fusion
  16.4 0.1 fusion.1
  16.5 0.0 copy-start.5
  16.6 6.2 %collective-permute-done.5.refs_2_ = f32[384,128]{1,0:T(8,128)S(1)} collective-permute-done((f32[384,128]{1,0:T(8,128)}, f32[384,128]{1,0:T(8,128)S(1)}, u32[]{:S(2)}, u32[]{:S(2)}) %collective-permute-start.5) | collective-permute-done | bytes 196640 | tf_op jit(solution)/shard_map/ppermute | solution.py:329
  22.8 4.5 %collective-permute-start.6 = (f32[400,128]{1,0:T(8,128)S(1)}, f32[400,128]{1,0:T(8,128)S(1)}, u32[]{:S(2)}, u32[]{:S(2)}) collective-permute-start(f32[400,128]{1,0:T(8,128)S(1)} %get-tuple-element.41), channel_id=1, source_target_pairs={{8,20},{9,21},{10,22},{11,23},{12,16},{13,17},{14,18},{15,19},{16,... | collective-permute-start | bytes 614408 | tf_op jit(solution)/shard_map/ppermute | solution.py:329
  27.3 0.0 collective-permute-done.3.refs_0_
  27.3 1.9 %collective-permute-start.4 = (f32[400,128]{1,0:T(8,128)S(1)}, f32[400,128]{1,0:T(8,128)S(1)}, u32[]{:S(2)}, u32[]{:S(2)}) collective-permute-start(f32[400,128]{1,0:T(8,128)S(1)} %get-tuple-element.38), channel_id=1, source_target_pairs={{8,16},{9,17},{10,18},{11,19},{12,20},{13,21},{14,22},{15,23},{16,... | collective-permute-start | bytes 614408 | tf_op jit(solution)/shard_map/ppermute | solution.py:329
  29.3 0.1 pad.22.clone
  29.4 0.1 pad_dynamic-slice_fusion
  29.4 0.1 pad.18.clone
  29.5 3.8 %collective-permute-done.6.refs_3_ = f32[400,128]{1,0:T(8,128)S(1)} collective-permute-done((f32[400,128]{1,0:T(8,128)S(1)}, f32[400,128]{1,0:T(8,128)S(1)}, u32[]{:S(2)}, u32[]{:S(2)}) %collective-permute-start.6) | collective-permute-done | bytes 204832 | tf_op jit(solution)/shard_map/ppermute | solution.py:329
  33.3 1.3 %collective-permute-start.9 = (f32[384,128]{1,0:T(8,128)}, f32[384,128]{1,0:T(8,128)S(1)}, u32[]{:S(2)}, u32[]{:S(2)}) collective-permute-start(f32[384,128]{1,0:T(8,128)} %bitcast.27), channel_id=1, source_target_pairs={{0,20},{1,21},{2,22},{3,23},{4,16},{5,17},{6,18},{7,19},{24,12},{2... | collective-permute-start | bytes 589832 | tf_op jit(solution)/shard_map/ppermute | solution.py:329
  34.6 2.6 %collective-permute-done.4.refs_1_ = f32[400,128]{1,0:T(8,128)S(1)} collective-permute-done((f32[400,128]{1,0:T(8,128)S(1)}, f32[400,128]{1,0:T(8,128)S(1)}, u32[]{:S(2)}, u32[]{:S(2)}) %collective-permute-start.4) | collective-permute-done | bytes 204832 | tf_op jit(solution)/shard_map/ppermute | solution.py:329
  37.2 1.3 %collective-permute-start.7 = (f32[384,128]{1,0:T(8,128)}, f32[384,128]{1,0:T(8,128)S(1)}, u32[]{:S(2)}, u32[]{:S(2)}) collective-permute-start(f32[384,128]{1,0:T(8,128)} %bitcast.25), channel_id=1, source_target_pairs={{0,16},{1,17},{2,18},{3,19},{4,20},{5,21},{6,22},{7,23},{24,8},{25... | collective-permute-start | bytes 589832 | tf_op jit(solution)/shard_map/ppermute | solution.py:329
  38.5 0.0 all-to-all-done.refs_2_
  38.6 0.8 maximum_maximum_fusion.1
  39.4 0.9 pad_maximum_fusion.1
  40.3 1.8 %collective-permute-start = (f32[688,128]{1,0:T(8,128)}, f32[688,128]{1,0:T(8,128)S(1)}, u32[]{:S(2)}, u32[]{:S(2)}) collective-permute-start(f32[688,128]{1,0:T(8,128)} %pad_maximum_fusion.1), channel_id=1, source_target_pairs={{0,1},{1,2},{2,3},{4,5},{5,6},{6,7},{8,9},{9,10},{10,11},{12,13},{... | collective-permute-start | bytes 1056776 | tf_op jit(solution)/shard_map/ppermute | solution.py:360
  42.0 0.1 pad_dynamic-slice_fusion.1
  42.1 1.3 %collective-permute-start.1 = (f32[544,128]{1,0:T(8,128)}, f32[544,128]{1,0:T(8,128)S(1)}, u32[]{:S(2)}, u32[]{:S(2)}) collective-permute-start(f32[544,128]{1,0:T(8,128)} %bitcast.61), channel_id=1, source_target_pairs={{1,0},{2,1},{3,2},{5,4},{6,5},{7,6},{9,8},{10,9},{11,10},{13,12},{... | collective-permute-start | bytes 835592 | tf_op jit(solution)/shard_map/ppermute | solution.py:361
  43.4 0.1 pad_add_fusion.refs_0_.side_ref
  43.5 0.0 collective-permute-done.9.refs_6_
  43.5 1.3 %collective-permute-start.10 = (f32[400,128]{1,0:T(8,128)}, f32[400,128]{1,0:T(8,128)S(1)}, u32[]{:S(2)}, u32[]{:S(2)}) collective-permute-start(f32[400,128]{1,0:T(8,128)} %copy-done.2), channel_id=1, source_target_pairs={{0,20},{1,21},{2,22},{3,23},{4,16},{5,17},{6,18},{7,19},{24,12},{2... | collective-permute-start | bytes 614408 | tf_op jit(solution)/shard_map/ppermute | solution.py:329
  44.8 1.1 %collective-permute-done.7.refs_4_ = f32[384,128]{1,0:T(8,128)S(1)} collective-permute-done((f32[384,128]{1,0:T(8,128)}, f32[384,128]{1,0:T(8,128)S(1)}, u32[]{:S(2)}, u32[]{:S(2)}) %collective-permute-start.7) | collective-permute-done | bytes 196640 | tf_op jit(solution)/shard_map/ppermute | solution.py:329
  45.9 1.3 %collective-permute-start.8 = (f32[400,128]{1,0:T(8,128)}, f32[400,128]{1,0:T(8,128)S(1)}, u32[]{:S(2)}, u32[]{:S(2)}) collective-permute-start(f32[400,128]{1,0:T(8,128)} %copy-done.1), channel_id=1, source_target_pairs={{0,16},{1,17},{2,18},{3,19},{4,20},{5,21},{6,22},{7,23},{24,8},{25... | collective-permute-start | bytes 614408 | tf_op jit(solution)/shard_map/ppermute | solution.py:329
  47.2 0.1 add_select_fusion.refs_1_
  47.2 0.0 collective-permute-done.1.refs_4_
  47.3 0.0 collective-permute-done.refs_3_
  47.3 0.2 broadcast_in_dim.40.refs_5_
  47.4 3.8 %shard_map.46 = (bf16[784,512]{1,0:T(8,128)(2,1)S(1)}, bf16[784,512]{1,0:T(8,128)(2,1)S(1)}, f32[2,2,128,256]{3,2,1,0:T(8,128)S(1)}, f32[2,2,128,256]{3,2,1,0:T(8,128)S(1)}) custom-call(s32[4]{0:T(128)S(1)} %pad_add_fusion.refs_0_.side_ref, f32[2]{0:T(128)S(1)} %add_select_fusion.refs_1_, f32[4,784,128]{2,1,0:T(8,128)S(1)} %all-to-all-done.refs_2_, ...), custom_call_target="tpu_custom_call" | custom-call | flops 1 | bytes 1 | tf_op jit(solution)/shard_map/pallas_call | solution.py:370
  51.3 5.1 %collective-permute-start.2 = (f32[2,2,128,256]{3,2,1,0:T(8,128)S(1)}, f32[2,2,128,256]{3,2,1,0:T(8,128)S(1)}, u32[]{:S(2)}, u32[]{:S(2)}) collective-permute-start(f32[2,2,128,256]{3,2,1,0:T(8,128)S(1)} %get-tuple-element.27), channel_id=1, source_target_pairs={{0,1},{1,0},{2,3},{3,2},{4,5},{5,4},{6,7},{7,6},{8,9},{9,8},{10,11... | collective-permute-start | bytes 1572872 | tf_op jit(solution)/shard_map/ppermute | solution.py:381
  56.4 0.0 collective-permute-done.10.refs_7_
  56.4 1.2 %collective-permute-done.8.refs_5_ = f32[400,128]{1,0:T(8,128)S(1)} collective-permute-done((f32[400,128]{1,0:T(8,128)}, f32[400,128]{1,0:T(8,128)S(1)}, u32[]{:S(2)}, u32[]{:S(2)}) %collective-permute-start.8) | collective-permute-done | bytes 204832 | tf_op jit(solution)/shard_map/ppermute | solution.py:329
  57.6 3.4 %shard_map.47 = (f32[8,128,128]{2,1,0:T(8,128)S(1)}, f32[8,128,128]{2,1,0:T(8,128)S(1)}) custom-call(s32[4]{0:T(128)S(1)} %pad_add_fusion.refs_0_.side_ref, bf16[784,512]{1,0:T(8,128)(2,1)S(1)} %get-tuple-element.28.high_ref, bf16[784,512]{1,0:T(8,128)(2,1)S(1)} %get-tuple-element.29.low_ref, f32[384,128]{1,0:T(8,128)S(1)} %collective-permute-done.3.refs_0_, ...), custom_call_target="tpu_custom_call" | custom-call | flops 99999997952 | bytes 1 | tf_op jit(solution)/shard_map/pallas_call | solution.py:384
  61.1 0.0 collective-permute-done.2
  61.1 0.1 add.50
  61.2 1.4 %collective-permute-start.14 = (f32[8,128,128]{2,1,0:T(8,128)S(1)}, f32[8,128,128]{2,1,0:T(8,128)S(1)}, u32[]{:S(2)}, u32[]{:S(2)}) collective-permute-start(f32[8,128,128]{2,1,0:T(8,128)S(1)} %get-tuple-element.46), channel_id=1, source_target_pairs={{0,1},{1,0},{2,3},{3,2},{4,5},{5,4},{6,7},{7,6},{8,9},{9,8},{10,11... | collective-permute-start | bytes 1572872 | tf_op jit(solution)/shard_map/ppermute | solution.py:381
  62.6 1.5 %collective-permute-done.14 = f32[8,128,128]{2,1,0:T(8,128)S(1)} collective-permute-done((f32[8,128,128]{2,1,0:T(8,128)S(1)}, f32[8,128,128]{2,1,0:T(8,128)S(1)}, u32[]{:S(2)}, u32[]{:S(2)}) %collective-permute-start.14) | collective-permute-done | bytes 524320 | tf_op jit(solution)/shard_map/ppermute | solution.py:381
  64.1 0.8 add.62
  65.0 5.2 %all-to-all-start.1 = ((f32[8,128,128]{2,1,0:T(8,128)}), f32[8,128,128]{2,1,0:T(8,128)S(1)}, u32[]{:S(2)}, u32[]{:S(2)}) async-start(f32[8,128,128]{2,1,0:T(8,128)} %add.62), calls=%async_computation.1 | async-start | bytes 1048576 | tf_op jit(solution)/shard_map/all_to_all | solution.py:405
  70.2 0.1 collective-permute-start.11
  70.3 8.0 %collective-permute-done.11 = f32[2,128,256]{2,1,0:T(8,128)S(1)} collective-permute-done((f32[2,128,256]{2,1,0:T(8,128)S(1)}, f32[2,128,256]{2,1,0:T(8,128)S(1)}, u32[]{:S(2)}, u32[]{:S(2)}) %collective-permute-start.11) | collective-permute-done | bytes 262176 | tf_op jit(solution)/shard_map/ppermute | solution.py:394
  78.4 1.8 %collective-permute-start.12 = (f32[128,256]{1,0:T(8,128)S(1)}, f32[128,256]{1,0:T(8,128)S(1)}, u32[]{:S(2)}, u32[]{:S(2)}) collective-permute-start(f32[128,256]{1,0:T(8,128)S(1)} %slice_bitcast_fusion.1), channel_id=1, source_target_pairs={{0,4},{4,0},{1,5},{5,1},{2,6},{6,2},{3,7},{7,3},{8,12},{12,8},{9,1... | collective-permute-start | bytes 393224 | tf_op jit(solution)/shard_map/ppermute | solution.py:395
  80.2 0.0 all-to-all-done.1
  80.2 0.1 copy.19
  80.4 3.4 %collective-permute-start.15 = (f32[128,128]{1,0:T(8,128)S(1)}, f32[128,128]{1,0:T(8,128)S(1)}, u32[]{:S(2)}, u32[]{:S(2)}) collective-permute-start(f32[128,128]{1,0:T(8,128)S(1)} %get-tuple-element.69), channel_id=1, source_target_pairs={{8,16},{9,24},{10,2},{11,3},{12,6},{13,7},{14,20},{15,28},{16,17},... | collective-permute-start | bytes 196616 | tf_op jit(solution)/shard_map/ppermute | solution.py:413
  83.7 1.3 %collective-permute-start.16 = (f32[128,128]{1,0:T(8,128)S(1)}, f32[128,128]{1,0:T(8,128)S(1)}, u32[]{:S(2)}, u32[]{:S(2)}) collective-permute-start(f32[128,128]{1,0:T(8,128)S(1)} %get-tuple-element.70), channel_id=1, source_target_pairs={{8,2},{9,3},{10,20},{11,28},{12,16},{13,24},{14,6},{15,7},{16,10},... | collective-permute-start | bytes 196616 | tf_op jit(solution)/shard_map/ppermute | solution.py:412
  85.1 1.3 %collective-permute-start.13 = (f32[128,256]{1,0:T(8,128)S(1)}, f32[128,256]{1,0:T(8,128)S(1)}, u32[]{:S(2)}, u32[]{:S(2)}) collective-permute-start(f32[128,256]{1,0:T(8,128)S(1)} %fusion.2), channel_id=1, source_target_pairs={{2,0},{3,1},{6,4},{7,5},{10,8},{11,9},{14,12},{15,13},{16,18},{17,... | collective-permute-start | bytes 393224 | tf_op jit(solution)/shard_map/ppermute | solution.py:403
  86.4 0.0 collective-permute-done.15
  86.4 0.5 collective-permute-done.16
  86.9 5.9 %collective-permute-done.13 = f32[128,256]{1,0:T(8,128)S(1)} collective-permute-done((f32[128,256]{1,0:T(8,128)S(1)}, f32[128,256]{1,0:T(8,128)S(1)}, u32[]{:S(2)}, u32[]{:S(2)}) %collective-permute-start.13) | collective-permute-done | bytes 131104 | tf_op jit(solution)/shard_map/ppermute | solution.py:403
  92.8 0.7 maximum_select_fusion
  (29 shorter events, 0.2 us)
Async XLA Ops:
  4.3 4.4 %copy-start = (f32[3072,128]{1,0:T(8,128)S(1)}, f32[3072,128]{1,0:T(8,128)}, u32[]{:S(2)}) copy-start(f32[3072,128]{1,0:T(8,128)} %param.4) | copy-start | bytes 4718596
  4.3 34.2 %all-to-all-start = ((f32[4,784,128]{2,1,0:T(8,128)}), f32[4,784,128]{2,1,0:T(8,128)S(1)}, u32[]{:S(2)}, u32[]{:S(2)}) async-start(f32[4,784,128]{2,1,0:T(8,128)} %pad_maximum_fusion), calls=%async_computation | async-start | bytes 3211264 | tf_op jit(solution)/shard_map/all_to_all | solution.py:339
  8.6 7.6 %copy-start.3 = (s32[6,512]{1,0:T(8,128)S(1)}, s32[6,512]{1,0:T(8,128)}, u32[]{:S(2)}) copy-start(s32[6,512]{1,0:T(8,128)} %param.5) | copy-start | bytes 36868
  8.6 7.6 %copy-start.4 = (f32[8]{0:T(128)S(1)}, f32[8]{0:T(128)}, u32[]{:S(2)}) copy-start(f32[8]{0:T(128)} %param.6) | copy-start | bytes 100
  9.5 13.3 %collective-permute-start.5 = (f32[384,128]{1,0:T(8,128)}, f32[384,128]{1,0:T(8,128)S(1)}, u32[]{:S(2)}, u32[]{:S(2)}) collective-permute-start(f32[384,128]{1,0:T(8,128)} %bitcast.27), channel_id=1, source_target_pairs={{8,20},{9,21},{10,22},{11,23},{12,16},{13,17},{14,18},{15,19},{16,... | collective-permute-start | bytes 589832 | tf_op jit(solution)/shard_map/ppermute | solution.py:329
  13.9 13.4 %collective-permute-start.3 = (f32[384,128]{1,0:T(8,128)}, f32[384,128]{1,0:T(8,128)S(1)}, u32[]{:S(2)}, u32[]{:S(2)}) collective-permute-start(f32[384,128]{1,0:T(8,128)} %bitcast.25), channel_id=1, source_target_pairs={{8,16},{9,17},{10,18},{11,19},{12,20},{13,21},{14,22},{15,23},{16,... | collective-permute-start | bytes 589832 | tf_op jit(solution)/shard_map/ppermute | solution.py:329
  16.5 18.1 %copy-start.1 = (f32[400,128]{1,0:T(8,128)}, f32[400,128]{1,0:T(8,128)S(1)}, u32[]{:S(2)}) copy-start(f32[400,128]{1,0:T(8,128)S(1)} %get-tuple-element.38) | copy-start | bytes 614404
  16.5 22.9 %copy-start.2 = (f32[400,128]{1,0:T(8,128)}, f32[400,128]{1,0:T(8,128)S(1)}, u32[]{:S(2)}) copy-start(f32[400,128]{1,0:T(8,128)S(1)} %get-tuple-element.41) | copy-start | bytes 614404
  16.5 30.6 %copy-start.5 = (f32[2]{0:T(128)S(1)}, f32[2]{0:T(128)}, u32[]{:S(2)}) copy-start(f32[2]{0:T(128)} %constant.59.clone) | copy-start | bytes 28
  22.8 10.5 %collective-permute-start.6 = (f32[400,128]{1,0:T(8,128)S(1)}, f32[400,128]{1,0:T(8,128)S(1)}, u32[]{:S(2)}, u32[]{:S(2)}) collective-permute-start(f32[400,128]{1,0:T(8,128)S(1)} %get-tuple-element.41), channel_id=1, source_target_pairs={{8,20},{9,21},{10,22},{11,23},{12,16},{13,17},{14,18},{15,19},{16,... | collective-permute-start | bytes 614408 | tf_op jit(solution)/shard_map/ppermute | solution.py:329
  27.3 9.9 %collective-permute-start.4 = (f32[400,128]{1,0:T(8,128)S(1)}, f32[400,128]{1,0:T(8,128)S(1)}, u32[]{:S(2)}, u32[]{:S(2)}) collective-permute-start(f32[400,128]{1,0:T(8,128)S(1)} %get-tuple-element.38), channel_id=1, source_target_pairs={{8,16},{9,17},{10,18},{11,19},{12,20},{13,21},{14,22},{15,23},{16,... | collective-permute-start | bytes 614408 | tf_op jit(solution)/shard_map/ppermute | solution.py:329
  33.3 10.1 %collective-permute-start.9 = (f32[384,128]{1,0:T(8,128)}, f32[384,128]{1,0:T(8,128)S(1)}, u32[]{:S(2)}, u32[]{:S(2)}) collective-permute-start(f32[384,128]{1,0:T(8,128)} %bitcast.27), channel_id=1, source_target_pairs={{0,20},{1,21},{2,22},{3,23},{4,16},{5,17},{6,18},{7,19},{24,12},{2... | collective-permute-start | bytes 589832 | tf_op jit(solution)/shard_map/ppermute | solution.py:329
  37.2 8.7 %collective-permute-start.7 = (f32[384,128]{1,0:T(8,128)}, f32[384,128]{1,0:T(8,128)S(1)}, u32[]{:S(2)}, u32[]{:S(2)}) collective-permute-start(f32[384,128]{1,0:T(8,128)} %bitcast.25), channel_id=1, source_target_pairs={{0,16},{1,17},{2,18},{3,19},{4,20},{5,21},{6,22},{7,23},{24,8},{25... | collective-permute-start | bytes 589832 | tf_op jit(solution)/shard_map/ppermute | solution.py:329
  40.3 7.0 %collective-permute-start = (f32[688,128]{1,0:T(8,128)}, f32[688,128]{1,0:T(8,128)S(1)}, u32[]{:S(2)}, u32[]{:S(2)}) collective-permute-start(f32[688,128]{1,0:T(8,128)} %pad_maximum_fusion.1), channel_id=1, source_target_pairs={{0,1},{1,2},{2,3},{4,5},{5,6},{6,7},{8,9},{9,10},{10,11},{12,13},{... | collective-permute-start | bytes 1056776 | tf_op jit(solution)/shard_map/ppermute | solution.py:360
  42.1 5.1 %collective-permute-start.1 = (f32[544,128]{1,0:T(8,128)}, f32[544,128]{1,0:T(8,128)S(1)}, u32[]{:S(2)}, u32[]{:S(2)}) collective-permute-start(f32[544,128]{1,0:T(8,128)} %bitcast.61), channel_id=1, source_target_pairs={{1,0},{2,1},{3,2},{5,4},{6,5},{7,6},{9,8},{10,9},{11,10},{13,12},{... | collective-permute-start | bytes 835592 | tf_op jit(solution)/shard_map/ppermute | solution.py:361
  43.5 12.9 %collective-permute-start.10 = (f32[400,128]{1,0:T(8,128)}, f32[400,128]{1,0:T(8,128)S(1)}, u32[]{:S(2)}, u32[]{:S(2)}) collective-permute-start(f32[400,128]{1,0:T(8,128)} %copy-done.2), channel_id=1, source_target_pairs={{0,20},{1,21},{2,22},{3,23},{4,16},{5,17},{6,18},{7,19},{24,12},{2... | collective-permute-start | bytes 614408 | tf_op jit(solution)/shard_map/ppermute | solution.py:329
  45.9 11.8 %collective-permute-start.8 = (f32[400,128]{1,0:T(8,128)}, f32[400,128]{1,0:T(8,128)S(1)}, u32[]{:S(2)}, u32[]{:S(2)}) collective-permute-start(f32[400,128]{1,0:T(8,128)} %copy-done.1), channel_id=1, source_target_pairs={{0,16},{1,17},{2,18},{3,19},{4,20},{5,21},{6,22},{7,23},{24,8},{25... | collective-permute-start | bytes 614408 | tf_op jit(solution)/shard_map/ppermute | solution.py:329
  51.3 9.8 %collective-permute-start.2 = (f32[2,2,128,256]{3,2,1,0:T(8,128)S(1)}, f32[2,2,128,256]{3,2,1,0:T(8,128)S(1)}, u32[]{:S(2)}, u32[]{:S(2)}) collective-permute-start(f32[2,2,128,256]{3,2,1,0:T(8,128)S(1)} %get-tuple-element.27), channel_id=1, source_target_pairs={{0,1},{1,0},{2,3},{3,2},{4,5},{5,4},{6,7},{7,6},{8,9},{9,8},{10,11... | collective-permute-start | bytes 1572872 | tf_op jit(solution)/shard_map/ppermute | solution.py:381
  61.2 2.9 %collective-permute-start.14 = (f32[8,128,128]{2,1,0:T(8,128)S(1)}, f32[8,128,128]{2,1,0:T(8,128)S(1)}, u32[]{:S(2)}, u32[]{:S(2)}) collective-permute-start(f32[8,128,128]{2,1,0:T(8,128)S(1)} %get-tuple-element.46), channel_id=1, source_target_pairs={{0,1},{1,0},{2,3},{3,2},{4,5},{5,4},{6,7},{7,6},{8,9},{9,8},{10,11... | collective-permute-start | bytes 1572872 | tf_op jit(solution)/shard_map/ppermute | solution.py:381
  65.0 15.2 %all-to-all-start.1 = ((f32[8,128,128]{2,1,0:T(8,128)}), f32[8,128,128]{2,1,0:T(8,128)S(1)}, u32[]{:S(2)}, u32[]{:S(2)}) async-start(f32[8,128,128]{2,1,0:T(8,128)} %add.62), calls=%async_computation.1 | async-start | bytes 1048576 | tf_op jit(solution)/shard_map/all_to_all | solution.py:405
  70.2 8.1 %collective-permute-start.11 = (f32[2,128,256]{2,1,0:T(8,128)S(1)}, f32[2,128,256]{2,1,0:T(8,128)S(1)}, u32[]{:S(2)}, u32[]{:S(2)}) collective-permute-start(f32[2,128,256]{2,1,0:T(8,128)S(1)} %slice_bitcast_fusion), channel_id=1, source_target_pairs={{0,8},{8,0},{1,9},{9,1},{2,10},{10,2},{3,11},{11,3},{4,12},{12,4},... | collective-permute-start | bytes 786440 | tf_op jit(solution)/shard_map/ppermute | solution.py:394
  78.4 6.6 %collective-permute-start.12 = (f32[128,256]{1,0:T(8,128)S(1)}, f32[128,256]{1,0:T(8,128)S(1)}, u32[]{:S(2)}, u32[]{:S(2)}) collective-permute-start(f32[128,256]{1,0:T(8,128)S(1)} %slice_bitcast_fusion.1), channel_id=1, source_target_pairs={{0,4},{4,0},{1,5},{5,1},{2,6},{6,2},{3,7},{7,3},{8,12},{12,8},{9,1... | collective-permute-start | bytes 393224 | tf_op jit(solution)/shard_map/ppermute | solution.py:395
  80.4 6.0 %collective-permute-start.15 = (f32[128,128]{1,0:T(8,128)S(1)}, f32[128,128]{1,0:T(8,128)S(1)}, u32[]{:S(2)}, u32[]{:S(2)}) collective-permute-start(f32[128,128]{1,0:T(8,128)S(1)} %get-tuple-element.69), channel_id=1, source_target_pairs={{8,16},{9,24},{10,2},{11,3},{12,6},{13,7},{14,20},{15,28},{16,17},... | collective-permute-start | bytes 196616 | tf_op jit(solution)/shard_map/ppermute | solution.py:413
  83.7 3.2 %collective-permute-start.16 = (f32[128,128]{1,0:T(8,128)S(1)}, f32[128,128]{1,0:T(8,128)S(1)}, u32[]{:S(2)}, u32[]{:S(2)}) collective-permute-start(f32[128,128]{1,0:T(8,128)S(1)} %get-tuple-element.70), channel_id=1, source_target_pairs={{8,2},{9,3},{10,20},{11,28},{12,16},{13,24},{14,6},{15,7},{16,10},... | collective-permute-start | bytes 196616 | tf_op jit(solution)/shard_map/ppermute | solution.py:412
  85.1 7.8 %collective-permute-start.13 = (f32[128,256]{1,0:T(8,128)S(1)}, f32[128,256]{1,0:T(8,128)S(1)}, u32[]{:S(2)}, u32[]{:S(2)}) collective-permute-start(f32[128,256]{1,0:T(8,128)S(1)} %fusion.2), channel_id=1, source_target_pairs={{2,0},{3,1},{6,4},{7,5},{10,8},{11,9},{14,12},{15,13},{16,18},{17,... | collective-permute-start | bytes 393224 | tf_op jit(solution)/shard_map/ppermute | solution.py:403

commit v3 on v2

--- a/solution.py
+++ b/solution.py
@@ -109,7 +109,6 @@
 GROUP = 128
 STRIP = 128
 SEAM = 16
-LAST = 3
 
 
 def flat(h, l, x, y, c):
@@ -155,10 +154,10 @@
     return high, (value - high.astype(jnp.float32)).astype(jnp.bfloat16)
 
 
-def product(left_high, left_low, right_high, right_low):
+def product(left_high, left_low, right_high, right_low, turned=False):
     def one(a, b):
         return lax.dot_general(
-            a, b, (((0,), (0,)), ((), ())), preferred_element_type=jnp.float32
+            a, b, (((1 if turned else 0,), (0,)), ((), ())), preferred_element_type=jnp.float32
         )
 
     return one(left_high, right_high) + one(left_high, right_low) + one(left_low, right_high)
@@ -168,6 +167,7 @@
     rows,
     side_ref,
     seam_ref,
+    ends_ref,
     field_ref,
     above_ref,
     below_ref,
@@ -178,6 +178,8 @@
     other_ref,
     sh,
     sl,
+    ph,
+    pw,
 ):
     wide = STRIP + 16
     line_number = lax.broadcasted_iota(jnp.int32, (SEAM, GROUP), 0)
@@ -209,11 +211,16 @@
         for r in range(-1, rows):
             n = r + 1
             if n < rows:
-                main = field_ref[g, n * STRIP : (n + 1) * STRIP]
+                if n in (0, rows - 1):
+                    at = 0 if n == 0 else STRIP
+                    main = ends_ref[g, at : at + STRIP]
+                else:
+                    main = field_ref[g, (n - 1) * STRIP : n * STRIP]
+                sides = 2 * STRIP + n
                 after = line(
                     main,
-                    field_ref[g, body + n : body + n + 1],
-                    field_ref[g, body + 8 + n : body + 9 + n],
+                    ends_ref[g, sides : sides + 1],
+                    ends_ref[g, sides + 8 : sides + 9],
                 )
                 high, low = split(main)
                 sh[n * STRIP : (n + 1) * STRIP, columns] = high
@@ -232,20 +239,20 @@
                 )
                 seam = jnp.where(line_number == r, beside, seam)
                 high, low = split(total[8 : 8 + STRIP])
-                high_ref[r * STRIP : (r + 1) * STRIP, columns] = high
-                low_ref[r * STRIP : (r + 1) * STRIP, columns] = low
+                ph[r * STRIP : (r + 1) * STRIP, columns] = high
+                pw[r * STRIP : (r + 1) * STRIP, columns] = low
             low_end, low_up = before + 2.0 * after, before_up + 2.0 * after_up
             carried = weight * (2.0 * low_end + low_up)
             carried_next = weight * (low_end + 2.0 * low_up)
             before, before_up = after, after_up
         high, low = split(seam)
-        high_ref[body : body + SEAM, columns] = high
-        low_ref[body : body + SEAM, columns] = low
+        ph[body : body + SEAM, columns] = high
+        pw[body : body + SEAM, columns] = low
     for a in range(2):
         left = slice(a * 256, (a + 1) * 256)
         tiles = [
             product(
-                sh[:, left], sl[:, left], high_ref[:body, right], low_ref[:body, right]
+                sh[:, left], sl[:, left], ph[:body, right], pw[:body, right]
             )
             for right in (slice(0, 256), slice(256, 512))
         ]
@@ -255,45 +262,38 @@
             rows_of = slice(i * GROUP, (i + 1) * GROUP)
             mine_ref[l ^ a, x ^ i] = mine[rows_of]
             other_ref[l ^ a, x ^ i] = other[rows_of]
-
-
-def cross_kernel(side_ref, high_ref, low_ref, *refs):
-    *pieces, mine_ref, other_ref = refs
+    for turned_ref, panel in ((high_ref, ph), (low_ref, pw)):
+        turned_ref[...] = panel[...].T
+
+
+def cross_kernel(side_ref, high_ref, low_ref, s0, s1, s2, s3, mine_ref, other_ref, tiles):
     core, half, x = side_ref[0], side_ref[1], side_ref[2]
-
-    def put(to_core, slot, block):
-        @pl.when(core == to_core)
-        def _():
-            mine_ref[slot] = block
-
-        @pl.when(core != to_core)
-        def _():
-            other_ref[slot] = block
-
-    for pair in range(2):
-        first, second = (
-            jnp.concatenate([pieces[k][...], pieces[k + 1][...]], 0)
-            for k in (4 * pair, 4 * pair + 2)
-        )
-        sh, sl = split(jnp.concatenate([first, second], 1))
+    for pair, (first, second) in enumerate(((s0, s1), (s2, s3))):
+        h0, l0 = split(first[...])
+        h1, l1 = split(second[...])
+        sh = jnp.concatenate([h0, h1], 1)
+        sl = jnp.concatenate([l0, l1], 1)
         for a in range(2):
             own = slice(a * 256, (a + 1) * 256)
-
-            @pl.when(half == 0)
-            def _():
-                tile = product(high_ref[:, own], low_ref[:, own], sh, sl)
+            tiles[pair, a] = product(high_ref[own], low_ref[own], sh, sl, turned=True)
+
+    def place(h, c):
+        for pair in range(2):
+            for a in range(2):
+                ref = mine_ref if (a if h else pair) == c else other_ref
                 for i in range(2):
                     for j in range(2):
-                        block = tile[i * GROUP : (i + 1) * GROUP, j * GROUP : (j + 1) * GROUP]
-                        put(pair, (2 * a + i) * 2 + (x ^ j), block)
-
-            @pl.when(half == 1)
-            def _():
-                tile = product(sh, sl, high_ref[:, own], low_ref[:, own])
-                for i in range(2):
-                    for j in range(2):
-                        block = tile[i * GROUP : (i + 1) * GROUP, j * GROUP : (j + 1) * GROUP]
-                        put(a, (2 * (1 - pair) + (x ^ i)) * 2 + j, block)
+                        block = tiles[
+                            pair, a, i * GROUP : (i + 1) * GROUP, j * GROUP : (j + 1) * GROUP
+                        ]
+                        if h:
+                            ref[(2 * (1 - pair) + (x ^ j)) * 2 + i] = block.T
+                        else:
+                            ref[(2 * a + i) * 2 + (x ^ j)] = block
+
+    for h in range(2):
+        for c in range(2):
+            pl.when((half == h) & (core == c))(lambda: place(h, c))
 
 
 VMEM = pl.BlockSpec(memory_space=pltpu.VMEM)
@@ -312,31 +312,24 @@
 
     def strip_at(t):
         main = lax.dynamic_slice_in_dim(field, t * STRIP, STRIP, 1)
-        return [
-            main[: rows - LAST].reshape(-1, GROUP),
-            jnp.concatenate([main[rows - LAST :].reshape(-1, GROUP), seam], 0),
-        ]
-
-    far = [[], []]
-    for flip in range(2):
-        strip = strip_at(2 * (1 - h) + (x ^ flip))
-        done = None
-        for outer in (False, True):
-            for piece in strip:
-                if done is not None:
-                    piece, done = lax.optimization_barrier((piece, done))
-                    far[flip][-1] = done
-                done = lax.ppermute(piece, ALL, crossing(outer, flip))
-                far[flip].append(done)
+        return [jnp.concatenate([main.reshape(nodes, GROUP), seam], 0)]
+
+    halves = [strip_at(2 * (1 - h) + (x ^ flip))[0] for flip in range(2)]
+    near = [lax.ppermute(halves[0], ALL, crossing(False, 0))]
+
     none = jnp.zeros((rows, GROUP), jnp.float32)
     pad = jnp.zeros((8 - rows, GROUP), jnp.float32)
-    pieces = []
+    ends, between = [], []
     for t in (2, 3, 0, 1):
         left = field[:, t * STRIP - 1] if t > 0 else none
         right = field[:, (t + 1) * STRIP] if t < 3 else none
-        main = field[:, t * STRIP : (t + 1) * STRIP].reshape(nodes, GROUP)
-        pieces.append(jnp.concatenate([main, left, pad, right, pad], 0))
-    strips = lax.all_to_all(jnp.stack(pieces), PLACE, 0, 0, tiled=True)
+        main = field[:, t * STRIP : (t + 1) * STRIP]
+        ends.append(jnp.concatenate([main[0], main[rows - 1], left, pad, right, pad], 0))
+        between.append(main[1 : rows - 1].reshape((rows - 2) * STRIP, GROUP))
+    ends = lax.all_to_all(jnp.stack(ends), PLACE, 0, 0, tiled=True)
+    between = lax.all_to_all(jnp.stack(between), PLACE, 0, 0, tiled=True)
+    half, ends = lax.optimization_barrier((halves[1], ends))
+    near.append(lax.ppermute(half, ALL, crossing(False, 1)))
 
     total_nodes = snapshots.shape[0] * 4
     weight = weights_of(region_ids, conductivity) / math.sqrt(total_nodes)
@@ -344,38 +337,44 @@
     weight = lax.dynamic_slice_in_dim(weight, (2 * (1 - l) + x) * STRIP, STRIP + 16, 1)
     weight = jnp.broadcast_to(weight[:, :, None], (rows, STRIP + 16, GROUP))
 
-    def edge(r):
+    def edge(at, r):
         return jnp.concatenate(
             [
-                strips[:, r * STRIP : (r + 1) * STRIP],
-                strips[:, nodes + r : nodes + r + 1],
-                strips[:, nodes + 8 + r : nodes + 9 + r],
+                ends[:, at : at + STRIP],
+                ends[:, 2 * STRIP + r : 2 * STRIP + r + 1],
+                ends[:, 2 * STRIP + 8 + r : 2 * STRIP + 9 + r],
                 jnp.zeros((4, 6, GROUP), jnp.float32),
             ],
             1,
         ).reshape(4 * (STRIP + 8), GROUP)
 
-    above = jnp.concatenate([edge(rows - 1), weight[rows - 1]], 0)
-    below = edge(0)
+    above = jnp.concatenate([edge(STRIP, rows - 1), weight[rows - 1]], 0)
+    below = edge(0, 0)
     above = lax.ppermute(above, TILE, [(m, m + 1) for m in range(3)])
     below = lax.ppermute(below, TILE, [(m + 1, m) for m in range(3)])
-    far = [far[flip][2 * outer + k] for outer in range(2) for flip in range(2) for k in range(2)]
+    far = []
+    for flip in range(2):
+        half, near[flip], above, below = lax.optimization_barrier(
+            (halves[flip], near[flip], above, below)
+        )
+        far.append(lax.ppermute(half, ALL, crossing(True, flip)))
 
     side = jnp.stack([c, h, x, l]).astype(jnp.int32)
     seam_side = jnp.stack([(h == 0) & (x == 1), (h == 1) & (x == 0)]).astype(jnp.float32)
     seam_side = seam_side * jnp.array([1.0, -1.0], jnp.float32)
     blocks = jax.ShapeDtypeStruct((8, GROUP, GROUP), jnp.float32)
     own_blocks = jax.ShapeDtypeStruct((2, 2, GROUP, 2 * GROUP), jnp.float32)
-    half_float = jax.ShapeDtypeStruct((nodes + SEAM, 4 * GROUP), jnp.bfloat16)
+    half_float = jax.ShapeDtypeStruct((4 * GROUP, nodes + SEAM), jnp.bfloat16)
     high, low, own_mine, own_other = pl.pallas_call(
         lambda *refs: own_kernel(rows, *refs),
         out_shape=(half_float, half_float, own_blocks, own_blocks),
-        in_specs=[SMEM] * 2 + [VMEM] * 4,
+        in_specs=[SMEM] * 2 + [VMEM] * 5,
         out_specs=(VMEM,) * 4,
-        scratch_shapes=[pltpu.VMEM((nodes, 4 * GROUP), jnp.bfloat16)] * 2,
+        scratch_shapes=[pltpu.VMEM((nodes, 4 * GROUP), jnp.bfloat16)] * 2
+        + [pltpu.VMEM((nodes + SEAM, 4 * GROUP), jnp.bfloat16)] * 2,
         compiler_params=pltpu.CompilerParams(vmem_limit_bytes=40 * 1024 * 1024),
         cost_estimate=pl.CostEstimate(flops=1, bytes_accessed=1, transcendentals=0),
-    )(side, seam_side, strips, above, below, weight)
+    )(side, seam_side, ends, between, above, below, weight)
 
     def both_cores(mine, other):
         return mine + lax.ppermute(other, "c", [(0, 1), (1, 0)])
@@ -384,13 +383,15 @@
     cross_mine, cross_other = pl.pallas_call(
         cross_kernel,
         out_shape=(blocks, blocks),
-        in_specs=[SMEM] + [VMEM] * 10,
+        in_specs=[SMEM] + [VMEM] * 6,
         out_specs=(VMEM,) * 2,
+        scratch_shapes=[pltpu.VMEM((2, 2, 256, 256), jnp.float32)],
         compiler_params=pltpu.CompilerParams(vmem_limit_bytes=40 * 1024 * 1024),
         cost_estimate=pl.CostEstimate(flops=10**11, bytes_accessed=1, transcendentals=0),
-    )(side, high, low, *far)
-
-    own, cross_mine, cross_other = lax.optimization_barrier((own, cross_mine, cross_other))
+    )(side, high, low, *near, *far)
+
+    cross = both_cores(cross_mine, cross_other)
+    own, cross = lax.optimization_barrier((own, cross))
     own = own[0] + lax.ppermute(own[1], "l", [(0, 1), (1, 0)])
     own = own[0] + lax.ppermute(own[1], "x", [(0, 1), (1, 0)])
     to_holder = [
@@ -402,9 +403,7 @@
     ]
     own = own + lax.ppermute(own, ALL, to_holder)
 
-    cross = lax.all_to_all(
-        both_cores(cross_mine, cross_other), ALL, 0, 0, tiled=True, axis_index_groups=MIDDLE_GROUPS
-    )
+    cross = lax.all_to_all(cross, ALL, 0, 0, tiled=True, axis_index_groups=MIDDLE_GROUPS)
     cross = jnp.sum(cross, 0)
     even = (x + y) % 2 == 0
     turned = cross.T

time: 94.2 us -> 88.6 us (0.941)
  starting transfers between devices: 45.3 us -> 36.5 us
  waiting for transfers between devices: 31 us -> 34.8 us
  local copies, waits for them, and re-layouts: 4.5 us -> 3.06 us
  other arithmetic: 5.06 us -> 6.47 us
    ppermute x8 -> x4, starting transfers between devices: 18.3 us -> 10.1 us  [the longest x1 4.49 us: local_strips(): near.append(lax.ppermute(half, ALL, crossing(False, 1)))]
    ppermute x8 -> x4, waiting for transfers between devices: 14.9 us -> 8.26 us  [the longest x2 6.95 us: local_strips(): far.append(lax.ppermute(half, ALL, crossing(True, flip)))]
    all_to_all x2 -> x3, waiting for transfers between devices: 0.01 us -> 6.05 us  [the longest x1 3.89 us: local_strips(): between = lax.all_to_all(jnp.stack(between), PLACE, 0, 0, tiled=True)]
    ppermute x1, waiting for transfers between devices: 0.01 us -> 4.07 us  [local_strips(): below = lax.ppermute(below, TILE, [(m + 1, m) for m in range(3)])]
    ppermute x2, starting transfers between devices: 6.54 us -> 4.28 us  [both_cores(): return mine + lax.ppermute(other, 'c', [(0, 1), (1, 0)])]
    all_to_all x2 -> x3, starting transfers between devices: 9.57 us -> 11.8 us  [the longest x1 4.22 us: local_strips(): ends = lax.all_to_all(jnp.stack(ends), PLACE, 0, 0, tiled=True)]
    slice x5 -> x4, local copies, waits for them, and re-layouts: 2.4 us -> 0.2 us  [the longest x1 0.09 us: local_strips(): above = jnp.concatenate([edge(STRIP, rows - 1), weight[rows - 1]], 0)]
    squeeze x3 -> x4, local copies, waits for them, and re-layouts: 0.01 us -> 1.11 us  [the longest x1 1.1 us: local_strips(): main[rows - 1]]
  transfers between devices with their start and end apart: 19 -> 16, of which waited for: 9 -> 9; matrix products, arithmetic and copies ran while one was open for 4% -> 6% of each run, Pallas kernels for 8% -> 8%
where the time goes in v3:
time: 88.6 us; the launch traced here: 87.9 us
  starting transfers between devices  36.5 us (41%)
  waiting for transfers between devices  34.8 us (39%)
  Pallas kernels  6.7 us (8%)
  other arithmetic  6.47 us (7%)
  local copies, waits for them, and re-layouts  3.06 us (3%)
    ppermute x1, waiting for transfers between devices, local_strips(): own = own[0] + lax.ppermute(own[1], 'l', [(0, 1), (1, 0)])  8.54 us
    ppermute x2, waiting for transfers between devices, local_strips(): far.append(lax.ppermute(half, ALL, crossing(True, flip)))  6.95 us
    ppermute x1, waiting for transfers between devices, local_strips(): own = own + lax.ppermute(own, ALL, to_holder)  5.86 us
    ppermute x1, starting transfers between devices, local_strips(): near.append(lax.ppermute(half, ALL, crossing(False, 1)))  4.49 us
    ppermute x2, starting transfers between devices, both_cores(): return mine + lax.ppermute(other, 'c', [(0, 1), (1, 0)])  4.28 us
    all_to_all x1, starting transfers between devices, local_strips(): ends = lax.all_to_all(jnp.stack(ends), PLACE, 0, 0, tiled=True)  4.22 us
    all_to_all x1, starting transfers between devices, local_strips(): between = lax.all_to_all(jnp.stack(between), PLACE, 0, 0, tiled=True)  4.1 us
    ppermute x1, waiting for transfers between devices, local_strips(): below = lax.ppermute(below, TILE, [(m + 1, m) for m in range(3)])  4.07 us
  transfers between devices with their start and end apart: 16, of which 9 were waited for; matrix products, arithmetic and copies ran while one was open for 6% of the time, Pallas kernels for 8%

profile of v3, /device:TPU:8, one launch (start us, length us, event | category | flops | bytes accessed | tf_op | source)
XLA Modules:
  0.0 87.9 jit_solution(14474650307853874300)
XLA Ops:
  0.0 0.9 fusion.4
  0.9 1.1 %slice_bitcast_fusion.9 = (f32[128,128]{1,0:T(8,128)S(1)}, f32[128,128]{1,0:T(8,128)S(1)}, f32[128,128]{1,0:T(8,128)S(1)}, f32[128,128]{1,0:T(8,128)S(1)}, f32[1...) fusion(f32[6,512,128]{2,1,0:T(8,128)} %bitcast.62), kind=kLoop, calls=%fused_computation.23 | loop fusion | bytes 1048576 | tf_op jit(solution)/shard_map/squeeze | solution.py:327
  2.0 0.1 concatenate.36
  2.1 0.1 concatenate.35
  2.1 0.1 concatenate.34
  2.2 0.1 concatenate.37
  2.2 0.8 pad_maximum_fusion.3
  3.1 4.2 %all-to-all-start = ((f32[4,272,128]{2,1,0:T(8,128)}), f32[4,272,128]{2,1,0:T(8,128)S(1)}, u32[]{:S(2)}, u32[]{:S(2)}) async-start(f32[4,272,128]{2,1,0:T(8,128)} %pad_maximum_fusion.3), calls=%async_computation | async-start | bytes 1114112 | tf_op jit(solution)/shard_map/all_to_all | solution.py:329
  7.3 0.1 pad.30.clone
  7.4 0.0 copy-done
  7.4 0.1 constant_dynamic-slice_fusion
  7.4 0.9 %fusion.1 = (f32[784,128]{1,0:T(8,128)S(1)}, f32[784,128]{1,0:T(8,128)}) fusion(f32[6,128]{1,0:T(8,128)S(1)} %get-tuple-element.80, f32[768,128]{1,0:T(8,128)S(1)} %bitcast.65, f32[784]{0:T(1024)S(1)} %pad.30.clone, f32[768,128]{1,0:T(8,128)S(1)} %bitcast.66), kind=kLoop, calls=%fused_computation.5 | loop fusion | flops 401408 | bytes 1595456 | tf_op jit(solution)/shard_map/concatenate | solution.py:315
  8.4 3.0 %collective-permute-start.1 = (f32[784,128]{1,0:T(8,128)S(1)}, f32[784,128]{1,0:T(8,128)S(1)}, u32[]{:S(2)}, u32[]{:S(2)}) collective-permute-start(f32[784,128]{1,0:T(8,128)S(1)} %get-tuple-element.35), channel_id=1, source_target_pairs={{8,16},{9,17},{10,18},{11,19},{12,20},{13,21},{14,22},{15,23},{16,... | collective-permute-start | bytes 1204232 | tf_op jit(solution)/shard_map/ppermute | solution.py:318
  11.4 0.1 pad.16.clone
  11.5 0.0 copy-done.2
  11.5 0.0 copy-done.3
  11.5 0.1 select_reduce_fusion
  11.6 0.1 pad_dynamic-slice_fusion
  11.7 0.1 pad.12.clone
  11.8 0.1 fusion.3
  11.9 1.0 %pad_maximum_fusion = f32[4,512,128]{2,1,0:T(8,128)} fusion(f32[1,512,128]{2,1,0:T(8,128)S(1)} %bitcast.71, f32[1,512,128]{2,1,0:T(8,128)S(1)} %bitcast.70, f32[1,512,128]{2,1,0:T(8,128)S(1)} %bitcast.69, f32[1,512,128]{2,1,0:T(8,128)S(1)} %bitcast.68), kind=kLoop, calls=%fused_computation | loop fusion | flops 786432 | bytes 2097152 | tf_op jit(solution)/shard_map/stack | solution.py:330
  12.9 0.0 copy-done.1
  12.9 2.2 %all-to-all-done.refs_2_ = f32[4,272,128]{2,1,0:T(8,128)S(1)} async-done(((f32[4,272,128]{2,1,0:T(8,128)}), f32[4,272,128]{2,1,0:T(8,128)S(1)}, u32[]{:S(2)}, u32[]{:S(2)}) %all-to-all-start) | async-done | bytes 557088 | tf_op jit(solution)/shard_map/all_to_all | solution.py:329
  15.1 4.1 %all-to-all-start.1 = ((f32[4,512,128]{2,1,0:T(8,128)}), f32[4,512,128]{2,1,0:T(8,128)S(1)}, u32[]{:S(2)}, u32[]{:S(2)}) async-start(f32[4,512,128]{2,1,0:T(8,128)} %pad_maximum_fusion), calls=%async_computation.1 | async-start | bytes 2097152 | tf_op jit(solution)/shard_map/all_to_all | solution.py:330
  19.2 4.5 %collective-permute-start = (f32[784,128]{1,0:T(8,128)}, f32[784,128]{1,0:T(8,128)S(1)}, u32[]{:S(2)}, u32[]{:S(2)}) collective-permute-start(f32[784,128]{1,0:T(8,128)} %get-tuple-element.36), channel_id=1, source_target_pairs={{8,20},{9,21},{10,22},{11,23},{12,16},{13,17},{14,18},{15,19},{16,... | collective-permute-start | bytes 1204232 | tf_op jit(solution)/shard_map/ppermute | solution.py:332
  23.7 0.8 maximum_maximum_fusion.1
  24.5 0.9 %pad_maximum_fusion.4 = f32[688,128]{1,0:T(8,128)} fusion(f32[544,128]{1,0:T(8,128)S(1)} %bitcast.67, f32[688]{0:T(1024)S(1)} %pad.12.clone), kind=kLoop, calls=%fused_computation.6 | loop fusion | flops 88064 | bytes 633536 | tf_op jit(solution)/shard_map/concatenate | solution.py:351
  25.4 1.3 %collective-permute-start.2 = (f32[688,128]{1,0:T(8,128)}, f32[688,128]{1,0:T(8,128)S(1)}, u32[]{:S(2)}, u32[]{:S(2)}) collective-permute-start(f32[688,128]{1,0:T(8,128)} %pad_maximum_fusion.4), channel_id=1, source_target_pairs={{0,1},{1,2},{2,3},{4,5},{5,6},{6,7},{8,9},{9,10},{10,11},{12,13},{... | collective-permute-start | bytes 1056776 | tf_op jit(solution)/shard_map/ppermute | solution.py:353
  26.7 1.3 %collective-permute-start.3 = (f32[544,128]{1,0:T(8,128)}, f32[544,128]{1,0:T(8,128)S(1)}, u32[]{:S(2)}, u32[]{:S(2)}) collective-permute-start(f32[544,128]{1,0:T(8,128)} %bitcast.33), channel_id=1, source_target_pairs={{1,0},{2,1},{3,2},{5,4},{6,5},{7,6},{9,8},{10,9},{11,10},{13,12},{... | collective-permute-start | bytes 835592 | tf_op jit(solution)/shard_map/ppermute | solution.py:354
  28.1 0.0 collective-permute-done.1.s0
  28.1 4.1 %collective-permute-done.3.refs_5_ = f32[544,128]{1,0:T(8,128)S(1)} collective-permute-done((f32[544,128]{1,0:T(8,128)}, f32[544,128]{1,0:T(8,128)S(1)}, u32[]{:S(2)}, u32[]{:S(2)}) %collective-permute-start.3) | collective-permute-done | bytes 278560 | tf_op jit(solution)/shard_map/ppermute | solution.py:354
  32.1 0.0 collective-permute-done.2.refs_4_
  32.1 1.3 %collective-permute-start.5 = (f32[784,128]{1,0:T(8,128)}, f32[784,128]{1,0:T(8,128)S(1)}, u32[]{:S(2)}, u32[]{:S(2)}) collective-permute-start(f32[784,128]{1,0:T(8,128)} %copy-done.1), channel_id=1, source_target_pairs={{0,16},{1,17},{2,18},{3,19},{4,20},{5,21},{6,22},{7,23},{24,8},{25... | collective-permute-start | bytes 1204232 | tf_op jit(solution)/shard_map/ppermute | solution.py:360
  33.4 1.3 %collective-permute-done.s1 = f32[784,128]{1,0:T(8,128)S(1)} collective-permute-done((f32[784,128]{1,0:T(8,128)}, f32[784,128]{1,0:T(8,128)S(1)}, u32[]{:S(2)}, u32[]{:S(2)}) %collective-permute-start) | collective-permute-done | bytes 401440 | tf_op jit(solution)/shard_map/ppermute | solution.py:332
  34.7 1.3 %collective-permute-start.6 = (f32[784,128]{1,0:T(8,128)}, f32[784,128]{1,0:T(8,128)}, u32[]{:S(2)}, u32[]{:S(2)}) collective-permute-start(f32[784,128]{1,0:T(8,128)} %get-tuple-element.36), channel_id=1, source_target_pairs={{0,20},{1,21},{2,22},{3,23},{4,16},{5,17},{6,18},{7,19},{24,12},{2... | collective-permute-start | bytes 1204232 | tf_op jit(solution)/shard_map/ppermute | solution.py:360
  36.0 0.1 pad_add_fusion.refs_0_.side_ref
  36.1 0.1 pad_dynamic-slice_fusion.1
  36.2 0.1 add_select_fusion.refs_1_
  36.3 3.9 %all-to-all-done.1.refs_3_ = f32[4,512,128]{2,1,0:T(8,128)S(1)} async-done(((f32[4,512,128]{2,1,0:T(8,128)}), f32[4,512,128]{2,1,0:T(8,128)S(1)}, u32[]{:S(2)}, u32[]{:S(2)}) %all-to-all-start.1) | async-done | bytes 1048608 | tf_op jit(solution)/shard_map/all_to_all | solution.py:330
  40.2 0.2 broadcast_in_dim.41.refs_6_
  40.3 3.8 %shard_map.46 = (bf16[512,784]{1,0:T(8,128)(2,1)S(1)}, bf16[512,784]{1,0:T(8,128)(2,1)S(1)}, f32[2,2,128,256]{3,2,1,0:T(8,128)S(1)}, f32[2,2,128,256]{3,2,1,0:T(8,128)S(1)}) custom-call(s32[4]{0:T(128)S(1)} %pad_add_fusion.refs_0_.side_ref, f32[2]{0:T(128)S(1)} %add_select_fusion.refs_1_, f32[4,272,128]{2,1,0:T(8,128)S(1)} %all-to-all-done.refs_2_, ...), custom_call_target="tpu_custom_call" | custom-call | flops 1 | bytes 1 | tf_op jit(solution)/shard_map/pallas_call | solution.py:368
  44.2 0.1 collective-permute-start.4
  44.2 0.0 collective-permute-done.5.s2
  44.3 6.9 %collective-permute-done.6.s3 = f32[784,128]{1,0:T(8,128)} collective-permute-done((f32[784,128]{1,0:T(8,128)}, f32[784,128]{1,0:T(8,128)}, u32[]{:S(2)}, u32[]{:S(2)}) %collective-permute-start.6) | collective-permute-done | bytes 401440 | tf_op jit(solution)/shard_map/ppermute | solution.py:360
  51.2 2.9 %shard_map.47 = (f32[8,128,128]{2,1,0:T(8,128)S(1)}, f32[8,128,128]{2,1,0:T(8,128)S(1)}) custom-call(s32[4]{0:T(128)S(1)} %pad_add_fusion.refs_0_.side_ref, bf16[512,784]{1,0:T(8,128)(2,1)S(1)} %get-tuple-element.31.high_ref, bf16[512,784]{1,0:T(8,128)(2,1)S(1)} %get-tuple-element.32.low_ref, f32[784,128]{1,0:T(8,128)S(1)} %collective-permute-done.1.s0, ...), custom_call_target="tpu_custom_call" | custom-call | flops 99999997952 | bytes 1 | tf_op jit(solution)/shard_map/pallas_call | solution.py:383
  54.1 4.2 %collective-permute-start.7 = (f32[8,128,128]{2,1,0:T(8,128)S(1)}, f32[8,128,128]{2,1,0:T(8,128)S(1)}, u32[]{:S(2)}, u32[]{:S(2)}) collective-permute-start(f32[8,128,128]{2,1,0:T(8,128)S(1)} %get-tuple-element.38), channel_id=1, source_target_pairs={{0,1},{1,0},{2,3},{3,2},{4,5},{5,4},{6,7},{7,6},{8,9},{9,8},{10,11... | collective-permute-start | bytes 1572872 | tf_op jit(solution)/shard_map/ppermute | solution.py:380
  58.3 0.0 collective-permute-done.4
  58.3 0.1 add.54
  58.4 1.5 %collective-permute-done.7 = f32[8,128,128]{2,1,0:T(8,128)S(1)} collective-permute-done((f32[8,128,128]{2,1,0:T(8,128)S(1)}, f32[8,128,128]{2,1,0:T(8,128)S(1)}, u32[]{:S(2)}, u32[]{:S(2)}) %collective-permute-start.7) | collective-permute-done | bytes 524320 | tf_op jit(solution)/shard_map/ppermute | solution.py:380
  59.8 0.8 add.55
  60.7 3.5 %all-to-all-start.2 = ((f32[8,128,128]{2,1,0:T(8,128)}), f32[8,128,128]{2,1,0:T(8,128)S(1)}, u32[]{:S(2)}, u32[]{:S(2)}) async-start(f32[8,128,128]{2,1,0:T(8,128)} %add.55), calls=%async_computation.2 | async-start | bytes 1048576 | tf_op jit(solution)/shard_map/all_to_all | solution.py:406
  64.2 0.1 collective-permute-start.8
  64.3 8.5 %collective-permute-done.8 = f32[2,128,256]{2,1,0:T(8,128)S(1)} collective-permute-done((f32[2,128,256]{2,1,0:T(8,128)S(1)}, f32[2,128,256]{2,1,0:T(8,128)S(1)}, u32[]{:S(2)}, u32[]{:S(2)}) %collective-permute-start.8) | collective-permute-done | bytes 262176 | tf_op jit(solution)/shard_map/ppermute | solution.py:395
  72.9 2.0 %collective-permute-start.9 = (f32[128,256]{1,0:T(8,128)S(1)}, f32[128,256]{1,0:T(8,128)S(1)}, u32[]{:S(2)}, u32[]{:S(2)}) collective-permute-start(f32[128,256]{1,0:T(8,128)S(1)} %slice_bitcast_fusion.1), channel_id=1, source_target_pairs={{0,4},{4,0},{1,5},{5,1},{2,6},{6,2},{3,7},{7,3},{8,12},{12,8},{9,1... | collective-permute-start | bytes 393224 | tf_op jit(solution)/shard_map/ppermute | solution.py:396
  74.9 0.0 all-to-all-done.2
  74.9 0.1 copy.26
  75.0 3.1 %collective-permute-start.11 = (f32[128,128]{1,0:T(8,128)S(1)}, f32[128,128]{1,0:T(8,128)S(1)}, u32[]{:S(2)}, u32[]{:S(2)}) collective-permute-start(f32[128,128]{1,0:T(8,128)S(1)} %get-tuple-element.69), channel_id=1, source_target_pairs={{8,16},{9,24},{10,2},{11,3},{12,6},{13,7},{14,20},{15,28},{16,17},... | collective-permute-start | bytes 196616 | tf_op jit(solution)/shard_map/ppermute | solution.py:412
  78.2 1.3 %collective-permute-start.12 = (f32[128,128]{1,0:T(8,128)S(1)}, f32[128,128]{1,0:T(8,128)S(1)}, u32[]{:S(2)}, u32[]{:S(2)}) collective-permute-start(f32[128,128]{1,0:T(8,128)S(1)} %get-tuple-element.70), channel_id=1, source_target_pairs={{8,2},{9,3},{10,20},{11,28},{12,16},{13,24},{14,6},{15,7},{16,10},... | collective-permute-start | bytes 196616 | tf_op jit(solution)/shard_map/ppermute | solution.py:411
  79.5 0.0 collective-permute-done.9
  79.5 1.3 %collective-permute-start.10 = (f32[128,256]{1,0:T(8,128)S(1)}, f32[128,256]{1,0:T(8,128)S(1)}, u32[]{:S(2)}, u32[]{:S(2)}) collective-permute-start(f32[128,256]{1,0:T(8,128)S(1)} %fusion.2), channel_id=1, source_target_pairs={{2,0},{3,1},{6,4},{7,5},{10,8},{11,9},{14,12},{15,13},{16,18},{17,... | collective-permute-start | bytes 393224 | tf_op jit(solution)/shard_map/ppermute | solution.py:404
  80.8 0.0 collective-permute-done.11
  80.8 0.5 collective-permute-done.12
  81.4 5.9 %collective-permute-done.10 = f32[128,256]{1,0:T(8,128)S(1)} collective-permute-done((f32[128,256]{1,0:T(8,128)S(1)}, f32[128,256]{1,0:T(8,128)S(1)}, u32[]{:S(2)}, u32[]{:S(2)}) %collective-permute-start.10) | collective-permute-done | bytes 131104 | tf_op jit(solution)/shard_map/ppermute | solution.py:404
  87.2 0.7 maximum_select_fusion
  (23 shorter events, 0.2 us)
Async XLA Ops:
  2.1 5.3 %copy-start = (f32[3072,128]{1,0:T(8,128)S(1)}, f32[3072,128]{1,0:T(8,128)}, u32[]{:S(2)}) copy-start(f32[3072,128]{1,0:T(8,128)} %param.4) | copy-start | bytes 4718596
  3.1 12.0 %all-to-all-start = ((f32[4,272,128]{2,1,0:T(8,128)}), f32[4,272,128]{2,1,0:T(8,128)S(1)}, u32[]{:S(2)}, u32[]{:S(2)}) async-start(f32[4,272,128]{2,1,0:T(8,128)} %pad_maximum_fusion.3), calls=%async_computation | async-start | bytes 1114112 | tf_op jit(solution)/shard_map/all_to_all | solution.py:329
  7.4 4.1 %copy-start.2 = (s32[6,512]{1,0:T(8,128)S(1)}, s32[6,512]{1,0:T(8,128)}, u32[]{:S(2)}) copy-start(s32[6,512]{1,0:T(8,128)} %param.5) | copy-start | bytes 36868
  7.4 4.1 %copy-start.3 = (f32[8]{0:T(128)S(1)}, f32[8]{0:T(128)}, u32[]{:S(2)}) copy-start(f32[8]{0:T(128)} %param.6) | copy-start | bytes 100
  8.4 4.5 %copy-start.1 = (f32[784,128]{1,0:T(8,128)}, f32[784,128]{1,0:T(8,128)S(1)}, u32[]{:S(2)}) copy-start(f32[784,128]{1,0:T(8,128)S(1)} %get-tuple-element.35) | copy-start | bytes 1204228
  8.4 19.7 %collective-permute-start.1 = (f32[784,128]{1,0:T(8,128)S(1)}, f32[784,128]{1,0:T(8,128)S(1)}, u32[]{:S(2)}, u32[]{:S(2)}) collective-permute-start(f32[784,128]{1,0:T(8,128)S(1)} %get-tuple-element.35), channel_id=1, source_target_pairs={{8,16},{9,17},{10,18},{11,19},{12,20},{13,21},{14,22},{15,23},{16,... | collective-permute-start | bytes 1204232 | tf_op jit(solution)/shard_map/ppermute | solution.py:318
  15.1 25.1 %all-to-all-start.1 = ((f32[4,512,128]{2,1,0:T(8,128)}), f32[4,512,128]{2,1,0:T(8,128)S(1)}, u32[]{:S(2)}, u32[]{:S(2)}) async-start(f32[4,512,128]{2,1,0:T(8,128)} %pad_maximum_fusion), calls=%async_computation.1 | async-start | bytes 2097152 | tf_op jit(solution)/shard_map/all_to_all | solution.py:330
  19.2 17.0 %copy-start.4 = (f32[2]{0:T(128)S(1)}, f32[2]{0:T(128)}, u32[]{:S(2)}) copy-start(f32[2]{0:T(128)} %constant.59.clone) | copy-start | bytes 28
  19.2 15.6 %collective-permute-start = (f32[784,128]{1,0:T(8,128)}, f32[784,128]{1,0:T(8,128)S(1)}, u32[]{:S(2)}, u32[]{:S(2)}) collective-permute-start(f32[784,128]{1,0:T(8,128)} %get-tuple-element.36), channel_id=1, source_target_pairs={{8,20},{9,21},{10,22},{11,23},{12,16},{13,17},{14,18},{15,19},{16,... | collective-permute-start | bytes 1204232 | tf_op jit(solution)/shard_map/ppermute | solution.py:332
  25.4 6.7 %collective-permute-start.2 = (f32[688,128]{1,0:T(8,128)}, f32[688,128]{1,0:T(8,128)S(1)}, u32[]{:S(2)}, u32[]{:S(2)}) collective-permute-start(f32[688,128]{1,0:T(8,128)} %pad_maximum_fusion.4), channel_id=1, source_target_pairs={{0,1},{1,2},{2,3},{4,5},{5,6},{6,7},{8,9},{9,10},{10,11},{12,13},{... | collective-permute-start | bytes 1056776 | tf_op jit(solution)/shard_map/ppermute | solution.py:353
  26.7 5.4 %collective-permute-start.3 = (f32[544,128]{1,0:T(8,128)}, f32[544,128]{1,0:T(8,128)S(1)}, u32[]{:S(2)}, u32[]{:S(2)}) collective-permute-start(f32[544,128]{1,0:T(8,128)} %bitcast.33), channel_id=1, source_target_pairs={{1,0},{2,1},{3,2},{5,4},{6,5},{7,6},{9,8},{10,9},{11,10},{13,12},{... | collective-permute-start | bytes 835592 | tf_op jit(solution)/shard_map/ppermute | solution.py:354
  32.1 12.1 %collective-permute-start.5 = (f32[784,128]{1,0:T(8,128)}, f32[784,128]{1,0:T(8,128)S(1)}, u32[]{:S(2)}, u32[]{:S(2)}) collective-permute-start(f32[784,128]{1,0:T(8,128)} %copy-done.1), channel_id=1, source_target_pairs={{0,16},{1,17},{2,18},{3,19},{4,20},{5,21},{6,22},{7,23},{24,8},{25... | collective-permute-start | bytes 1204232 | tf_op jit(solution)/shard_map/ppermute | solution.py:360
  34.7 16.5 %collective-permute-start.6 = (f32[784,128]{1,0:T(8,128)}, f32[784,128]{1,0:T(8,128)}, u32[]{:S(2)}, u32[]{:S(2)}) collective-permute-start(f32[784,128]{1,0:T(8,128)} %get-tuple-element.36), channel_id=1, source_target_pairs={{0,20},{1,21},{2,22},{3,23},{4,16},{5,17},{6,18},{7,19},{24,12},{2... | collective-permute-start | bytes 1204232 | tf_op jit(solution)/shard_map/ppermute | solution.py:360
  44.2 14.1 %collective-permute-start.4 = (f32[2,2,128,256]{3,2,1,0:T(8,128)S(1)}, f32[2,2,128,256]{3,2,1,0:T(8,128)S(1)}, u32[]{:S(2)}, u32[]{:S(2)}) collective-permute-start(f32[2,2,128,256]{3,2,1,0:T(8,128)S(1)} %get-tuple-element.30), channel_id=1, source_target_pairs={{0,1},{1,0},{2,3},{3,2},{4,5},{5,4},{6,7},{7,6},{8,9},{9,8},{10,11... | collective-permute-start | bytes 1572872 | tf_op jit(solution)/shard_map/ppermute | solution.py:380
  54.1 5.7 %collective-permute-start.7 = (f32[8,128,128]{2,1,0:T(8,128)S(1)}, f32[8,128,128]{2,1,0:T(8,128)S(1)}, u32[]{:S(2)}, u32[]{:S(2)}) collective-permute-start(f32[8,128,128]{2,1,0:T(8,128)S(1)} %get-tuple-element.38), channel_id=1, source_target_pairs={{0,1},{1,0},{2,3},{3,2},{4,5},{5,4},{6,7},{7,6},{8,9},{9,8},{10,11... | collective-permute-start | bytes 1572872 | tf_op jit(solution)/shard_map/ppermute | solution.py:380
  60.7 14.2 %all-to-all-start.2 = ((f32[8,128,128]{2,1,0:T(8,128)}), f32[8,128,128]{2,1,0:T(8,128)S(1)}, u32[]{:S(2)}, u32[]{:S(2)}) async-start(f32[8,128,128]{2,1,0:T(8,128)} %add.55), calls=%async_computation.2 | async-start | bytes 1048576 | tf_op jit(solution)/shard_map/all_to_all | solution.py:406
  64.2 8.7 %collective-permute-start.8 = (f32[2,128,256]{2,1,0:T(8,128)S(1)}, f32[2,128,256]{2,1,0:T(8,128)S(1)}, u32[]{:S(2)}, u32[]{:S(2)}) collective-permute-start(f32[2,128,256]{2,1,0:T(8,128)S(1)} %slice_bitcast_fusion), channel_id=1, source_target_pairs={{0,8},{8,0},{1,9},{9,1},{2,10},{10,2},{3,11},{11,3},{4,12},{12,4},... | collective-permute-start | bytes 786440 | tf_op jit(solution)/shard_map/ppermute | solution.py:395
  72.9 6.6 %collective-permute-start.9 = (f32[128,256]{1,0:T(8,128)S(1)}, f32[128,256]{1,0:T(8,128)S(1)}, u32[]{:S(2)}, u32[]{:S(2)}) collective-permute-start(f32[128,256]{1,0:T(8,128)S(1)} %slice_bitcast_fusion.1), channel_id=1, source_target_pairs={{0,4},{4,0},{1,5},{5,1},{2,6},{6,2},{3,7},{7,3},{8,12},{12,8},{9,1... | collective-permute-start | bytes 393224 | tf_op jit(solution)/shard_map/ppermute | solution.py:396
  75.0 5.8 %collective-permute-start.11 = (f32[128,128]{1,0:T(8,128)S(1)}, f32[128,128]{1,0:T(8,128)S(1)}, u32[]{:S(2)}, u32[]{:S(2)}) collective-permute-start(f32[128,128]{1,0:T(8,128)S(1)} %get-tuple-element.69), channel_id=1, source_target_pairs={{8,16},{9,24},{10,2},{11,3},{12,6},{13,7},{14,20},{15,28},{16,17},... | collective-permute-start | bytes 196616 | tf_op jit(solution)/shard_map/ppermute | solution.py:412
  78.2 3.2 %collective-permute-start.12 = (f32[128,128]{1,0:T(8,128)S(1)}, f32[128,128]{1,0:T(8,128)S(1)}, u32[]{:S(2)}, u32[]{:S(2)}) collective-permute-start(f32[128,128]{1,0:T(8,128)S(1)} %get-tuple-element.70), channel_id=1, source_target_pairs={{8,2},{9,3},{10,20},{11,28},{12,16},{13,24},{14,6},{15,7},{16,10},... | collective-permute-start | bytes 196616 | tf_op jit(solution)/shard_map/ppermute | solution.py:411
  79.5 7.7 %collective-permute-start.10 = (f32[128,256]{1,0:T(8,128)S(1)}, f32[128,256]{1,0:T(8,128)S(1)}, u32[]{:S(2)}, u32[]{:S(2)}) collective-permute-start(f32[128,256]{1,0:T(8,128)S(1)} %fusion.2), channel_id=1, source_target_pairs={{2,0},{3,1},{6,4},{7,5},{10,8},{11,9},{14,12},{15,13},{16,18},{17,... | collective-permute-start | bytes 393224 | tf_op jit(solution)/shard_map/ppermute | solution.py:404

commit v4 on v3

--- a/solution.py
+++ b/solution.py
@@ -266,16 +266,20 @@
         turned_ref[...] = panel[...].T
 
 
-def cross_kernel(side_ref, high_ref, low_ref, s0, s1, s2, s3, mine_ref, other_ref, tiles):
+def early_kernel(high_ref, low_ref, s0, s1, s2, pair_ref, third_ref):
+    h0, l0 = split(s0[...])
+    h1, l1 = split(s1[...])
+    sh = jnp.concatenate([h0, h1], 1)
+    sl = jnp.concatenate([l0, l1], 1)
+    pair_ref[...] = product(high_ref[...], low_ref[...], sh, sl, turned=True)
+    sh, sl = split(s2[...])
+    third_ref[...] = product(high_ref[...], low_ref[...], sh, sl, turned=True)
+
+
+def cross_kernel(side_ref, high_ref, low_ref, last, pair_ref, third_ref, mine_ref, other_ref, fourth):
     core, half, x = side_ref[0], side_ref[1], side_ref[2]
-    for pair, (first, second) in enumerate(((s0, s1), (s2, s3))):
-        h0, l0 = split(first[...])
-        h1, l1 = split(second[...])
-        sh = jnp.concatenate([h0, h1], 1)
-        sl = jnp.concatenate([l0, l1], 1)
-        for a in range(2):
-            own = slice(a * 256, (a + 1) * 256)
-            tiles[pair, a] = product(high_ref[own], low_ref[own], sh, sl, turned=True)
+    sh, sl = split(last[...])
+    fourth[...] = product(high_ref[...], low_ref[...], sh, sl, turned=True)
 
     def place(h, c):
         for pair in range(2):
@@ -283,9 +287,11 @@
                 ref = mine_ref if (a if h else pair) == c else other_ref
                 for i in range(2):
                     for j in range(2):
-                        block = tiles[
-                            pair, a, i * GROUP : (i + 1) * GROUP, j * GROUP : (j + 1) * GROUP
-                        ]
+                        rows_of = slice((2 * a + i) * GROUP, (2 * a + i + 1) * GROUP)
+                        if pair == 0:
+                            block = pair_ref[rows_of, j * GROUP : (j + 1) * GROUP]
+                        else:
+                            block = (fourth if j else third_ref)[rows_of]
                         if h:
                             ref[(2 * (1 - pair) + (x ^ j)) * 2 + i] = block.T
                         else:
@@ -352,12 +358,10 @@
     below = edge(0, 0)
     above = lax.ppermute(above, TILE, [(m, m + 1) for m in range(3)])
     below = lax.ppermute(below, TILE, [(m + 1, m) for m in range(3)])
-    far = []
-    for flip in range(2):
-        half, near[flip], above, below = lax.optimization_barrier(
-            (halves[flip], near[flip], above, below)
-        )
-        far.append(lax.ppermute(half, ALL, crossing(True, flip)))
+    half, near[0], below = lax.optimization_barrier((halves[0], near[0], below))
+    far = [lax.ppermute(half, ALL, crossing(True, 0))]
+    half, near[1], above, below = lax.optimization_barrier((halves[1], near[1], above, below))
+    far.append(lax.ppermute(half, ALL, crossing(True, 1)))
 
     side = jnp.stack([c, h, x, l]).astype(jnp.int32)
     seam_side = jnp.stack([(h == 0) & (x == 1), (h == 1) & (x == 0)]).astype(jnp.float32)
@@ -380,15 +384,24 @@
         return mine + lax.ppermute(other, "c", [(0, 1), (1, 0)])
 
     own = both_cores(own_mine, own_other)
+    wide = [jax.ShapeDtypeStruct((4 * GROUP, n * GROUP), jnp.float32) for n in (2, 1)]
+    early = pl.pallas_call(
+        early_kernel,
+        out_shape=wide,
+        in_specs=[VMEM] * 5,
+        out_specs=[VMEM] * 2,
+        compiler_params=pltpu.CompilerParams(vmem_limit_bytes=40 * 1024 * 1024),
+        cost_estimate=pl.CostEstimate(flops=1, bytes_accessed=1, transcendentals=0),
+    )(high, low, *near, far[0])
     cross_mine, cross_other = pl.pallas_call(
         cross_kernel,
         out_shape=(blocks, blocks),
-        in_specs=[SMEM] + [VMEM] * 6,
+        in_specs=[SMEM] + [VMEM] * 5,
         out_specs=(VMEM,) * 2,
-        scratch_shapes=[pltpu.VMEM((2, 2, 256, 256), jnp.float32)],
+        scratch_shapes=[pltpu.VMEM((4 * GROUP, GROUP), jnp.float32)],
         compiler_params=pltpu.CompilerParams(vmem_limit_bytes=40 * 1024 * 1024),
         cost_estimate=pl.CostEstimate(flops=10**11, bytes_accessed=1, transcendentals=0),
-    )(side, high, low, *near, *far)
+    )(side, high, low, far[1], *early)
 
     cross = both_cores(cross_mine, cross_other)
     own, cross = lax.optimization_barrier((own, cross))

time: 88.6 us -> 87.7 us (0.990)
  waiting for transfers between devices: 34.8 us -> 33.1 us
    ppermute x2, waiting for transfers between devices: 6.95 us -> 5.25 us  [the longest x1 5.25 us: local_strips(): far.append(lax.ppermute(half, ALL, crossing(True, 1)))]
    pallas_call x0 -> x1, Pallas kernels: none -> 1.68 us  [local_strips(): pl.pallas_call(early_kernel, out_shape=wide, in_specs=[VMEM] * 5, out_spe...]
    pallas_call x1, Pallas kernels: 2.89 us -> 1.95 us  [local_strips(): pl.pallas_call(cross_kernel, out_shape=(blocks, blocks), in_specs=[SMEM]...]
  transfers between devices with their start and end apart: 16 -> 16, of which waited for: 9 -> 9; matrix products, arithmetic and copies ran while one was open for 6% -> 6% of each run, Pallas kernels for 8% -> 9%
where the time goes in v4:
time: 87.7 us; the launch traced here: 87 us
  starting transfers between devices  36.6 us (42%)
  waiting for transfers between devices  33.1 us (38%)
  Pallas kernels  7.44 us (8%)
  other arithmetic  6.5 us (7%)
  local copies, waits for them, and re-layouts  3.06 us (3%)
    ppermute x1, waiting for transfers between devices, local_strips(): own = own[0] + lax.ppermute(own[1], 'l', [(0, 1), (1, 0)])  8.54 us
    ppermute x1, waiting for transfers between devices, local_strips(): own = own + lax.ppermute(own, ALL, to_holder)  5.86 us
    ppermute x1, waiting for transfers between devices, local_strips(): far.append(lax.ppermute(half, ALL, crossing(True, 1)))  5.25 us
    ppermute x1, starting transfers between devices, local_strips(): near.append(lax.ppermute(half, ALL, crossing(False, 1)))  4.49 us
    ppermute x2, starting transfers between devices, both_cores(): return mine + lax.ppermute(other, 'c', [(0, 1), (1, 0)])  4.31 us
    all_to_all x1, starting transfers between devices, local_strips(): ends = lax.all_to_all(jnp.stack(ends), PLACE, 0, 0, tiled=True)  4.22 us
    all_to_all x1, starting transfers between devices, local_strips(): between = lax.all_to_all(jnp.stack(between), PLACE, 0, 0, tiled=True)  4.1 us
    ppermute x1, waiting for transfers between devices, local_strips(): below = lax.ppermute(below, TILE, [(m + 1, m) for m in range(3)])  4.07 us
  transfers between devices with their start and end apart: 16, of which 9 were waited for; matrix products, arithmetic and copies ran while one was open for 6% of the time, Pallas kernels for 9%

profile of v4, /device:TPU:8, one launch (start us, length us, event | category | flops | bytes accessed | tf_op | source)
XLA Modules:
  0.0 87.0 jit_solution(248905473660079435)
XLA Ops:
  0.0 0.9 %fusion.4 = (f32[6,1,128]{2,1,0:T(1,128)S(1)}, f32[6,1,128]{2,1,0:T(1,128)S(1)}, f32[6,1,128]{2,1,0:T(1,128)S(1)}, f32[6,1,128]{2,1,0:T(1,128)S(1)}, f32[6,1,128]{2,1,0:T(1,128)S(1)}, /*index=5*/f32[6,1,128]{2,1,0:T(1,128)S(1)}) fusion(f32[6,512,128]{2,1,0:T(8,128)} %bitcast.61), kind=kLoop, calls=%fused_computation.43 | loop fusion | bytes 36864 | tf_op jit(solution)/shard_map/slice | solution.py:331
  0.9 1.1 %slice_bitcast_fusion.9 = (f32[128,128]{1,0:T(8,128)S(1)}, f32[128,128]{1,0:T(8,128)S(1)}, f32[128,128]{1,0:T(8,128)S(1)}, f32[128,128]{1,0:T(8,128)S(1)}, f32[1...) fusion(f32[6,512,128]{2,1,0:T(8,128)} %bitcast.62), kind=kLoop, calls=%fused_computation.23 | loop fusion | bytes 1048576 | tf_op jit(solution)/shard_map/squeeze | solution.py:333
  2.0 0.1 concatenate.36
  2.1 0.1 concatenate.35
  2.1 0.1 concatenate.34
  2.2 0.1 concatenate.37
  2.2 0.8 pad_maximum_fusion.3
  3.1 4.2 %all-to-all-start = ((f32[4,272,128]{2,1,0:T(8,128)}), f32[4,272,128]{2,1,0:T(8,128)S(1)}, u32[]{:S(2)}, u32[]{:S(2)}) async-start(f32[4,272,128]{2,1,0:T(8,128)} %pad_maximum_fusion.3), calls=%async_computation | async-start | bytes 1114112 | tf_op jit(solution)/shard_map/all_to_all | solution.py:335
  7.3 0.1 pad.30.clone
  7.4 0.0 copy-done
  7.4 0.1 constant_dynamic-slice_fusion
  7.5 0.9 %fusion.1 = (f32[784,128]{1,0:T(8,128)S(1)}, f32[784,128]{1,0:T(8,128)}) fusion(f32[6,128]{1,0:T(8,128)S(1)} %get-tuple-element.82, f32[768,128]{1,0:T(8,128)S(1)} %bitcast.65, f32[784]{0:T(1024)S(1)} %pad.30.clone, f32[768,128]{1,0:T(8,128)S(1)} %bitcast.66), kind=kLoop, calls=%fused_computation.5 | loop fusion | flops 401408 | bytes 1595456 | tf_op jit(solution)/shard_map/concatenate | solution.py:321
  8.4 3.0 %collective-permute-start.2 = (f32[784,128]{1,0:T(8,128)S(1)}, f32[784,128]{1,0:T(8,128)S(1)}, u32[]{:S(2)}, u32[]{:S(2)}) collective-permute-start(f32[784,128]{1,0:T(8,128)S(1)} %get-tuple-element.36), channel_id=1, source_target_pairs={{8,16},{9,17},{10,18},{11,19},{12,20},{13,21},{14,22},{15,23},{16,... | collective-permute-start | bytes 1204232 | tf_op jit(solution)/shard_map/ppermute | solution.py:324
  11.4 0.1 pad.19.clone
  11.5 0.0 copy-done.2
  11.5 0.1 select_reduce_fusion
  11.6 0.1 pad_dynamic-slice_fusion
  11.7 0.1 pad.15.clone
  11.8 0.1 fusion.3
  11.9 1.0 %pad_maximum_fusion = f32[4,512,128]{2,1,0:T(8,128)} fusion(f32[1,512,128]{2,1,0:T(8,128)S(1)} %bitcast.71, f32[1,512,128]{2,1,0:T(8,128)S(1)} %bitcast.70, f32[1,512,128]{2,1,0:T(8,128)S(1)} %bitcast.69, f32[1,512,128]{2,1,0:T(8,128)S(1)} %bitcast.68), kind=kLoop, calls=%fused_computation | loop fusion | flops 786432 | bytes 2097152 | tf_op jit(solution)/shard_map/stack | solution.py:336
  12.9 2.2 %all-to-all-done.refs_2_ = f32[4,272,128]{2,1,0:T(8,128)S(1)} async-done(((f32[4,272,128]{2,1,0:T(8,128)}), f32[4,272,128]{2,1,0:T(8,128)S(1)}, u32[]{:S(2)}, u32[]{:S(2)}) %all-to-all-start) | async-done | bytes 557088 | tf_op jit(solution)/shard_map/all_to_all | solution.py:335
  15.1 4.1 %all-to-all-start.1 = ((f32[4,512,128]{2,1,0:T(8,128)}), f32[4,512,128]{2,1,0:T(8,128)S(1)}, u32[]{:S(2)}, u32[]{:S(2)}) async-start(f32[4,512,128]{2,1,0:T(8,128)} %pad_maximum_fusion), calls=%async_computation.1 | async-start | bytes 2097152 | tf_op jit(solution)/shard_map/all_to_all | solution.py:336
  19.2 4.5 %collective-permute-start = (f32[784,128]{1,0:T(8,128)}, f32[784,128]{1,0:T(8,128)S(1)}, u32[]{:S(2)}, u32[]{:S(2)}) collective-permute-start(f32[784,128]{1,0:T(8,128)} %get-tuple-element.33), channel_id=1, source_target_pairs={{8,20},{9,21},{10,22},{11,23},{12,16},{13,17},{14,18},{15,19},{16,... | collective-permute-start | bytes 1204232 | tf_op jit(solution)/shard_map/ppermute | solution.py:338
  23.7 0.8 maximum_maximum_fusion.1
  24.6 0.9 %pad_maximum_fusion.4 = f32[688,128]{1,0:T(8,128)} fusion(f32[544,128]{1,0:T(8,128)S(1)} %bitcast.67, f32[688]{0:T(1024)S(1)} %pad.15.clone), kind=kLoop, calls=%fused_computation.6 | loop fusion | flops 88064 | bytes 633536 | tf_op jit(solution)/shard_map/concatenate | solution.py:357
  25.5 1.3 %collective-permute-start.1 = (f32[688,128]{1,0:T(8,128)}, f32[688,128]{1,0:T(8,128)S(1)}, u32[]{:S(2)}, u32[]{:S(2)}) collective-permute-start(f32[688,128]{1,0:T(8,128)} %pad_maximum_fusion.4), channel_id=1, source_target_pairs={{0,1},{1,2},{2,3},{4,5},{5,6},{6,7},{8,9},{9,10},{10,11},{12,13},{... | collective-permute-start | bytes 1056776 | tf_op jit(solution)/shard_map/ppermute | solution.py:359
  26.8 1.3 %collective-permute-start.3 = (f32[544,128]{1,0:T(8,128)}, f32[544,128]{1,0:T(8,128)S(1)}, u32[]{:S(2)}, u32[]{:S(2)}) collective-permute-start(f32[544,128]{1,0:T(8,128)} %bitcast.33), channel_id=1, source_target_pairs={{1,0},{2,1},{3,2},{5,4},{6,5},{7,6},{9,8},{10,9},{11,10},{13,12},{... | collective-permute-start | bytes 835592 | tf_op jit(solution)/shard_map/ppermute | solution.py:360
  28.1 0.0 collective-permute-done.2.s0
  28.1 4.1 %collective-permute-done.3.refs_5_ = f32[544,128]{1,0:T(8,128)S(1)} collective-permute-done((f32[544,128]{1,0:T(8,128)}, f32[544,128]{1,0:T(8,128)S(1)}, u32[]{:S(2)}, u32[]{:S(2)}) %collective-permute-start.3) | collective-permute-done | bytes 278560 | tf_op jit(solution)/shard_map/ppermute | solution.py:360
  32.2 1.3 %collective-permute-start.6 = (f32[784,128]{1,0:T(8,128)}, f32[784,128]{1,0:T(8,128)S(1)}, u32[]{:S(2)}, u32[]{:S(2)}) collective-permute-start(f32[784,128]{1,0:T(8,128)} %copy-done.1), channel_id=1, source_target_pairs={{0,16},{1,17},{2,18},{3,19},{4,20},{5,21},{6,22},{7,23},{24,8},{25... | collective-permute-start | bytes 1204232 | tf_op jit(solution)/shard_map/ppermute | solution.py:362
  33.5 0.0 collective-permute-done.1.refs_4_
  33.5 1.3 %collective-permute-done.s1 = f32[784,128]{1,0:T(8,128)S(1)} collective-permute-done((f32[784,128]{1,0:T(8,128)}, f32[784,128]{1,0:T(8,128)S(1)}, u32[]{:S(2)}, u32[]{:S(2)}) %collective-permute-start) | collective-permute-done | bytes 401440 | tf_op jit(solution)/shard_map/ppermute | solution.py:338
  34.8 1.3 %collective-permute-start.5 = (f32[784,128]{1,0:T(8,128)}, f32[784,128]{1,0:T(8,128)}, u32[]{:S(2)}, u32[]{:S(2)}) collective-permute-start(f32[784,128]{1,0:T(8,128)} %get-tuple-element.33), channel_id=1, source_target_pairs={{0,20},{1,21},{2,22},{3,23},{4,16},{5,17},{6,18},{7,19},{24,12},{2... | collective-permute-start | bytes 1204232 | tf_op jit(solution)/shard_map/ppermute | solution.py:364
  36.0 0.1 pad_add_fusion.refs_0_.side_ref
  36.1 0.1 pad_dynamic-slice_fusion.1
  36.2 0.0 copy-done.4
  36.2 0.1 add_select_fusion.refs_1_
  36.3 3.9 %all-to-all-done.1.refs_3_ = f32[4,512,128]{2,1,0:T(8,128)S(1)} async-done(((f32[4,512,128]{2,1,0:T(8,128)}), f32[4,512,128]{2,1,0:T(8,128)S(1)}, u32[]{:S(2)}, u32[]{:S(2)}) %all-to-all-start.1) | async-done | bytes 1048608 | tf_op jit(solution)/shard_map/all_to_all | solution.py:336
  40.2 0.2 broadcast_in_dim.41.refs_6_
  40.4 3.8 %shard_map.46 = (bf16[512,784]{1,0:T(8,128)(2,1)S(1)}, bf16[512,784]{1,0:T(8,128)(2,1)S(1)}, f32[2,2,128,256]{3,2,1,0:T(8,128)S(1)}, f32[2,2,128,256]{3,2,1,0:T(8,128)S(1)}) custom-call(s32[4]{0:T(128)S(1)} %pad_add_fusion.refs_0_.side_ref, f32[2]{0:T(128)S(1)} %add_select_fusion.refs_1_, f32[4,272,128]{2,1,0:T(8,128)S(1)} %all-to-all-done.refs_2_, ...), custom_call_target="tpu_custom_call" | custom-call | flops 1 | bytes 1 | tf_op jit(solution)/shard_map/pallas_call | solution.py:372
  44.2 0.1 collective-permute-start.4
  44.3 0.0 collective-permute-done.6.s2
  44.3 1.7 %shard_map.47 = (f32[512,256]{1,0:T(8,128)S(1)}, f32[512,128]{1,0:T(8,128)S(1)}) custom-call(bf16[512,784]{1,0:T(8,128)(2,1)S(1)} %get-tuple-element.31.high_ref, bf16[512,784]{1,0:T(8,128)(2,1)S(1)} %get-tuple-element.32.low_ref, f32[784,128]{1,0:T(8,128)S(1)} %collective-permute-done.2.s0, f32[784,128]{1,0:T(8,128)S(1)} %collective-permute-done.s1, ...), custom_call_target="tpu_custom_call" | custom-call | flops 1 | bytes 1 | tf_op jit(solution)/shard_map/pallas_call | solution.py:388
  46.0 5.2 %collective-permute-done.5.last = f32[784,128]{1,0:T(8,128)} collective-permute-done((f32[784,128]{1,0:T(8,128)}, f32[784,128]{1,0:T(8,128)}, u32[]{:S(2)}, u32[]{:S(2)}) %collective-permute-start.5) | collective-permute-done | bytes 401440 | tf_op jit(solution)/shard_map/ppermute | solution.py:364
  51.2 1.9 %shard_map.48 = (f32[8,128,128]{2,1,0:T(8,128)S(1)}, f32[8,128,128]{2,1,0:T(8,128)S(1)}) custom-call(s32[4]{0:T(128)S(1)} %pad_add_fusion.refs_0_.side_ref, bf16[512,784]{1,0:T(8,128)(2,1)S(1)} %get-tuple-element.31.high_ref, bf16[512,784]{1,0:T(8,128)(2,1)S(1)} %get-tuple-element.32.low_ref, f32[784,128]{1,0:T(8,128)} %collective-permute-done.5.last, ...), custom_call_target="tpu_custom_call" | custom-call | flops 99999997952 | bytes 1 | tf_op jit(solution)/shard_map/pallas_call | solution.py:396
  53.2 4.2 %collective-permute-start.7 = (f32[8,128,128]{2,1,0:T(8,128)S(1)}, f32[8,128,128]{2,1,0:T(8,128)S(1)}, u32[]{:S(2)}, u32[]{:S(2)}) collective-permute-start(f32[8,128,128]{2,1,0:T(8,128)S(1)} %get-tuple-element.40), channel_id=1, source_target_pairs={{0,1},{1,0},{2,3},{3,2},{4,5},{5,4},{6,7},{7,6},{8,9},{9,8},{10,11... | collective-permute-start | bytes 1572872 | tf_op jit(solution)/shard_map/ppermute | solution.py:384
  57.4 0.0 collective-permute-done.4
  57.4 0.1 add.54
  57.4 1.5 %collective-permute-done.7 = f32[8,128,128]{2,1,0:T(8,128)S(1)} collective-permute-done((f32[8,128,128]{2,1,0:T(8,128)S(1)}, f32[8,128,128]{2,1,0:T(8,128)S(1)}, u32[]{:S(2)}, u32[]{:S(2)}) %collective-permute-start.7) | collective-permute-done | bytes 524320 | tf_op jit(solution)/shard_map/ppermute | solution.py:384
  58.9 0.9 add.55
  59.8 3.5 %all-to-all-start.2 = ((f32[8,128,128]{2,1,0:T(8,128)}), f32[8,128,128]{2,1,0:T(8,128)S(1)}, u32[]{:S(2)}, u32[]{:S(2)}) async-start(f32[8,128,128]{2,1,0:T(8,128)} %add.55), calls=%async_computation.2 | async-start | bytes 1048576 | tf_op jit(solution)/shard_map/all_to_all | solution.py:419
  63.3 0.1 collective-permute-start.8
  63.4 8.5 %collective-permute-done.8 = f32[2,128,256]{2,1,0:T(8,128)S(1)} collective-permute-done((f32[2,128,256]{2,1,0:T(8,128)S(1)}, f32[2,128,256]{2,1,0:T(8,128)S(1)}, u32[]{:S(2)}, u32[]{:S(2)}) %collective-permute-start.8) | collective-permute-done | bytes 262176 | tf_op jit(solution)/shard_map/ppermute | solution.py:408
  72.0 2.0 %collective-permute-start.9 = (f32[128,256]{1,0:T(8,128)S(1)}, f32[128,256]{1,0:T(8,128)S(1)}, u32[]{:S(2)}, u32[]{:S(2)}) collective-permute-start(f32[128,256]{1,0:T(8,128)S(1)} %slice_bitcast_fusion.1), channel_id=1, source_target_pairs={{0,4},{4,0},{1,5},{5,1},{2,6},{6,2},{3,7},{7,3},{8,12},{12,8},{9,1... | collective-permute-start | bytes 393224 | tf_op jit(solution)/shard_map/ppermute | solution.py:409
  74.0 0.0 all-to-all-done.2
  74.0 0.1 copy.26
  74.1 3.1 %collective-permute-start.11 = (f32[128,128]{1,0:T(8,128)S(1)}, f32[128,128]{1,0:T(8,128)S(1)}, u32[]{:S(2)}, u32[]{:S(2)}) collective-permute-start(f32[128,128]{1,0:T(8,128)S(1)} %get-tuple-element.71), channel_id=1, source_target_pairs={{8,16},{9,24},{10,2},{11,3},{12,6},{13,7},{14,20},{15,28},{16,17},... | collective-permute-start | bytes 196616 | tf_op jit(solution)/shard_map/ppermute | solution.py:425
  77.3 1.3 %collective-permute-start.12 = (f32[128,128]{1,0:T(8,128)S(1)}, f32[128,128]{1,0:T(8,128)S(1)}, u32[]{:S(2)}, u32[]{:S(2)}) collective-permute-start(f32[128,128]{1,0:T(8,128)S(1)} %get-tuple-element.72), channel_id=1, source_target_pairs={{8,2},{9,3},{10,20},{11,28},{12,16},{13,24},{14,6},{15,7},{16,10},... | collective-permute-start | bytes 196616 | tf_op jit(solution)/shard_map/ppermute | solution.py:424
  78.6 0.0 collective-permute-done.9
  78.6 1.3 %collective-permute-start.10 = (f32[128,256]{1,0:T(8,128)S(1)}, f32[128,256]{1,0:T(8,128)S(1)}, u32[]{:S(2)}, u32[]{:S(2)}) collective-permute-start(f32[128,256]{1,0:T(8,128)S(1)} %fusion.2), channel_id=1, source_target_pairs={{2,0},{3,1},{6,4},{7,5},{10,8},{11,9},{14,12},{15,13},{16,18},{17,... | collective-permute-start | bytes 393224 | tf_op jit(solution)/shard_map/ppermute | solution.py:417
  79.9 0.0 collective-permute-done.11
  79.9 0.5 collective-permute-done.12
  80.5 5.9 %collective-permute-done.10 = f32[128,256]{1,0:T(8,128)S(1)} collective-permute-done((f32[128,256]{1,0:T(8,128)S(1)}, f32[128,256]{1,0:T(8,128)S(1)}, u32[]{:S(2)}, u32[]{:S(2)}) %collective-permute-start.10) | collective-permute-done | bytes 131104 | tf_op jit(solution)/shard_map/ppermute | solution.py:417
  86.3 0.7 maximum_select_fusion
  (24 shorter events, 0.2 us)
Async XLA Ops:
  2.1 5.3 %copy-start = (f32[3072,128]{1,0:T(8,128)S(1)}, f32[3072,128]{1,0:T(8,128)}, u32[]{:S(2)}) copy-start(f32[3072,128]{1,0:T(8,128)} %param.4) | copy-start | bytes 4718596
  3.1 12.0 %all-to-all-start = ((f32[4,272,128]{2,1,0:T(8,128)}), f32[4,272,128]{2,1,0:T(8,128)S(1)}, u32[]{:S(2)}, u32[]{:S(2)}) async-start(f32[4,272,128]{2,1,0:T(8,128)} %pad_maximum_fusion.3), calls=%async_computation | async-start | bytes 1114112 | tf_op jit(solution)/shard_map/all_to_all | solution.py:335
  7.4 4.1 %copy-start.2 = (s32[6,512]{1,0:T(8,128)S(1)}, s32[6,512]{1,0:T(8,128)}, u32[]{:S(2)}) copy-start(s32[6,512]{1,0:T(8,128)} %param.5) | copy-start | bytes 36868
  7.4 4.1 %copy-start.3 = (f32[8]{0:T(128)S(1)}, f32[8]{0:T(128)}, u32[]{:S(2)}) copy-start(f32[8]{0:T(128)} %param.6) | copy-start | bytes 100
  8.4 4.5 %copy-start.1 = (f32[784,128]{1,0:T(8,128)}, f32[784,128]{1,0:T(8,128)S(1)}, u32[]{:S(2)}) copy-start(f32[784,128]{1,0:T(8,128)S(1)} %get-tuple-element.36) | copy-start | bytes 1204228
  8.4 19.7 %collective-permute-start.2 = (f32[784,128]{1,0:T(8,128)S(1)}, f32[784,128]{1,0:T(8,128)S(1)}, u32[]{:S(2)}, u32[]{:S(2)}) collective-permute-start(f32[784,128]{1,0:T(8,128)S(1)} %get-tuple-element.36), channel_id=1, source_target_pairs={{8,16},{9,17},{10,18},{11,19},{12,20},{13,21},{14,22},{15,23},{16,... | collective-permute-start | bytes 1204232 | tf_op jit(solution)/shard_map/ppermute | solution.py:324
  15.1 25.1 %all-to-all-start.1 = ((f32[4,512,128]{2,1,0:T(8,128)}), f32[4,512,128]{2,1,0:T(8,128)S(1)}, u32[]{:S(2)}, u32[]{:S(2)}) async-start(f32[4,512,128]{2,1,0:T(8,128)} %pad_maximum_fusion), calls=%async_computation.1 | async-start | bytes 2097152 | tf_op jit(solution)/shard_map/all_to_all | solution.py:336
  19.2 17.0 %copy-start.4 = (f32[2]{0:T(128)S(1)}, f32[2]{0:T(128)}, u32[]{:S(2)}) copy-start(f32[2]{0:T(128)} %constant.59.clone) | copy-start | bytes 28
  19.2 15.6 %collective-permute-start = (f32[784,128]{1,0:T(8,128)}, f32[784,128]{1,0:T(8,128)S(1)}, u32[]{:S(2)}, u32[]{:S(2)}) collective-permute-start(f32[784,128]{1,0:T(8,128)} %get-tuple-element.33), channel_id=1, source_target_pairs={{8,20},{9,21},{10,22},{11,23},{12,16},{13,17},{14,18},{15,19},{16,... | collective-permute-start | bytes 1204232 | tf_op jit(solution)/shard_map/ppermute | solution.py:338
  25.5 8.0 %collective-permute-start.1 = (f32[688,128]{1,0:T(8,128)}, f32[688,128]{1,0:T(8,128)S(1)}, u32[]{:S(2)}, u32[]{:S(2)}) collective-permute-start(f32[688,128]{1,0:T(8,128)} %pad_maximum_fusion.4), channel_id=1, source_target_pairs={{0,1},{1,2},{2,3},{4,5},{5,6},{6,7},{8,9},{9,10},{10,11},{12,13},{... | collective-permute-start | bytes 1056776 | tf_op jit(solution)/shard_map/ppermute | solution.py:359
  26.8 5.4 %collective-permute-start.3 = (f32[544,128]{1,0:T(8,128)}, f32[544,128]{1,0:T(8,128)S(1)}, u32[]{:S(2)}, u32[]{:S(2)}) collective-permute-start(f32[544,128]{1,0:T(8,128)} %bitcast.33), channel_id=1, source_target_pairs={{1,0},{2,1},{3,2},{5,4},{6,5},{7,6},{9,8},{10,9},{11,10},{13,12},{... | collective-permute-start | bytes 835592 | tf_op jit(solution)/shard_map/ppermute | solution.py:360
  32.2 12.1 %collective-permute-start.6 = (f32[784,128]{1,0:T(8,128)}, f32[784,128]{1,0:T(8,128)S(1)}, u32[]{:S(2)}, u32[]{:S(2)}) collective-permute-start(f32[784,128]{1,0:T(8,128)} %copy-done.1), channel_id=1, source_target_pairs={{0,16},{1,17},{2,18},{3,19},{4,20},{5,21},{6,22},{7,23},{24,8},{25... | collective-permute-start | bytes 1204232 | tf_op jit(solution)/shard_map/ppermute | solution.py:362
  34.8 16.5 %collective-permute-start.5 = (f32[784,128]{1,0:T(8,128)}, f32[784,128]{1,0:T(8,128)}, u32[]{:S(2)}, u32[]{:S(2)}) collective-permute-start(f32[784,128]{1,0:T(8,128)} %get-tuple-element.33), channel_id=1, source_target_pairs={{0,20},{1,21},{2,22},{3,23},{4,16},{5,17},{6,18},{7,19},{24,12},{2... | collective-permute-start | bytes 1204232 | tf_op jit(solution)/shard_map/ppermute | solution.py:364
  44.2 13.2 %collective-permute-start.4 = (f32[2,2,128,256]{3,2,1,0:T(8,128)S(1)}, f32[2,2,128,256]{3,2,1,0:T(8,128)S(1)}, u32[]{:S(2)}, u32[]{:S(2)}) collective-permute-start(f32[2,2,128,256]{3,2,1,0:T(8,128)S(1)} %get-tuple-element.30), channel_id=1, source_target_pairs={{0,1},{1,0},{2,3},{3,2},{4,5},{5,4},{6,7},{7,6},{8,9},{9,8},{10,11... | collective-permute-start | bytes 1572872 | tf_op jit(solution)/shard_map/ppermute | solution.py:384
  53.2 5.7 %collective-permute-start.7 = (f32[8,128,128]{2,1,0:T(8,128)S(1)}, f32[8,128,128]{2,1,0:T(8,128)S(1)}, u32[]{:S(2)}, u32[]{:S(2)}) collective-permute-start(f32[8,128,128]{2,1,0:T(8,128)S(1)} %get-tuple-element.40), channel_id=1, source_target_pairs={{0,1},{1,0},{2,3},{3,2},{4,5},{5,4},{6,7},{7,6},{8,9},{9,8},{10,11... | collective-permute-start | bytes 1572872 | tf_op jit(solution)/shard_map/ppermute | solution.py:384
  59.8 14.2 %all-to-all-start.2 = ((f32[8,128,128]{2,1,0:T(8,128)}), f32[8,128,128]{2,1,0:T(8,128)S(1)}, u32[]{:S(2)}, u32[]{:S(2)}) async-start(f32[8,128,128]{2,1,0:T(8,128)} %add.55), calls=%async_computation.2 | async-start | bytes 1048576 | tf_op jit(solution)/shard_map/all_to_all | solution.py:419
  63.3 8.7 %collective-permute-start.8 = (f32[2,128,256]{2,1,0:T(8,128)S(1)}, f32[2,128,256]{2,1,0:T(8,128)S(1)}, u32[]{:S(2)}, u32[]{:S(2)}) collective-permute-start(f32[2,128,256]{2,1,0:T(8,128)S(1)} %slice_bitcast_fusion), channel_id=1, source_target_pairs={{0,8},{8,0},{1,9},{9,1},{2,10},{10,2},{3,11},{11,3},{4,12},{12,4},... | collective-permute-start | bytes 786440 | tf_op jit(solution)/shard_map/ppermute | solution.py:408
  72.0 6.6 %collective-permute-start.9 = (f32[128,256]{1,0:T(8,128)S(1)}, f32[128,256]{1,0:T(8,128)S(1)}, u32[]{:S(2)}, u32[]{:S(2)}) collective-permute-start(f32[128,256]{1,0:T(8,128)S(1)} %slice_bitcast_fusion.1), channel_id=1, source_target_pairs={{0,4},{4,0},{1,5},{5,1},{2,6},{6,2},{3,7},{7,3},{8,12},{12,8},{9,1... | collective-permute-start | bytes 393224 | tf_op jit(solution)/shard_map/ppermute | solution.py:409
  74.1 5.8 %collective-permute-start.11 = (f32[128,128]{1,0:T(8,128)S(1)}, f32[128,128]{1,0:T(8,128)S(1)}, u32[]{:S(2)}, u32[]{:S(2)}) collective-permute-start(f32[128,128]{1,0:T(8,128)S(1)} %get-tuple-element.71), channel_id=1, source_target_pairs={{8,16},{9,24},{10,2},{11,3},{12,6},{13,7},{14,20},{15,28},{16,17},... | collective-permute-start | bytes 196616 | tf_op jit(solution)/shard_map/ppermute | solution.py:425
  77.3 3.2 %collective-permute-start.12 = (f32[128,128]{1,0:T(8,128)S(1)}, f32[128,128]{1,0:T(8,128)S(1)}, u32[]{:S(2)}, u32[]{:S(2)}) collective-permute-start(f32[128,128]{1,0:T(8,128)S(1)} %get-tuple-element.72), channel_id=1, source_target_pairs={{8,2},{9,3},{10,20},{11,28},{12,16},{13,24},{14,6},{15,7},{16,10},... | collective-permute-start | bytes 196616 | tf_op jit(solution)/shard_map/ppermute | solution.py:424
  78.6 7.7 %collective-permute-start.10 = (f32[128,256]{1,0:T(8,128)S(1)}, f32[128,256]{1,0:T(8,128)S(1)}, u32[]{:S(2)}, u32[]{:S(2)}) collective-permute-start(f32[128,256]{1,0:T(8,128)S(1)} %fusion.2), channel_id=1, source_target_pairs={{2,0},{3,1},{6,4},{7,5},{10,8},{11,9},{14,12},{15,13},{16,18},{17,... | collective-permute-start | bytes 393224 | tf_op jit(solution)/shard_map/ppermute | solution.py:417

commit v5 on v4

--- a/solution.py
+++ b/solution.py
@@ -400,7 +400,7 @@
         out_specs=(VMEM,) * 2,
         scratch_shapes=[pltpu.VMEM((4 * GROUP, GROUP), jnp.float32)],
         compiler_params=pltpu.CompilerParams(vmem_limit_bytes=40 * 1024 * 1024),
-        cost_estimate=pl.CostEstimate(flops=10**11, bytes_accessed=1, transcendentals=0),
+        cost_estimate=pl.CostEstimate(flops=1, bytes_accessed=1, transcendentals=0),
     )(side, high, low, far[1], *early)
 
     cross = both_cores(cross_mine, cross_other)

time: 87.7 us -> 87.1 us (level)
  waiting for transfers between devices: 33.1 us -> 30.5 us
  local copies, waits for them, and re-layouts: 3.06 us -> 4.77 us
    ppermute x1, waiting for transfers between devices: 5.25 us -> 3.44 us  [local_strips(): far.append(lax.ppermute(half, ALL, crossing(True, 1)))]
    unnamed x10 -> x14, local copies, waits for them, and re-layouts: 0.02 us -> 1.73 us
  transfers between devices with their start and end apart: 16 -> 16, of which waited for: 9 -> 9; matrix products, arithmetic and copies ran while one was open for 6% -> 6% of each run, Pallas kernels for 9% -> 8%
where the time goes in v5:
time: 87.1 us; the launch traced here: 86.4 us
  starting transfers between devices  37.3 us (43%)
  waiting for transfers between devices  30.5 us (35%)
  Pallas kernels  6.96 us (8%)
  other arithmetic  6.52 us (7%)
  local copies, waits for them, and re-layouts  4.77 us (5%)
    ppermute x1, waiting for transfers between devices, local_strips(): own = own[0] + lax.ppermute(own[1], 'l', [(0, 1), (1, 0)])  8.54 us
    ppermute x1, waiting for transfers between devices, local_strips(): own = own + lax.ppermute(own, ALL, to_holder)  5.86 us
    ppermute x2, starting transfers between devices, both_cores(): return mine + lax.ppermute(other, 'c', [(0, 1), (1, 0)])  5.03 us
    ppermute x1, starting transfers between devices, local_strips(): near.append(lax.ppermute(half, ALL, crossing(False, 1)))  4.49 us
    all_to_all x1, starting transfers between devices, local_strips(): ends = lax.all_to_all(jnp.stack(ends), PLACE, 0, 0, tiled=True)  4.22 us
    all_to_all x1, starting transfers between devices, local_strips(): between = lax.all_to_all(jnp.stack(between), PLACE, 0, 0, tiled=True)  4.1 us
    ppermute x1, waiting for transfers between devices, local_strips(): below = lax.ppermute(below, TILE, [(m + 1, m) for m in range(3)])  4.07 us
    all_to_all x1, waiting for transfers between devices, local_strips(): between = lax.all_to_all(jnp.stack(between), PLACE, 0, 0, tiled=True)  3.89 us
  transfers between devices with their start and end apart: 16, of which 9 were waited for; matrix products, arithmetic and copies ran while one was open for 6% of the time, Pallas kernels for 8%

profile of v5, /device:TPU:8, one launch (start us, length us, event | category | flops | bytes accessed | tf_op | source)
XLA Modules:
  0.0 86.4 jit_solution(10409534160387723957)
XLA Ops:
  0.0 0.9 %fusion.4 = (f32[6,1,128]{2,1,0:T(1,128)S(1)}, f32[6,1,128]{2,1,0:T(1,128)S(1)}, f32[6,1,128]{2,1,0:T(1,128)S(1)}, f32[6,1,128]{2,1,0:T(1,128)S(1)}, f32[6,1,128]{2,1,0:T(1,128)S(1)}, /*index=5*/f32[6,1,128]{2,1,0:T(1,128)S(1)}) fusion(f32[6,512,128]{2,1,0:T(8,128)} %bitcast.61), kind=kLoop, calls=%fused_computation.43 | loop fusion | bytes 36864 | tf_op jit(solution)/shard_map/slice | solution.py:331
  0.9 1.1 %slice_bitcast_fusion.9 = (f32[128,128]{1,0:T(8,128)S(1)}, f32[128,128]{1,0:T(8,128)S(1)}, f32[128,128]{1,0:T(8,128)S(1)}, f32[128,128]{1,0:T(8,128)S(1)}, f32[1...) fusion(f32[6,512,128]{2,1,0:T(8,128)} %bitcast.62), kind=kLoop, calls=%fused_computation.23 | loop fusion | bytes 1048576 | tf_op jit(solution)/shard_map/squeeze | solution.py:333
  2.0 0.1 concatenate.36
  2.1 0.1 concatenate.35
  2.1 0.1 concatenate.34
  2.2 0.1 concatenate.37
  2.2 0.9 pad_maximum_fusion.3
  3.1 4.2 %all-to-all-start = ((f32[4,272,128]{2,1,0:T(8,128)}), f32[4,272,128]{2,1,0:T(8,128)S(1)}, u32[]{:S(2)}, u32[]{:S(2)}) async-start(f32[4,272,128]{2,1,0:T(8,128)} %pad_maximum_fusion.3), calls=%async_computation | async-start | bytes 1114112 | tf_op jit(solution)/shard_map/all_to_all | solution.py:335
  7.3 0.1 pad.30.clone
  7.4 0.0 copy-done.2
  7.4 0.1 constant_dynamic-slice_fusion
  7.5 0.9 %fusion.1 = (f32[784,128]{1,0:T(8,128)S(1)}, f32[784,128]{1,0:T(8,128)}) fusion(f32[6,128]{1,0:T(8,128)S(1)} %get-tuple-element.82, f32[768,128]{1,0:T(8,128)S(1)} %bitcast.65, f32[784]{0:T(1024)S(1)} %pad.30.clone, f32[768,128]{1,0:T(8,128)S(1)} %bitcast.66), kind=kLoop, calls=%fused_computation.5 | loop fusion | flops 401408 | bytes 1595456 | tf_op jit(solution)/shard_map/concatenate | solution.py:321
  8.4 3.0 %collective-permute-start.2 = (f32[784,128]{1,0:T(8,128)S(1)}, f32[784,128]{1,0:T(8,128)S(1)}, u32[]{:S(2)}, u32[]{:S(2)}) collective-permute-start(f32[784,128]{1,0:T(8,128)S(1)} %get-tuple-element.36), channel_id=1, source_target_pairs={{8,16},{9,17},{10,18},{11,19},{12,20},{13,21},{14,22},{15,23},{16,... | collective-permute-start | bytes 1204232 | tf_op jit(solution)/shard_map/ppermute | solution.py:324
  11.5 0.1 pad.19.clone
  11.5 0.1 select_reduce_fusion
  11.6 0.1 pad_dynamic-slice_fusion
  11.7 0.1 pad.15.clone
  11.8 0.1 fusion.3
  11.9 1.0 %pad_maximum_fusion = f32[4,512,128]{2,1,0:T(8,128)} fusion(f32[1,512,128]{2,1,0:T(8,128)S(1)} %bitcast.71, f32[1,512,128]{2,1,0:T(8,128)S(1)} %bitcast.70, f32[1,512,128]{2,1,0:T(8,128)S(1)} %bitcast.69, f32[1,512,128]{2,1,0:T(8,128)S(1)} %bitcast.68), kind=kLoop, calls=%fused_computation | loop fusion | flops 786432 | bytes 2097152 | tf_op jit(solution)/shard_map/stack | solution.py:336
  12.9 2.1 %all-to-all-done.refs_2_ = f32[4,272,128]{2,1,0:T(8,128)S(1)} async-done(((f32[4,272,128]{2,1,0:T(8,128)}), f32[4,272,128]{2,1,0:T(8,128)S(1)}, u32[]{:S(2)}, u32[]{:S(2)}) %all-to-all-start) | async-done | bytes 557088 | tf_op jit(solution)/shard_map/all_to_all | solution.py:335
  15.1 4.1 %all-to-all-start.1 = ((f32[4,512,128]{2,1,0:T(8,128)}), f32[4,512,128]{2,1,0:T(8,128)S(1)}, u32[]{:S(2)}, u32[]{:S(2)}) async-start(f32[4,512,128]{2,1,0:T(8,128)} %pad_maximum_fusion), calls=%async_computation.1 | async-start | bytes 2097152 | tf_op jit(solution)/shard_map/all_to_all | solution.py:336
  19.2 4.5 %collective-permute-start = (f32[784,128]{1,0:T(8,128)}, f32[784,128]{1,0:T(8,128)S(1)}, u32[]{:S(2)}, u32[]{:S(2)}) collective-permute-start(f32[784,128]{1,0:T(8,128)} %get-tuple-element.33), channel_id=1, source_target_pairs={{8,20},{9,21},{10,22},{11,23},{12,16},{13,17},{14,18},{15,19},{16,... | collective-permute-start | bytes 1204232 | tf_op jit(solution)/shard_map/ppermute | solution.py:338
  23.7 0.8 maximum_maximum_fusion.1
  24.6 0.9 %pad_maximum_fusion.4 = f32[688,128]{1,0:T(8,128)} fusion(f32[544,128]{1,0:T(8,128)S(1)} %bitcast.67, f32[688]{0:T(1024)S(1)} %pad.15.clone), kind=kLoop, calls=%fused_computation.6 | loop fusion | flops 88064 | bytes 633536 | tf_op jit(solution)/shard_map/concatenate | solution.py:357
  25.5 1.3 %collective-permute-start.1 = (f32[688,128]{1,0:T(8,128)}, f32[688,128]{1,0:T(8,128)S(1)}, u32[]{:S(2)}, u32[]{:S(2)}) collective-permute-start(f32[688,128]{1,0:T(8,128)} %pad_maximum_fusion.4), channel_id=1, source_target_pairs={{0,1},{1,2},{2,3},{4,5},{5,6},{6,7},{8,9},{9,10},{10,11},{12,13},{... | collective-permute-start | bytes 1056776 | tf_op jit(solution)/shard_map/ppermute | solution.py:359
  26.8 1.3 %collective-permute-start.3 = (f32[544,128]{1,0:T(8,128)}, f32[544,128]{1,0:T(8,128)S(1)}, u32[]{:S(2)}, u32[]{:S(2)}) collective-permute-start(f32[544,128]{1,0:T(8,128)} %bitcast.33), channel_id=1, source_target_pairs={{1,0},{2,1},{3,2},{5,4},{6,5},{7,6},{9,8},{10,9},{11,10},{13,12},{... | collective-permute-start | bytes 835592 | tf_op jit(solution)/shard_map/ppermute | solution.py:360
  28.1 0.0 collective-permute-done.2.s0
  28.1 4.1 %collective-permute-done.3.refs_5_ = f32[544,128]{1,0:T(8,128)S(1)} collective-permute-done((f32[544,128]{1,0:T(8,128)}, f32[544,128]{1,0:T(8,128)S(1)}, u32[]{:S(2)}, u32[]{:S(2)}) %collective-permute-start.3) | collective-permute-done | bytes 278560 | tf_op jit(solution)/shard_map/ppermute | solution.py:360
  32.2 1.3 %collective-permute-start.6 = (f32[784,128]{1,0:T(8,128)}, f32[784,128]{1,0:T(8,128)S(1)}, u32[]{:S(2)}, u32[]{:S(2)}) collective-permute-start(f32[784,128]{1,0:T(8,128)} %copy-done.3), channel_id=1, source_target_pairs={{0,16},{1,17},{2,18},{3,19},{4,20},{5,21},{6,22},{7,23},{24,8},{25... | collective-permute-start | bytes 1204232 | tf_op jit(solution)/shard_map/ppermute | solution.py:362
  33.5 0.0 collective-permute-done.1.refs_4_
  33.5 0.7 copy-done
  34.2 0.6 collective-permute-done.s1
  34.8 1.3 %collective-permute-start.5 = (f32[784,128]{1,0:T(8,128)}, f32[784,128]{1,0:T(8,128)S(1)}, u32[]{:S(2)}, u32[]{:S(2)}) collective-permute-start(f32[784,128]{1,0:T(8,128)} %get-tuple-element.33), channel_id=1, source_target_pairs={{0,20},{1,21},{2,22},{3,23},{4,16},{5,17},{6,18},{7,19},{24,12},{2... | collective-permute-start | bytes 1204232 | tf_op jit(solution)/shard_map/ppermute | solution.py:364
  36.1 0.1 pad_add_fusion.refs_0_.side_ref
  36.1 0.1 pad_dynamic-slice_fusion.1
  36.2 0.1 add_select_fusion.refs_1_
  36.3 3.9 %all-to-all-done.1.refs_3_ = f32[4,512,128]{2,1,0:T(8,128)S(1)} async-done(((f32[4,512,128]{2,1,0:T(8,128)}), f32[4,512,128]{2,1,0:T(8,128)S(1)}, u32[]{:S(2)}, u32[]{:S(2)}) %all-to-all-start.1) | async-done | bytes 1048608 | tf_op jit(solution)/shard_map/all_to_all | solution.py:336
  40.2 0.2 broadcast_in_dim.41.refs_6_
  40.4 1.0 %copy-done.1 = f32[688,128]{1,0:T(8,128)S(1)} copy-done((f32[688,128]{1,0:T(8,128)S(1)}, f32[688,128]{1,0:T(8,128)}, u32[]{:S(2)}) %copy-start.1) | copy-done | bytes 352280
  41.4 3.8 %shard_map.46 = (bf16[512,784]{1,0:T(8,128)(2,1)S(1)}, bf16[512,784]{1,0:T(8,128)(2,1)S(1)}, f32[2,2,128,256]{3,2,1,0:T(8,128)S(1)}, f32[2,2,128,256]{3,2,1,0:T(8,128)S(1)}) custom-call(s32[4]{0:T(128)S(1)} %pad_add_fusion.refs_0_.side_ref, f32[2]{0:T(128)S(1)} %add_select_fusion.refs_1_, f32[4,272,128]{2,1,0:T(8,128)S(1)} %all-to-all-done.refs_2_, ...), custom_call_target="tpu_custom_call" | custom-call | flops 1 | bytes 1 | tf_op jit(solution)/shard_map/pallas_call | solution.py:372
  45.2 0.8 collective-permute-start.4
  46.0 0.0 collective-permute-done.6.s2
  46.0 1.7 %shard_map.47 = (f32[512,256]{1,0:T(8,128)S(1)}, f32[512,128]{1,0:T(8,128)S(1)}) custom-call(bf16[512,784]{1,0:T(8,128)(2,1)S(1)} %get-tuple-element.31.high_ref, bf16[512,784]{1,0:T(8,128)(2,1)S(1)} %get-tuple-element.32.low_ref, f32[784,128]{1,0:T(8,128)S(1)} %collective-permute-done.2.s0, f32[784,128]{1,0:T(8,128)S(1)} %collective-permute-done.s1, ...), custom_call_target="tpu_custom_call" | custom-call | flops 1 | bytes 1 | tf_op jit(solution)/shard_map/pallas_call | solution.py:388
  47.7 3.4 %collective-permute-done.5.last = f32[784,128]{1,0:T(8,128)S(1)} collective-permute-done((f32[784,128]{1,0:T(8,128)}, f32[784,128]{1,0:T(8,128)S(1)}, u32[]{:S(2)}, u32[]{:S(2)}) %collective-permute-start.5) | collective-permute-done | bytes 401440 | tf_op jit(solution)/shard_map/ppermute | solution.py:364
  51.1 1.5 %shard_map.48 = (f32[8,128,128]{2,1,0:T(8,128)S(1)}, f32[8,128,128]{2,1,0:T(8,128)S(1)}) custom-call(s32[4]{0:T(128)S(1)} %pad_add_fusion.refs_0_.side_ref, bf16[512,784]{1,0:T(8,128)(2,1)S(1)} %get-tuple-element.31.high_ref, bf16[512,784]{1,0:T(8,128)(2,1)S(1)} %get-tuple-element.32.low_ref, f32[784,128]{1,0:T(8,128)S(1)} %collective-permute-done.5.last, ...), custom_call_target="tpu_custom_call" | custom-call | flops 1 | bytes 1 | tf_op jit(solution)/shard_map/pallas_call | solution.py:396
  52.6 4.2 %collective-permute-start.7 = (f32[8,128,128]{2,1,0:T(8,128)S(1)}, f32[8,128,128]{2,1,0:T(8,128)S(1)}, u32[]{:S(2)}, u32[]{:S(2)}) collective-permute-start(f32[8,128,128]{2,1,0:T(8,128)S(1)} %get-tuple-element.40), channel_id=1, source_target_pairs={{0,1},{1,0},{2,3},{3,2},{4,5},{5,4},{6,7},{7,6},{8,9},{9,8},{10,11... | collective-permute-start | bytes 1572872 | tf_op jit(solution)/shard_map/ppermute | solution.py:384
  56.8 0.0 collective-permute-done.4
  56.8 0.1 add.54
  56.9 1.5 %collective-permute-done.7 = f32[8,128,128]{2,1,0:T(8,128)S(1)} collective-permute-done((f32[8,128,128]{2,1,0:T(8,128)S(1)}, f32[8,128,128]{2,1,0:T(8,128)S(1)}, u32[]{:S(2)}, u32[]{:S(2)}) %collective-permute-start.7) | collective-permute-done | bytes 524320 | tf_op jit(solution)/shard_map/ppermute | solution.py:384
  58.3 0.9 add.55
  59.2 3.5 %all-to-all-start.2 = ((f32[8,128,128]{2,1,0:T(8,128)}), f32[8,128,128]{2,1,0:T(8,128)S(1)}, u32[]{:S(2)}, u32[]{:S(2)}) async-start(f32[8,128,128]{2,1,0:T(8,128)} %add.55), calls=%async_computation.2 | async-start | bytes 1048576 | tf_op jit(solution)/shard_map/all_to_all | solution.py:419
  62.7 0.1 collective-permute-start.8
  62.8 8.5 %collective-permute-done.8 = f32[2,128,256]{2,1,0:T(8,128)S(1)} collective-permute-done((f32[2,128,256]{2,1,0:T(8,128)S(1)}, f32[2,128,256]{2,1,0:T(8,128)S(1)}, u32[]{:S(2)}, u32[]{:S(2)}) %collective-permute-start.8) | collective-permute-done | bytes 262176 | tf_op jit(solution)/shard_map/ppermute | solution.py:408
  71.4 2.0 %collective-permute-start.9 = (f32[128,256]{1,0:T(8,128)S(1)}, f32[128,256]{1,0:T(8,128)S(1)}, u32[]{:S(2)}, u32[]{:S(2)}) collective-permute-start(f32[128,256]{1,0:T(8,128)S(1)} %slice_bitcast_fusion.1), channel_id=1, source_target_pairs={{0,4},{4,0},{1,5},{5,1},{2,6},{6,2},{3,7},{7,3},{8,12},{12,8},{9,1... | collective-permute-start | bytes 393224 | tf_op jit(solution)/shard_map/ppermute | solution.py:409
  73.4 0.0 all-to-all-done.2
  73.4 0.1 copy.26
  73.6 3.1 %collective-permute-start.11 = (f32[128,128]{1,0:T(8,128)S(1)}, f32[128,128]{1,0:T(8,128)S(1)}, u32[]{:S(2)}, u32[]{:S(2)}) collective-permute-start(f32[128,128]{1,0:T(8,128)S(1)} %get-tuple-element.71), channel_id=1, source_target_pairs={{8,16},{9,24},{10,2},{11,3},{12,6},{13,7},{14,20},{15,28},{16,17},... | collective-permute-start | bytes 196616 | tf_op jit(solution)/shard_map/ppermute | solution.py:425
  76.7 1.3 %collective-permute-start.12 = (f32[128,128]{1,0:T(8,128)S(1)}, f32[128,128]{1,0:T(8,128)S(1)}, u32[]{:S(2)}, u32[]{:S(2)}) collective-permute-start(f32[128,128]{1,0:T(8,128)S(1)} %get-tuple-element.72), channel_id=1, source_target_pairs={{8,2},{9,3},{10,20},{11,28},{12,16},{13,24},{14,6},{15,7},{16,10},... | collective-permute-start | bytes 196616 | tf_op jit(solution)/shard_map/ppermute | solution.py:424
  78.0 0.0 collective-permute-done.9
  78.0 1.3 %collective-permute-start.10 = (f32[128,256]{1,0:T(8,128)S(1)}, f32[128,256]{1,0:T(8,128)S(1)}, u32[]{:S(2)}, u32[]{:S(2)}) collective-permute-start(f32[128,256]{1,0:T(8,128)S(1)} %fusion.2), channel_id=1, source_target_pairs={{2,0},{3,1},{6,4},{7,5},{10,8},{11,9},{14,12},{15,13},{16,18},{17,... | collective-permute-start | bytes 393224 | tf_op jit(solution)/shard_map/ppermute | solution.py:417
  79.3 0.0 collective-permute-done.11
  79.3 0.5 collective-permute-done.12
  79.9 5.9 %collective-permute-done.10 = f32[128,256]{1,0:T(8,128)S(1)} collective-permute-done((f32[128,256]{1,0:T(8,128)S(1)}, f32[128,256]{1,0:T(8,128)S(1)}, u32[]{:S(2)}, u32[]{:S(2)}) %collective-permute-start.10) | collective-permute-done | bytes 131104 | tf_op jit(solution)/shard_map/ppermute | solution.py:417
  85.8 0.7 maximum_select_fusion
  (28 shorter events, 0.2 us)
Async XLA Ops:
  2.1 5.3 %copy-start.2 = (f32[3072,128]{1,0:T(8,128)S(1)}, f32[3072,128]{1,0:T(8,128)}, u32[]{:S(2)}) copy-start(f32[3072,128]{1,0:T(8,128)} %param.4) | copy-start | bytes 4718596
  3.1 12.0 %all-to-all-start = ((f32[4,272,128]{2,1,0:T(8,128)}), f32[4,272,128]{2,1,0:T(8,128)S(1)}, u32[]{:S(2)}, u32[]{:S(2)}) async-start(f32[4,272,128]{2,1,0:T(8,128)} %pad_maximum_fusion.3), calls=%async_computation | async-start | bytes 1114112 | tf_op jit(solution)/shard_map/all_to_all | solution.py:335
  7.4 4.1 %copy-start.4 = (s32[6,512]{1,0:T(8,128)S(1)}, s32[6,512]{1,0:T(8,128)}, u32[]{:S(2)}) copy-start(s32[6,512]{1,0:T(8,128)} %param.5) | copy-start | bytes 36868
  7.4 4.1 %copy-start.5 = (f32[8]{0:T(128)S(1)}, f32[8]{0:T(128)}, u32[]{:S(2)}) copy-start(f32[8]{0:T(128)} %param.6) | copy-start | bytes 100
  8.4 4.5 %copy-start.3 = (f32[784,128]{1,0:T(8,128)}, f32[784,128]{1,0:T(8,128)S(1)}, u32[]{:S(2)}) copy-start(f32[784,128]{1,0:T(8,128)S(1)} %get-tuple-element.36) | copy-start | bytes 1204228
  8.4 19.7 %collective-permute-start.2 = (f32[784,128]{1,0:T(8,128)S(1)}, f32[784,128]{1,0:T(8,128)S(1)}, u32[]{:S(2)}, u32[]{:S(2)}) collective-permute-start(f32[784,128]{1,0:T(8,128)S(1)} %get-tuple-element.36), channel_id=1, source_target_pairs={{8,16},{9,17},{10,18},{11,19},{12,20},{13,21},{14,22},{15,23},{16,... | collective-permute-start | bytes 1204232 | tf_op jit(solution)/shard_map/ppermute | solution.py:324
  15.1 25.1 %all-to-all-start.1 = ((f32[4,512,128]{2,1,0:T(8,128)}), f32[4,512,128]{2,1,0:T(8,128)S(1)}, u32[]{:S(2)}, u32[]{:S(2)}) async-start(f32[4,512,128]{2,1,0:T(8,128)} %pad_maximum_fusion), calls=%async_computation.1 | async-start | bytes 2097152 | tf_op jit(solution)/shard_map/all_to_all | solution.py:336
  19.2 17.0 %copy-start.6 = (f32[2]{0:T(128)S(1)}, f32[2]{0:T(128)}, u32[]{:S(2)}) copy-start(f32[2]{0:T(128)} %constant.59.clone) | copy-start | bytes 28
  19.2 15.6 %collective-permute-start = (f32[784,128]{1,0:T(8,128)}, f32[784,128]{1,0:T(8,128)S(1)}, u32[]{:S(2)}, u32[]{:S(2)}) collective-permute-start(f32[784,128]{1,0:T(8,128)} %get-tuple-element.33), channel_id=1, source_target_pairs={{8,20},{9,21},{10,22},{11,23},{12,16},{13,17},{14,18},{15,19},{16,... | collective-permute-start | bytes 1204232 | tf_op jit(solution)/shard_map/ppermute | solution.py:338
  25.5 8.0 %collective-permute-start.1 = (f32[688,128]{1,0:T(8,128)}, f32[688,128]{1,0:T(8,128)S(1)}, u32[]{:S(2)}, u32[]{:S(2)}) collective-permute-start(f32[688,128]{1,0:T(8,128)} %pad_maximum_fusion.4), channel_id=1, source_target_pairs={{0,1},{1,2},{2,3},{4,5},{5,6},{6,7},{8,9},{9,10},{10,11},{12,13},{... | collective-permute-start | bytes 1056776 | tf_op jit(solution)/shard_map/ppermute | solution.py:359
  26.8 5.4 %collective-permute-start.3 = (f32[544,128]{1,0:T(8,128)}, f32[544,128]{1,0:T(8,128)S(1)}, u32[]{:S(2)}, u32[]{:S(2)}) collective-permute-start(f32[544,128]{1,0:T(8,128)} %bitcast.33), channel_id=1, source_target_pairs={{1,0},{2,1},{3,2},{5,4},{6,5},{7,6},{9,8},{10,9},{11,10},{13,12},{... | collective-permute-start | bytes 835592 | tf_op jit(solution)/shard_map/ppermute | solution.py:360
  32.2 13.8 %collective-permute-start.6 = (f32[784,128]{1,0:T(8,128)}, f32[784,128]{1,0:T(8,128)S(1)}, u32[]{:S(2)}, u32[]{:S(2)}) collective-permute-start(f32[784,128]{1,0:T(8,128)} %copy-done.3), channel_id=1, source_target_pairs={{0,16},{1,17},{2,18},{3,19},{4,20},{5,21},{6,22},{7,23},{24,8},{25... | collective-permute-start | bytes 1204232 | tf_op jit(solution)/shard_map/ppermute | solution.py:362
  33.5 0.7 copy-start
  34.8 16.3 %collective-permute-start.5 = (f32[784,128]{1,0:T(8,128)}, f32[784,128]{1,0:T(8,128)S(1)}, u32[]{:S(2)}, u32[]{:S(2)}) collective-permute-start(f32[784,128]{1,0:T(8,128)} %get-tuple-element.33), channel_id=1, source_target_pairs={{0,20},{1,21},{2,22},{3,23},{4,16},{5,17},{6,18},{7,19},{24,12},{2... | collective-permute-start | bytes 1204232 | tf_op jit(solution)/shard_map/ppermute | solution.py:364
  40.4 1.0 %copy-start.1 = (f32[688,128]{1,0:T(8,128)S(1)}, f32[688,128]{1,0:T(8,128)}, u32[]{:S(2)}) copy-start(f32[688,128]{1,0:T(8,128)} %copy-done) | copy-start | bytes 1056772
  45.2 11.6 %collective-permute-start.4 = (f32[2,2,128,256]{3,2,1,0:T(8,128)S(1)}, f32[2,2,128,256]{3,2,1,0:T(8,128)S(1)}, u32[]{:S(2)}, u32[]{:S(2)}) collective-permute-start(f32[2,2,128,256]{3,2,1,0:T(8,128)S(1)} %get-tuple-element.30), channel_id=1, source_target_pairs={{0,1},{1,0},{2,3},{3,2},{4,5},{5,4},{6,7},{7,6},{8,9},{9,8},{10,11... | collective-permute-start | bytes 1572872 | tf_op jit(solution)/shard_map/ppermute | solution.py:384
  52.6 5.7 %collective-permute-start.7 = (f32[8,128,128]{2,1,0:T(8,128)S(1)}, f32[8,128,128]{2,1,0:T(8,128)S(1)}, u32[]{:S(2)}, u32[]{:S(2)}) collective-permute-start(f32[8,128,128]{2,1,0:T(8,128)S(1)} %get-tuple-element.40), channel_id=1, source_target_pairs={{0,1},{1,0},{2,3},{3,2},{4,5},{5,4},{6,7},{7,6},{8,9},{9,8},{10,11... | collective-permute-start | bytes 1572872 | tf_op jit(solution)/shard_map/ppermute | solution.py:384
  59.2 14.2 %all-to-all-start.2 = ((f32[8,128,128]{2,1,0:T(8,128)}), f32[8,128,128]{2,1,0:T(8,128)S(1)}, u32[]{:S(2)}, u32[]{:S(2)}) async-start(f32[8,128,128]{2,1,0:T(8,128)} %add.55), calls=%async_computation.2 | async-start | bytes 1048576 | tf_op jit(solution)/shard_map/all_to_all | solution.py:419
  62.7 8.7 %collective-permute-start.8 = (f32[2,128,256]{2,1,0:T(8,128)S(1)}, f32[2,128,256]{2,1,0:T(8,128)S(1)}, u32[]{:S(2)}, u32[]{:S(2)}) collective-permute-start(f32[2,128,256]{2,1,0:T(8,128)S(1)} %slice_bitcast_fusion), channel_id=1, source_target_pairs={{0,8},{8,0},{1,9},{9,1},{2,10},{10,2},{3,11},{11,3},{4,12},{12,4},... | collective-permute-start | bytes 786440 | tf_op jit(solution)/shard_map/ppermute | solution.py:408
  71.4 6.6 %collective-permute-start.9 = (f32[128,256]{1,0:T(8,128)S(1)}, f32[128,256]{1,0:T(8,128)S(1)}, u32[]{:S(2)}, u32[]{:S(2)}) collective-permute-start(f32[128,256]{1,0:T(8,128)S(1)} %slice_bitcast_fusion.1), channel_id=1, source_target_pairs={{0,4},{4,0},{1,5},{5,1},{2,6},{6,2},{3,7},{7,3},{8,12},{12,8},{9,1... | collective-permute-start | bytes 393224 | tf_op jit(solution)/shard_map/ppermute | solution.py:409
  73.6 5.8 %collective-permute-start.11 = (f32[128,128]{1,0:T(8,128)S(1)}, f32[128,128]{1,0:T(8,128)S(1)}, u32[]{:S(2)}, u32[]{:S(2)}) collective-permute-start(f32[128,128]{1,0:T(8,128)S(1)} %get-tuple-element.71), channel_id=1, source_target_pairs={{8,16},{9,24},{10,2},{11,3},{12,6},{13,7},{14,20},{15,28},{16,17},... | collective-permute-start | bytes 196616 | tf_op jit(solution)/shard_map/ppermute | solution.py:425
  76.7 3.2 %collective-permute-start.12 = (f32[128,128]{1,0:T(8,128)S(1)}, f32[128,128]{1,0:T(8,128)S(1)}, u32[]{:S(2)}, u32[]{:S(2)}) collective-permute-start(f32[128,128]{1,0:T(8,128)S(1)} %get-tuple-element.72), channel_id=1, source_target_pairs={{8,2},{9,3},{10,20},{11,28},{12,16},{13,24},{14,6},{15,7},{16,10},... | collective-permute-start | bytes 196616 | tf_op jit(solution)/shard_map/ppermute | solution.py:424
  78.0 7.7 %collective-permute-start.10 = (f32[128,256]{1,0:T(8,128)S(1)}, f32[128,256]{1,0:T(8,128)S(1)}, u32[]{:S(2)}, u32[]{:S(2)}) collective-permute-start(f32[128,256]{1,0:T(8,128)S(1)} %fusion.2), channel_id=1, source_target_pairs={{2,0},{3,1},{6,4},{7,5},{10,8},{11,9},{14,12},{15,13},{16,18},{17,... | collective-permute-start | bytes 393224 | tf_op jit(solution)/shard_map/ppermute | solution.py:417

commit v6 on v5

--- a/solution.py
+++ b/solution.py
@@ -291,7 +291,7 @@
                         if pair == 0:
                             block = pair_ref[rows_of, j * GROUP : (j + 1) * GROUP]
                         else:
-                            block = (fourth if j else third_ref)[rows_of]
+                            block = (third_ref if j else fourth)[rows_of]
                         if h:
                             ref[(2 * (1 - pair) + (x ^ j)) * 2 + i] = block.T
                         else:
@@ -358,10 +358,10 @@
     below = edge(0, 0)
     above = lax.ppermute(above, TILE, [(m, m + 1) for m in range(3)])
     below = lax.ppermute(below, TILE, [(m + 1, m) for m in range(3)])
-    half, near[0], below = lax.optimization_barrier((halves[0], near[0], below))
-    far = [lax.ppermute(half, ALL, crossing(True, 0))]
-    half, near[1], above, below = lax.optimization_barrier((halves[1], near[1], above, below))
-    far.append(lax.ppermute(half, ALL, crossing(True, 1)))
+    half, near[0], below = lax.optimization_barrier((halves[1], near[0], below))
+    far = [lax.ppermute(half, ALL, crossing(True, 1))]
+    half, near[1], above, below = lax.optimization_barrier((halves[0], near[1], above, below))
+    far.append(lax.ppermute(half, ALL, crossing(True, 0)))
 
     side = jnp.stack([c, h, x, l]).astype(jnp.int32)
     seam_side = jnp.stack([(h == 0) & (x == 1), (h == 1) & (x == 0)]).astype(jnp.float32)

time: 87.1 us -> 87.1 us (level)
  waiting for transfers between devices: 30.5 us -> 31.9 us
  starting transfers between devices: 37.3 us -> 36 us
    all_to_all x1, waiting for transfers between devices: 3.89 us -> 8.71 us  [local_strips(): between = lax.all_to_all(jnp.stack(between), PLACE, 0, 0, tiled=True)]
    ppermute x2, waiting for transfers between devices: 3.44 us -> 0.01 us  [the longest x1 0.01 us: local_strips(): far = [lax.ppermute(half, ALL, crossing(True, 1))]]
    ppermute x2, starting transfers between devices: 5.03 us -> 3.67 us  [both_cores(): return mine + lax.ppermute(other, 'c', [(0, 1), (1, 0)])]
  transfers between devices with their start and end apart: 16 -> 16, of which waited for: 9 -> 8; matrix products, arithmetic and copies ran while one was open for 6% -> 6% of each run, Pallas kernels for 8% -> 8%
where the time goes in v6:
time: 87.1 us; the launch traced here: 86.5 us
  starting transfers between devices  36 us (41%)
  waiting for transfers between devices  31.9 us (37%)
  Pallas kernels  6.96 us (8%)
  other arithmetic  6.52 us (7%)
  local copies, waits for them, and re-layouts  4.77 us (5%)
    all_to_all x1, waiting for transfers between devices, local_strips(): between = lax.all_to_all(jnp.stack(between), PLACE, 0, 0, tiled=True)  8.71 us
    ppermute x1, waiting for transfers between devices, local_strips(): own = own[0] + lax.ppermute(own[1], 'l', [(0, 1), (1, 0)])  8.51 us
    ppermute x1, waiting for transfers between devices, local_strips(): own = own + lax.ppermute(own, ALL, to_holder)  5.86 us
    ppermute x1, starting transfers between devices, local_strips(): near.append(lax.ppermute(half, ALL, crossing(False, 1)))  4.49 us
    all_to_all x1, starting transfers between devices, local_strips(): ends = lax.all_to_all(jnp.stack(ends), PLACE, 0, 0, tiled=True)  4.22 us
    all_to_all x1, starting transfers between devices, local_strips(): between = lax.all_to_all(jnp.stack(between), PLACE, 0, 0, tiled=True)  4.1 us
    ppermute x1, waiting for transfers between devices, local_strips(): below = lax.ppermute(below, TILE, [(m + 1, m) for m in range(3)])  4.07 us
    pallas_call x1, Pallas kernels, local_strips(): pl.pallas_call(lambda *refs: own_kernel(rows, *refs), out_shape=(half_flo...  3.8 us
  transfers between devices with their start and end apart: 16, of which 8 were waited for; matrix products, arithmetic and copies ran while one was open for 6% of the time, Pallas kernels for 8%

profile of v6, /device:TPU:8, one launch (start us, length us, event | category | flops | bytes accessed | tf_op | source)
XLA Modules:
  0.0 86.5 jit_solution(5938420408185983759)
XLA Ops:
  0.0 0.9 %fusion.4 = (f32[6,1,128]{2,1,0:T(1,128)S(1)}, f32[6,1,128]{2,1,0:T(1,128)S(1)}, f32[6,1,128]{2,1,0:T(1,128)S(1)}, f32[6,1,128]{2,1,0:T(1,128)S(1)}, f32[6,1,128]{2,1,0:T(1,128)S(1)}, /*index=5*/f32[6,1,128]{2,1,0:T(1,128)S(1)}) fusion(f32[6,512,128]{2,1,0:T(8,128)} %bitcast.61), kind=kLoop, calls=%fused_computation.43 | loop fusion | bytes 36864 | tf_op jit(solution)/shard_map/slice | solution.py:331
  0.9 1.1 %slice_bitcast_fusion.9 = (f32[128,128]{1,0:T(8,128)S(1)}, f32[128,128]{1,0:T(8,128)S(1)}, f32[128,128]{1,0:T(8,128)S(1)}, f32[128,128]{1,0:T(8,128)S(1)}, f32[1...) fusion(f32[6,512,128]{2,1,0:T(8,128)} %bitcast.62), kind=kLoop, calls=%fused_computation.23 | loop fusion | bytes 1048576 | tf_op jit(solution)/shard_map/squeeze | solution.py:333
  2.0 0.1 concatenate.36
  2.1 0.1 concatenate.35
  2.1 0.1 concatenate.34
  2.2 0.1 concatenate.37
  2.2 0.9 pad_maximum_fusion.3
  3.1 4.2 %all-to-all-start = ((f32[4,272,128]{2,1,0:T(8,128)}), f32[4,272,128]{2,1,0:T(8,128)S(1)}, u32[]{:S(2)}, u32[]{:S(2)}) async-start(f32[4,272,128]{2,1,0:T(8,128)} %pad_maximum_fusion.3), calls=%async_computation | async-start | bytes 1114112 | tf_op jit(solution)/shard_map/all_to_all | solution.py:335
  7.3 0.1 pad.30.clone
  7.4 0.0 copy-done.2
  7.4 0.1 constant_dynamic-slice_fusion
  7.5 0.9 %fusion.1 = (f32[784,128]{1,0:T(8,128)S(1)}, f32[784,128]{1,0:T(8,128)}) fusion(f32[6,128]{1,0:T(8,128)S(1)} %get-tuple-element.82, f32[768,128]{1,0:T(8,128)S(1)} %bitcast.65, f32[784]{0:T(1024)S(1)} %pad.30.clone, f32[768,128]{1,0:T(8,128)S(1)} %bitcast.66), kind=kLoop, calls=%fused_computation.5 | loop fusion | flops 401408 | bytes 1595456 | tf_op jit(solution)/shard_map/concatenate | solution.py:321
  8.4 3.0 %collective-permute-start.2 = (f32[784,128]{1,0:T(8,128)S(1)}, f32[784,128]{1,0:T(8,128)S(1)}, u32[]{:S(2)}, u32[]{:S(2)}) collective-permute-start(f32[784,128]{1,0:T(8,128)S(1)} %get-tuple-element.33), channel_id=1, source_target_pairs={{8,16},{9,17},{10,18},{11,19},{12,20},{13,21},{14,22},{15,23},{16,... | collective-permute-start | bytes 1204232 | tf_op jit(solution)/shard_map/ppermute | solution.py:324
  11.5 0.1 pad.16.clone
  11.5 0.1 select_reduce_fusion
  11.6 0.1 pad_dynamic-slice_fusion
  11.7 0.1 pad.12.clone
  11.8 0.1 fusion.3
  11.9 1.0 %pad_maximum_fusion = f32[4,512,128]{2,1,0:T(8,128)} fusion(f32[1,512,128]{2,1,0:T(8,128)S(1)} %bitcast.71, f32[1,512,128]{2,1,0:T(8,128)S(1)} %bitcast.70, f32[1,512,128]{2,1,0:T(8,128)S(1)} %bitcast.69, f32[1,512,128]{2,1,0:T(8,128)S(1)} %bitcast.68), kind=kLoop, calls=%fused_computation | loop fusion | flops 786432 | bytes 2097152 | tf_op jit(solution)/shard_map/stack | solution.py:336
  12.9 2.1 %all-to-all-done.refs_2_ = f32[4,272,128]{2,1,0:T(8,128)S(1)} async-done(((f32[4,272,128]{2,1,0:T(8,128)}), f32[4,272,128]{2,1,0:T(8,128)S(1)}, u32[]{:S(2)}, u32[]{:S(2)}) %all-to-all-start) | async-done | bytes 557088 | tf_op jit(solution)/shard_map/all_to_all | solution.py:335
  15.1 4.1 %all-to-all-start.1 = ((f32[4,512,128]{2,1,0:T(8,128)}), f32[4,512,128]{2,1,0:T(8,128)S(1)}, u32[]{:S(2)}, u32[]{:S(2)}) async-start(f32[4,512,128]{2,1,0:T(8,128)} %pad_maximum_fusion), calls=%async_computation.1 | async-start | bytes 2097152 | tf_op jit(solution)/shard_map/all_to_all | solution.py:336
  19.2 4.5 %collective-permute-start = (f32[784,128]{1,0:T(8,128)}, f32[784,128]{1,0:T(8,128)S(1)}, u32[]{:S(2)}, u32[]{:S(2)}) collective-permute-start(f32[784,128]{1,0:T(8,128)} %get-tuple-element.36), channel_id=1, source_target_pairs={{8,20},{9,21},{10,22},{11,23},{12,16},{13,17},{14,18},{15,19},{16,... | collective-permute-start | bytes 1204232 | tf_op jit(solution)/shard_map/ppermute | solution.py:338
  23.7 0.8 maximum_maximum_fusion.1
  24.6 0.9 %pad_maximum_fusion.4 = f32[688,128]{1,0:T(8,128)} fusion(f32[544,128]{1,0:T(8,128)S(1)} %bitcast.67, f32[688]{0:T(1024)S(1)} %pad.12.clone), kind=kLoop, calls=%fused_computation.6 | loop fusion | flops 88064 | bytes 633536 | tf_op jit(solution)/shard_map/concatenate | solution.py:357
  25.5 1.3 %collective-permute-start.1 = (f32[688,128]{1,0:T(8,128)}, f32[688,128]{1,0:T(8,128)S(1)}, u32[]{:S(2)}, u32[]{:S(2)}) collective-permute-start(f32[688,128]{1,0:T(8,128)} %pad_maximum_fusion.4), channel_id=1, source_target_pairs={{0,1},{1,2},{2,3},{4,5},{5,6},{6,7},{8,9},{9,10},{10,11},{12,13},{... | collective-permute-start | bytes 1056776 | tf_op jit(solution)/shard_map/ppermute | solution.py:359
  26.8 1.3 %collective-permute-start.3 = (f32[544,128]{1,0:T(8,128)}, f32[544,128]{1,0:T(8,128)S(1)}, u32[]{:S(2)}, u32[]{:S(2)}) collective-permute-start(f32[544,128]{1,0:T(8,128)} %bitcast.33), channel_id=1, source_target_pairs={{1,0},{2,1},{3,2},{5,4},{6,5},{7,6},{9,8},{10,9},{11,10},{13,12},{... | collective-permute-start | bytes 835592 | tf_op jit(solution)/shard_map/ppermute | solution.py:360
  28.1 0.0 collective-permute-done.2.s0
  28.1 4.1 %collective-permute-done.3.refs_5_ = f32[544,128]{1,0:T(8,128)S(1)} collective-permute-done((f32[544,128]{1,0:T(8,128)}, f32[544,128]{1,0:T(8,128)S(1)}, u32[]{:S(2)}, u32[]{:S(2)}) %collective-permute-start.3) | collective-permute-done | bytes 278560 | tf_op jit(solution)/shard_map/ppermute | solution.py:360
  32.2 1.3 %collective-permute-start.6 = (f32[784,128]{1,0:T(8,128)}, f32[784,128]{1,0:T(8,128)S(1)}, u32[]{:S(2)}, u32[]{:S(2)}) collective-permute-start(f32[784,128]{1,0:T(8,128)} %get-tuple-element.36), channel_id=1, source_target_pairs={{0,20},{1,21},{2,22},{3,23},{4,16},{5,17},{6,18},{7,19},{24,12},{2... | collective-permute-start | bytes 1204232 | tf_op jit(solution)/shard_map/ppermute | solution.py:362
  33.5 0.0 collective-permute-done.1.refs_4_
  33.5 0.7 copy-done
  34.2 0.6 collective-permute-done.s1
  34.8 1.3 %collective-permute-start.5 = (f32[784,128]{1,0:T(8,128)}, f32[784,128]{1,0:T(8,128)S(1)}, u32[]{:S(2)}, u32[]{:S(2)}) collective-permute-start(f32[784,128]{1,0:T(8,128)} %copy-done.3), channel_id=1, source_target_pairs={{0,16},{1,17},{2,18},{3,19},{4,20},{5,21},{6,22},{7,23},{24,8},{25... | collective-permute-start | bytes 1204232 | tf_op jit(solution)/shard_map/ppermute | solution.py:364
  36.1 0.1 pad_add_fusion.refs_0_.side_ref
  36.1 0.1 pad_dynamic-slice_fusion.1
  36.2 0.1 add_select_fusion.refs_1_
  36.3 8.7 %all-to-all-done.1.refs_3_ = f32[4,512,128]{2,1,0:T(8,128)S(1)} async-done(((f32[4,512,128]{2,1,0:T(8,128)}), f32[4,512,128]{2,1,0:T(8,128)S(1)}, u32[]{:S(2)}, u32[]{:S(2)}) %all-to-all-start.1) | async-done | bytes 1048608 | tf_op jit(solution)/shard_map/all_to_all | solution.py:336
  45.0 0.2 broadcast_in_dim.41.refs_6_
  45.2 1.0 %copy-done.1 = f32[688,128]{1,0:T(8,128)S(1)} copy-done((f32[688,128]{1,0:T(8,128)S(1)}, f32[688,128]{1,0:T(8,128)}, u32[]{:S(2)}) %copy-start.1) | copy-done | bytes 352280
  46.2 3.8 %shard_map.46 = (bf16[512,784]{1,0:T(8,128)(2,1)S(1)}, bf16[512,784]{1,0:T(8,128)(2,1)S(1)}, f32[2,2,128,256]{3,2,1,0:T(8,128)S(1)}, f32[2,2,128,256]{3,2,1,0:T(8,128)S(1)}) custom-call(s32[4]{0:T(128)S(1)} %pad_add_fusion.refs_0_.side_ref, f32[2]{0:T(128)S(1)} %add_select_fusion.refs_1_, f32[4,272,128]{2,1,0:T(8,128)S(1)} %all-to-all-done.refs_2_, ...), custom_call_target="tpu_custom_call" | custom-call | flops 1 | bytes 1 | tf_op jit(solution)/shard_map/pallas_call | solution.py:372
  50.0 0.1 collective-permute-start.4
  50.0 0.0 collective-permute-done.6.s2
  50.1 1.7 %shard_map.47 = (f32[512,256]{1,0:T(8,128)S(1)}, f32[512,128]{1,0:T(8,128)S(1)}) custom-call(bf16[512,784]{1,0:T(8,128)(2,1)S(1)} %get-tuple-element.31.high_ref, bf16[512,784]{1,0:T(8,128)(2,1)S(1)} %get-tuple-element.32.low_ref, f32[784,128]{1,0:T(8,128)S(1)} %collective-permute-done.2.s0, f32[784,128]{1,0:T(8,128)S(1)} %collective-permute-done.s1, ...), custom_call_target="tpu_custom_call" | custom-call | flops 1 | bytes 1 | tf_op jit(solution)/shard_map/pallas_call | solution.py:388
  51.8 0.0 collective-permute-done.5.last
  51.8 1.5 %shard_map.48 = (f32[8,128,128]{2,1,0:T(8,128)S(1)}, f32[8,128,128]{2,1,0:T(8,128)S(1)}) custom-call(s32[4]{0:T(128)S(1)} %pad_add_fusion.refs_0_.side_ref, bf16[512,784]{1,0:T(8,128)(2,1)S(1)} %get-tuple-element.31.high_ref, bf16[512,784]{1,0:T(8,128)(2,1)S(1)} %get-tuple-element.32.low_ref, f32[784,128]{1,0:T(8,128)S(1)} %collective-permute-done.5.last, ...), custom_call_target="tpu_custom_call" | custom-call | flops 1 | bytes 1 | tf_op jit(solution)/shard_map/pallas_call | solution.py:396
  53.2 3.6 %collective-permute-start.7 = (f32[8,128,128]{2,1,0:T(8,128)S(1)}, f32[8,128,128]{2,1,0:T(8,128)S(1)}, u32[]{:S(2)}, u32[]{:S(2)}) collective-permute-start(f32[8,128,128]{2,1,0:T(8,128)S(1)} %get-tuple-element.40), channel_id=1, source_target_pairs={{0,1},{1,0},{2,3},{3,2},{4,5},{5,4},{6,7},{7,6},{8,9},{9,8},{10,11... | collective-permute-start | bytes 1572872 | tf_op jit(solution)/shard_map/ppermute | solution.py:384
  56.8 0.0 collective-permute-done.4
  56.8 0.1 add.54
  56.9 1.5 %collective-permute-done.7 = f32[8,128,128]{2,1,0:T(8,128)S(1)} collective-permute-done((f32[8,128,128]{2,1,0:T(8,128)S(1)}, f32[8,128,128]{2,1,0:T(8,128)S(1)}, u32[]{:S(2)}, u32[]{:S(2)}) %collective-permute-start.7) | collective-permute-done | bytes 524320 | tf_op jit(solution)/shard_map/ppermute | solution.py:384
  58.4 0.9 add.55
  59.2 3.5 %all-to-all-start.2 = ((f32[8,128,128]{2,1,0:T(8,128)}), f32[8,128,128]{2,1,0:T(8,128)S(1)}, u32[]{:S(2)}, u32[]{:S(2)}) async-start(f32[8,128,128]{2,1,0:T(8,128)} %add.55), calls=%async_computation.2 | async-start | bytes 1048576 | tf_op jit(solution)/shard_map/all_to_all | solution.py:419
  62.8 0.1 collective-permute-start.8
  62.9 8.5 %collective-permute-done.8 = f32[2,128,256]{2,1,0:T(8,128)S(1)} collective-permute-done((f32[2,128,256]{2,1,0:T(8,128)S(1)}, f32[2,128,256]{2,1,0:T(8,128)S(1)}, u32[]{:S(2)}, u32[]{:S(2)}) %collective-permute-start.8) | collective-permute-done | bytes 262176 | tf_op jit(solution)/shard_map/ppermute | solution.py:408
  71.5 2.0 %collective-permute-start.9 = (f32[128,256]{1,0:T(8,128)S(1)}, f32[128,256]{1,0:T(8,128)S(1)}, u32[]{:S(2)}, u32[]{:S(2)}) collective-permute-start(f32[128,256]{1,0:T(8,128)S(1)} %slice_bitcast_fusion.1), channel_id=1, source_target_pairs={{0,4},{4,0},{1,5},{5,1},{2,6},{6,2},{3,7},{7,3},{8,12},{12,8},{9,1... | collective-permute-start | bytes 393224 | tf_op jit(solution)/shard_map/ppermute | solution.py:409
  73.5 0.0 all-to-all-done.2
  73.5 0.1 copy.26
  73.6 3.1 %collective-permute-start.11 = (f32[128,128]{1,0:T(8,128)S(1)}, f32[128,128]{1,0:T(8,128)S(1)}, u32[]{:S(2)}, u32[]{:S(2)}) collective-permute-start(f32[128,128]{1,0:T(8,128)S(1)} %get-tuple-element.71), channel_id=1, source_target_pairs={{8,16},{9,24},{10,2},{11,3},{12,6},{13,7},{14,20},{15,28},{16,17},... | collective-permute-start | bytes 196616 | tf_op jit(solution)/shard_map/ppermute | solution.py:425
  76.7 1.3 %collective-permute-start.12 = (f32[128,128]{1,0:T(8,128)S(1)}, f32[128,128]{1,0:T(8,128)S(1)}, u32[]{:S(2)}, u32[]{:S(2)}) collective-permute-start(f32[128,128]{1,0:T(8,128)S(1)} %get-tuple-element.72), channel_id=1, source_target_pairs={{8,2},{9,3},{10,20},{11,28},{12,16},{13,24},{14,6},{15,7},{16,10},... | collective-permute-start | bytes 196616 | tf_op jit(solution)/shard_map/ppermute | solution.py:424
  78.0 0.0 collective-permute-done.9
  78.1 1.3 %collective-permute-start.10 = (f32[128,256]{1,0:T(8,128)S(1)}, f32[128,256]{1,0:T(8,128)S(1)}, u32[]{:S(2)}, u32[]{:S(2)}) collective-permute-start(f32[128,256]{1,0:T(8,128)S(1)} %fusion.2), channel_id=1, source_target_pairs={{2,0},{3,1},{6,4},{7,5},{10,8},{11,9},{14,12},{15,13},{16,18},{17,... | collective-permute-start | bytes 393224 | tf_op jit(solution)/shard_map/ppermute | solution.py:417
  79.4 0.0 collective-permute-done.11
  79.4 0.5 collective-permute-done.12
  79.9 5.9 %collective-permute-done.10 = f32[128,256]{1,0:T(8,128)S(1)} collective-permute-done((f32[128,256]{1,0:T(8,128)S(1)}, f32[128,256]{1,0:T(8,128)S(1)}, u32[]{:S(2)}, u32[]{:S(2)}) %collective-permute-start.10) | collective-permute-done | bytes 131104 | tf_op jit(solution)/shard_map/ppermute | solution.py:417
  85.8 0.7 maximum_select_fusion
  (28 shorter events, 0.2 us)
Async XLA Ops:
  2.1 5.3 %copy-start.2 = (f32[3072,128]{1,0:T(8,128)S(1)}, f32[3072,128]{1,0:T(8,128)}, u32[]{:S(2)}) copy-start(f32[3072,128]{1,0:T(8,128)} %param.4) | copy-start | bytes 4718596
  3.1 12.0 %all-to-all-start = ((f32[4,272,128]{2,1,0:T(8,128)}), f32[4,272,128]{2,1,0:T(8,128)S(1)}, u32[]{:S(2)}, u32[]{:S(2)}) async-start(f32[4,272,128]{2,1,0:T(8,128)} %pad_maximum_fusion.3), calls=%async_computation | async-start | bytes 1114112 | tf_op jit(solution)/shard_map/all_to_all | solution.py:335
  7.4 4.1 %copy-start.4 = (s32[6,512]{1,0:T(8,128)S(1)}, s32[6,512]{1,0:T(8,128)}, u32[]{:S(2)}) copy-start(s32[6,512]{1,0:T(8,128)} %param.5) | copy-start | bytes 36868
  7.4 4.1 %copy-start.5 = (f32[8]{0:T(128)S(1)}, f32[8]{0:T(128)}, u32[]{:S(2)}) copy-start(f32[8]{0:T(128)} %param.6) | copy-start | bytes 100
  8.4 4.5 %copy-start.3 = (f32[784,128]{1,0:T(8,128)}, f32[784,128]{1,0:T(8,128)S(1)}, u32[]{:S(2)}) copy-start(f32[784,128]{1,0:T(8,128)S(1)} %get-tuple-element.33) | copy-start | bytes 1204228
  8.4 19.7 %collective-permute-start.2 = (f32[784,128]{1,0:T(8,128)S(1)}, f32[784,128]{1,0:T(8,128)S(1)}, u32[]{:S(2)}, u32[]{:S(2)}) collective-permute-start(f32[784,128]{1,0:T(8,128)S(1)} %get-tuple-element.33), channel_id=1, source_target_pairs={{8,16},{9,17},{10,18},{11,19},{12,20},{13,21},{14,22},{15,23},{16,... | collective-permute-start | bytes 1204232 | tf_op jit(solution)/shard_map/ppermute | solution.py:324
  15.1 29.9 %all-to-all-start.1 = ((f32[4,512,128]{2,1,0:T(8,128)}), f32[4,512,128]{2,1,0:T(8,128)S(1)}, u32[]{:S(2)}, u32[]{:S(2)}) async-start(f32[4,512,128]{2,1,0:T(8,128)} %pad_maximum_fusion), calls=%async_computation.1 | async-start | bytes 2097152 | tf_op jit(solution)/shard_map/all_to_all | solution.py:336
  19.2 17.0 %copy-start.6 = (f32[2]{0:T(128)S(1)}, f32[2]{0:T(128)}, u32[]{:S(2)}) copy-start(f32[2]{0:T(128)} %constant.59.clone) | copy-start | bytes 28
  19.2 15.6 %collective-permute-start = (f32[784,128]{1,0:T(8,128)}, f32[784,128]{1,0:T(8,128)S(1)}, u32[]{:S(2)}, u32[]{:S(2)}) collective-permute-start(f32[784,128]{1,0:T(8,128)} %get-tuple-element.36), channel_id=1, source_target_pairs={{8,20},{9,21},{10,22},{11,23},{12,16},{13,17},{14,18},{15,19},{16,... | collective-permute-start | bytes 1204232 | tf_op jit(solution)/shard_map/ppermute | solution.py:338
  25.5 8.0 %collective-permute-start.1 = (f32[688,128]{1,0:T(8,128)}, f32[688,128]{1,0:T(8,128)S(1)}, u32[]{:S(2)}, u32[]{:S(2)}) collective-permute-start(f32[688,128]{1,0:T(8,128)} %pad_maximum_fusion.4), channel_id=1, source_target_pairs={{0,1},{1,2},{2,3},{4,5},{5,6},{6,7},{8,9},{9,10},{10,11},{12,13},{... | collective-permute-start | bytes 1056776 | tf_op jit(solution)/shard_map/ppermute | solution.py:359
  26.8 5.4 %collective-permute-start.3 = (f32[544,128]{1,0:T(8,128)}, f32[544,128]{1,0:T(8,128)S(1)}, u32[]{:S(2)}, u32[]{:S(2)}) collective-permute-start(f32[544,128]{1,0:T(8,128)} %bitcast.33), channel_id=1, source_target_pairs={{1,0},{2,1},{3,2},{5,4},{6,5},{7,6},{9,8},{10,9},{11,10},{13,12},{... | collective-permute-start | bytes 835592 | tf_op jit(solution)/shard_map/ppermute | solution.py:360
  32.2 17.9 %collective-permute-start.6 = (f32[784,128]{1,0:T(8,128)}, f32[784,128]{1,0:T(8,128)S(1)}, u32[]{:S(2)}, u32[]{:S(2)}) collective-permute-start(f32[784,128]{1,0:T(8,128)} %get-tuple-element.36), channel_id=1, source_target_pairs={{0,20},{1,21},{2,22},{3,23},{4,16},{5,17},{6,18},{7,19},{24,12},{2... | collective-permute-start | bytes 1204232 | tf_op jit(solution)/shard_map/ppermute | solution.py:362
  33.5 0.7 copy-start
  34.8 17.0 %collective-permute-start.5 = (f32[784,128]{1,0:T(8,128)}, f32[784,128]{1,0:T(8,128)S(1)}, u32[]{:S(2)}, u32[]{:S(2)}) collective-permute-start(f32[784,128]{1,0:T(8,128)} %copy-done.3), channel_id=1, source_target_pairs={{0,16},{1,17},{2,18},{3,19},{4,20},{5,21},{6,22},{7,23},{24,8},{25... | collective-permute-start | bytes 1204232 | tf_op jit(solution)/shard_map/ppermute | solution.py:364
  45.2 1.0 %copy-start.1 = (f32[688,128]{1,0:T(8,128)S(1)}, f32[688,128]{1,0:T(8,128)}, u32[]{:S(2)}) copy-start(f32[688,128]{1,0:T(8,128)} %copy-done) | copy-start | bytes 1056772
  50.0 6.9 %collective-permute-start.4 = (f32[2,2,128,256]{3,2,1,0:T(8,128)S(1)}, f32[2,2,128,256]{3,2,1,0:T(8,128)S(1)}, u32[]{:S(2)}, u32[]{:S(2)}) collective-permute-start(f32[2,2,128,256]{3,2,1,0:T(8,128)S(1)} %get-tuple-element.30), channel_id=1, source_target_pairs={{0,1},{1,0},{2,3},{3,2},{4,5},{5,4},{6,7},{7,6},{8,9},{9,8},{10,11... | collective-permute-start | bytes 1572872 | tf_op jit(solution)/shard_map/ppermute | solution.py:384
  53.2 5.1 %collective-permute-start.7 = (f32[8,128,128]{2,1,0:T(8,128)S(1)}, f32[8,128,128]{2,1,0:T(8,128)S(1)}, u32[]{:S(2)}, u32[]{:S(2)}) collective-permute-start(f32[8,128,128]{2,1,0:T(8,128)S(1)} %get-tuple-element.40), channel_id=1, source_target_pairs={{0,1},{1,0},{2,3},{3,2},{4,5},{5,4},{6,7},{7,6},{8,9},{9,8},{10,11... | collective-permute-start | bytes 1572872 | tf_op jit(solution)/shard_map/ppermute | solution.py:384
  59.2 14.2 %all-to-all-start.2 = ((f32[8,128,128]{2,1,0:T(8,128)}), f32[8,128,128]{2,1,0:T(8,128)S(1)}, u32[]{:S(2)}, u32[]{:S(2)}) async-start(f32[8,128,128]{2,1,0:T(8,128)} %add.55), calls=%async_computation.2 | async-start | bytes 1048576 | tf_op jit(solution)/shard_map/all_to_all | solution.py:419
  62.8 8.6 %collective-permute-start.8 = (f32[2,128,256]{2,1,0:T(8,128)S(1)}, f32[2,128,256]{2,1,0:T(8,128)S(1)}, u32[]{:S(2)}, u32[]{:S(2)}) collective-permute-start(f32[2,128,256]{2,1,0:T(8,128)S(1)} %slice_bitcast_fusion), channel_id=1, source_target_pairs={{0,8},{8,0},{1,9},{9,1},{2,10},{10,2},{3,11},{11,3},{4,12},{12,4},... | collective-permute-start | bytes 786440 | tf_op jit(solution)/shard_map/ppermute | solution.py:408
  71.5 6.6 %collective-permute-start.9 = (f32[128,256]{1,0:T(8,128)S(1)}, f32[128,256]{1,0:T(8,128)S(1)}, u32[]{:S(2)}, u32[]{:S(2)}) collective-permute-start(f32[128,256]{1,0:T(8,128)S(1)} %slice_bitcast_fusion.1), channel_id=1, source_target_pairs={{0,4},{4,0},{1,5},{5,1},{2,6},{6,2},{3,7},{7,3},{8,12},{12,8},{9,1... | collective-permute-start | bytes 393224 | tf_op jit(solution)/shard_map/ppermute | solution.py:409
  73.6 5.8 %collective-permute-start.11 = (f32[128,128]{1,0:T(8,128)S(1)}, f32[128,128]{1,0:T(8,128)S(1)}, u32[]{:S(2)}, u32[]{:S(2)}) collective-permute-start(f32[128,128]{1,0:T(8,128)S(1)} %get-tuple-element.71), channel_id=1, source_target_pairs={{8,16},{9,24},{10,2},{11,3},{12,6},{13,7},{14,20},{15,28},{16,17},... | collective-permute-start | bytes 196616 | tf_op jit(solution)/shard_map/ppermute | solution.py:425
  76.7 3.2 %collective-permute-start.12 = (f32[128,128]{1,0:T(8,128)S(1)}, f32[128,128]{1,0:T(8,128)S(1)}, u32[]{:S(2)}, u32[]{:S(2)}) collective-permute-start(f32[128,128]{1,0:T(8,128)S(1)} %get-tuple-element.72), channel_id=1, source_target_pairs={{8,2},{9,3},{10,20},{11,28},{12,16},{13,24},{14,6},{15,7},{16,10},... | collective-permute-start | bytes 196616 | tf_op jit(solution)/shard_map/ppermute | solution.py:424
  78.1 7.7 %collective-permute-start.10 = (f32[128,256]{1,0:T(8,128)S(1)}, f32[128,256]{1,0:T(8,128)S(1)}, u32[]{:S(2)}, u32[]{:S(2)}) collective-permute-start(f32[128,256]{1,0:T(8,128)S(1)} %fusion.2), channel_id=1, source_target_pairs={{2,0},{3,1},{6,4},{7,5},{10,8},{11,9},{14,12},{15,13},{16,18},{17,... | collective-permute-start | bytes 393224 | tf_op jit(solution)/shard_map/ppermute | solution.py:417

commit v7 on v6

--- a/solution.py
+++ b/solution.py
@@ -323,17 +323,17 @@
     halves = [strip_at(2 * (1 - h) + (x ^ flip))[0] for flip in range(2)]
     near = [lax.ppermute(halves[0], ALL, crossing(False, 0))]
 
-    none = jnp.zeros((rows, GROUP), jnp.float32)
-    pad = jnp.zeros((8 - rows, GROUP), jnp.float32)
-    ends, between = [], []
-    for t in (2, 3, 0, 1):
-        left = field[:, t * STRIP - 1] if t > 0 else none
-        right = field[:, (t + 1) * STRIP] if t < 3 else none
-        main = field[:, t * STRIP : (t + 1) * STRIP]
-        ends.append(jnp.concatenate([main[0], main[rows - 1], left, pad, right, pad], 0))
-        between.append(main[1 : rows - 1].reshape((rows - 2) * STRIP, GROUP))
-    ends = lax.all_to_all(jnp.stack(ends), PLACE, 0, 0, tiled=True)
-    between = lax.all_to_all(jnp.stack(between), PLACE, 0, 0, tiled=True)
+    parts = field.reshape(rows, 4, STRIP, GROUP)
+    left = jnp.pad(parts[:, :3, STRIP - 1], ((0, 8 - rows), (1, 0), (0, 0)))
+    right = jnp.pad(parts[:, 1:, 0], ((0, 8 - rows), (0, 1), (0, 0)))
+    ends = jnp.concatenate(
+        [parts[0], parts[rows - 1], jnp.transpose(left, (1, 0, 2)), jnp.transpose(right, (1, 0, 2))], 1
+    )
+    ends = jnp.concatenate([ends[2:], ends[:2]], 0)
+    between = jnp.transpose(parts[1 : rows - 1], (1, 0, 2, 3)).reshape(4, -1, GROUP)
+    between = jnp.concatenate([between[2:], between[:2]], 0)
+    ends = lax.all_to_all(ends, PLACE, 0, 0, tiled=True)
+    between = lax.all_to_all(between, PLACE, 0, 0, tiled=True)
     half, ends = lax.optimization_barrier((halves[1], ends))
     near.append(lax.ppermute(half, ALL, crossing(False, 1)))
 
@@ -404,7 +404,6 @@
     )(side, high, low, far[1], *early)
 
     cross = both_cores(cross_mine, cross_other)
-    own, cross = lax.optimization_barrier((own, cross))
     own = own[0] + lax.ppermute(own[1], "l", [(0, 1), (1, 0)])
     own = own[0] + lax.ppermute(own[1], "x", [(0, 1), (1, 0)])
     to_holder = [

time: 87.1 us -> 87 us (level)
    concatenate x0 -> x3, other arithmetic: none -> 1.94 us  [the longest x1 1.04 us: local_strips(): between = jnp.concatenate([between[2:], between[:2]], 0)]
    another operation x2 -> x0, other arithmetic: 1.9 us -> none  [the longest x1 1.04 us: local_strips(): between = lax.all_to_all(jnp.stack(between), PLACE, 0, 0, tiled=True)]
    slice x2 -> x7, local copies, waits for them, and re-layouts: 0.94 us -> 2.26 us  [the longest x1 1.06 us: local_strips(): parts[0]]
    squeeze x4 -> x1, local copies, waits for them, and re-layouts: 1.11 us -> 0.01 us  [local_strips(): right = jnp.pad(parts[:, 1:, 0], ((0, 8 - rows), (0, 1), (0, 0)))]
    unnamed x14 -> x17, local copies, waits for them, and re-layouts: 1.73 us -> 1.74 us
where the time goes in v7:
time: 87 us; the launch traced here: 86.4 us
  starting transfers between devices  36 us (41%)
  waiting for transfers between devices  31.7 us (36%)
  Pallas kernels  6.96 us (8%)
  other arithmetic  6.56 us (8%)
  local copies, waits for them, and re-layouts  4.79 us (6%)
    all_to_all x1, waiting for transfers between devices, local_strips(): between = lax.all_to_all(between, PLACE, 0, 0, tiled=True)  8.71 us
    ppermute x1, waiting for transfers between devices, local_strips(): own = own[0] + lax.ppermute(own[1], 'l', [(0, 1), (1, 0)])  8.51 us
    ppermute x1, waiting for transfers between devices, local_strips(): own = own + lax.ppermute(own, ALL, to_holder)  5.86 us
    ppermute x1, starting transfers between devices, local_strips(): near.append(lax.ppermute(half, ALL, crossing(False, 1)))  4.49 us
    all_to_all x1, starting transfers between devices, local_strips(): ends = lax.all_to_all(ends, PLACE, 0, 0, tiled=True)  4.22 us
    all_to_all x1, starting transfers between devices, local_strips(): between = lax.all_to_all(between, PLACE, 0, 0, tiled=True)  4.1 us
    ppermute x1, waiting for transfers between devices, local_strips(): below = lax.ppermute(below, TILE, [(m + 1, m) for m in range(3)])  4.07 us
    pallas_call x1, Pallas kernels, local_strips(): pl.pallas_call(lambda *refs: own_kernel(rows, *refs), out_shape=(half_flo...  3.8 us
  transfers between devices with their start and end apart: 16, of which 8 were waited for; matrix products, arithmetic and copies ran while one was open for 6% of the time, Pallas kernels for 8%

profile of v7, /device:TPU:8, one launch (start us, length us, event | category | flops | bytes accessed | tf_op | source)
XLA Modules:
  0.0 86.4 jit_solution(1799182847648592815)
XLA Ops:
  0.0 1.1 %fusion.4 = (f32[512,128]{1,0:T(8,128)S(1)}, f32[512,128]{1,0:T(8,128)S(1)}) fusion(f32[3072,128]{1,0:T(8,128)} %param.4), kind=kLoop, calls=%fused_computation.36 | loop fusion | bytes 1048576 | tf_op jit(solution)/shard_map/slice | solution.py:330
  1.1 0.9 %fusion.5 = (f32[6,3,1,128]{3,2,1,0:T(1,128)S(1)}, f32[6,3,1,128]{3,2,1,0:T(1,128)S(1)}) fusion(f32[6,4,128,128]{3,2,1,0:T(8,128)} %bitcast.49), kind=kLoop, calls=%fused_computation.37 | loop fusion | bytes 36864 | tf_op jit(solution)/shard_map/slice | solution.py:327
  2.1 0.0 copy-start.2
  2.2 0.9 pad_maximum_fusion.4
  3.0 4.2 %all-to-all-start = ((f32[4,272,128]{2,1,0:T(8,128)}), f32[4,272,128]{2,1,0:T(8,128)S(1)}, u32[]{:S(2)}, u32[]{:S(2)}) async-start(f32[4,272,128]{2,1,0:T(8,128)} %pad_maximum_fusion.4), calls=%async_computation | async-start | bytes 1114112 | tf_op jit(solution)/shard_map/all_to_all | solution.py:335
  7.3 0.1 pad.40.clone
  7.3 0.1 constant_dynamic-slice_fusion
  7.4 0.0 copy-start.5
  7.4 0.0 copy-start.6
  7.4 0.9 %fusion.1 = (f32[784,128]{1,0:T(8,128)S(1)}, f32[784,128]{1,0:T(8,128)}) fusion(f32[6,128]{1,0:T(8,128)S(1)} %bitcast.59, f32[768,128]{1,0:T(8,128)S(1)} %bitcast.54, f32[784]{0:T(1024)S(1)} %pad.40.clone, f32[768,128]{1,0:T(8,128)S(1)} %bitcast.55), kind=kLoop, calls=%fused_computation.7 | loop fusion | flops 401408 | bytes 1595456 | tf_op jit(solution)/shard_map/concatenate | solution.py:321
  8.4 3.0 %collective-permute-start.2 = (f32[784,128]{1,0:T(8,128)S(1)}, f32[784,128]{1,0:T(8,128)S(1)}, u32[]{:S(2)}, u32[]{:S(2)}) collective-permute-start(f32[784,128]{1,0:T(8,128)S(1)} %get-tuple-element.31), channel_id=1, source_target_pairs={{8,16},{9,17},{10,18},{11,19},{12,20},{13,21},{14,22},{15,23},{16,... | collective-permute-start | bytes 1204232 | tf_op jit(solution)/shard_map/ppermute | solution.py:324
  11.4 0.1 slice.83
  11.5 0.1 pad.26.clone
  11.6 0.1 select_reduce_fusion
  11.7 0.1 pad_dynamic-slice_fusion
  11.8 0.1 pad.22.clone
  11.9 0.1 copy.24
  12.0 0.1 fusion.6
  12.0 1.0 %pad_maximum_fusion = f32[4,512,128]{2,1,0:T(8,128)} fusion(f32[2,512,128]{2,1,0:T(8,128)S(1)} %bitcast.53, f32[2,512,128]{2,1,0:T(8,128)S(1)} %bitcast.52), kind=kLoop, calls=%fused_computation | loop fusion | flops 262144 | bytes 2097152 | tf_op jit(solution)/shard_map/concatenate | solution.py:334
  13.1 1.9 %all-to-all-done.refs_2_ = f32[4,272,128]{2,1,0:T(8,128)S(1)} async-done(((f32[4,272,128]{2,1,0:T(8,128)}), f32[4,272,128]{2,1,0:T(8,128)S(1)}, u32[]{:S(2)}, u32[]{:S(2)}) %all-to-all-start) | async-done | bytes 557088 | tf_op jit(solution)/shard_map/all_to_all | solution.py:335
  15.0 4.1 %all-to-all-start.1 = ((f32[4,512,128]{2,1,0:T(8,128)}), f32[4,512,128]{2,1,0:T(8,128)S(1)}, u32[]{:S(2)}, u32[]{:S(2)}) async-start(f32[4,512,128]{2,1,0:T(8,128)} %pad_maximum_fusion), calls=%async_computation.1 | async-start | bytes 2097152 | tf_op jit(solution)/shard_map/all_to_all | solution.py:336
  19.1 4.5 %collective-permute-start = (f32[784,128]{1,0:T(8,128)}, f32[784,128]{1,0:T(8,128)S(1)}, u32[]{:S(2)}, u32[]{:S(2)}) collective-permute-start(f32[784,128]{1,0:T(8,128)} %get-tuple-element.34), channel_id=1, source_target_pairs={{8,20},{9,21},{10,22},{11,23},{12,16},{13,17},{14,18},{15,19},{16,... | collective-permute-start | bytes 1204232 | tf_op jit(solution)/shard_map/ppermute | solution.py:338
  23.7 0.8 maximum_maximum_fusion.1
  24.5 0.9 %pad_maximum_fusion.5 = f32[688,128]{1,0:T(8,128)} fusion(f32[544,128]{1,0:T(8,128)S(1)} %bitcast.56, f32[688]{0:T(1024)S(1)} %pad.22.clone), kind=kLoop, calls=%fused_computation.8 | loop fusion | flops 88064 | bytes 633536 | tf_op jit(solution)/shard_map/concatenate | solution.py:357
  25.4 1.3 %collective-permute-start.1 = (f32[688,128]{1,0:T(8,128)}, f32[688,128]{1,0:T(8,128)S(1)}, u32[]{:S(2)}, u32[]{:S(2)}) collective-permute-start(f32[688,128]{1,0:T(8,128)} %pad_maximum_fusion.5), channel_id=1, source_target_pairs={{0,1},{1,2},{2,3},{4,5},{5,6},{6,7},{8,9},{9,10},{10,11},{12,13},{... | collective-permute-start | bytes 1056776 | tf_op jit(solution)/shard_map/ppermute | solution.py:359
  26.7 1.3 %collective-permute-start.3 = (f32[544,128]{1,0:T(8,128)}, f32[544,128]{1,0:T(8,128)S(1)}, u32[]{:S(2)}, u32[]{:S(2)}) collective-permute-start(f32[544,128]{1,0:T(8,128)} %bitcast.23), channel_id=1, source_target_pairs={{1,0},{2,1},{3,2},{5,4},{6,5},{7,6},{9,8},{10,9},{11,10},{13,12},{... | collective-permute-start | bytes 835592 | tf_op jit(solution)/shard_map/ppermute | solution.py:360
  28.0 0.0 collective-permute-done.2.s0
  28.0 4.1 %collective-permute-done.3.refs_5_ = f32[544,128]{1,0:T(8,128)S(1)} collective-permute-done((f32[544,128]{1,0:T(8,128)}, f32[544,128]{1,0:T(8,128)S(1)}, u32[]{:S(2)}, u32[]{:S(2)}) %collective-permute-start.3) | collective-permute-done | bytes 278560 | tf_op jit(solution)/shard_map/ppermute | solution.py:360
  32.1 1.3 %collective-permute-start.9 = (f32[784,128]{1,0:T(8,128)}, f32[784,128]{1,0:T(8,128)S(1)}, u32[]{:S(2)}, u32[]{:S(2)}) collective-permute-start(f32[784,128]{1,0:T(8,128)} %get-tuple-element.34), channel_id=1, source_target_pairs={{0,20},{1,21},{2,22},{3,23},{4,16},{5,17},{6,18},{7,19},{24,12},{2... | collective-permute-start | bytes 1204232 | tf_op jit(solution)/shard_map/ppermute | solution.py:362
  33.4 0.0 collective-permute-done.1.refs_4_
  33.4 0.7 copy-done
  34.1 0.6 collective-permute-done.s1
  34.7 1.3 %collective-permute-start.8 = (f32[784,128]{1,0:T(8,128)}, f32[784,128]{1,0:T(8,128)S(1)}, u32[]{:S(2)}, u32[]{:S(2)}) collective-permute-start(f32[784,128]{1,0:T(8,128)} %copy-done.4), channel_id=1, source_target_pairs={{0,16},{1,17},{2,18},{3,19},{4,20},{5,21},{6,22},{7,23},{24,8},{25... | collective-permute-start | bytes 1204232 | tf_op jit(solution)/shard_map/ppermute | solution.py:364
  36.0 0.1 pad_add_fusion.refs_0_.side_ref
  36.1 0.1 pad_dynamic-slice_fusion.1
  36.1 0.1 add_select_fusion.refs_1_
  36.2 8.7 %all-to-all-done.1.refs_3_ = f32[4,512,128]{2,1,0:T(8,128)S(1)} async-done(((f32[4,512,128]{2,1,0:T(8,128)}), f32[4,512,128]{2,1,0:T(8,128)S(1)}, u32[]{:S(2)}, u32[]{:S(2)}) %all-to-all-start.1) | async-done | bytes 1048608 | tf_op jit(solution)/shard_map/all_to_all | solution.py:336
  44.9 0.2 broadcast_in_dim.33.refs_6_
  45.1 1.0 %copy-done.1 = f32[688,128]{1,0:T(8,128)S(1)} copy-done((f32[688,128]{1,0:T(8,128)S(1)}, f32[688,128]{1,0:T(8,128)}, u32[]{:S(2)}) %copy-start.1) | copy-done | bytes 352280
  46.1 3.8 %shard_map.46 = (bf16[512,784]{1,0:T(8,128)(2,1)S(1)}, bf16[512,784]{1,0:T(8,128)(2,1)S(1)}, f32[2,2,128,256]{3,2,1,0:T(8,128)S(1)}, f32[2,2,128,256]{3,2,1,0:T(8,128)S(1)}) custom-call(s32[4]{0:T(128)S(1)} %pad_add_fusion.refs_0_.side_ref, f32[2]{0:T(128)S(1)} %add_select_fusion.refs_1_, f32[4,272,128]{2,1,0:T(8,128)S(1)} %all-to-all-done.refs_2_, ...), custom_call_target="tpu_custom_call" | custom-call | flops 1 | bytes 1 | tf_op jit(solution)/shard_map/pallas_call | solution.py:372
  49.9 0.1 collective-permute-start.4
  50.0 0.0 collective-permute-done.9.s2
  50.0 1.7 %shard_map.47 = (f32[512,256]{1,0:T(8,128)S(1)}, f32[512,128]{1,0:T(8,128)S(1)}) custom-call(bf16[512,784]{1,0:T(8,128)(2,1)S(1)} %get-tuple-element.29.high_ref, bf16[512,784]{1,0:T(8,128)(2,1)S(1)} %get-tuple-element.30.low_ref, f32[784,128]{1,0:T(8,128)S(1)} %collective-permute-done.2.s0, f32[784,128]{1,0:T(8,128)S(1)} %collective-permute-done.s1, ...), custom_call_target="tpu_custom_call" | custom-call | flops 1 | bytes 1 | tf_op jit(solution)/shard_map/pallas_call | solution.py:388
  51.7 0.0 collective-permute-done.8.last
  51.7 1.5 %shard_map.48 = (f32[8,128,128]{2,1,0:T(8,128)S(1)}, f32[8,128,128]{2,1,0:T(8,128)S(1)}) custom-call(s32[4]{0:T(128)S(1)} %pad_add_fusion.refs_0_.side_ref, bf16[512,784]{1,0:T(8,128)(2,1)S(1)} %get-tuple-element.29.high_ref, bf16[512,784]{1,0:T(8,128)(2,1)S(1)} %get-tuple-element.30.low_ref, f32[784,128]{1,0:T(8,128)S(1)} %collective-permute-done.8.last, ...), custom_call_target="tpu_custom_call" | custom-call | flops 1 | bytes 1 | tf_op jit(solution)/shard_map/pallas_call | solution.py:396
  53.2 3.6 %collective-permute-start.10 = (f32[8,128,128]{2,1,0:T(8,128)S(1)}, f32[8,128,128]{2,1,0:T(8,128)S(1)}, u32[]{:S(2)}, u32[]{:S(2)}) collective-permute-start(f32[8,128,128]{2,1,0:T(8,128)S(1)} %get-tuple-element.38), channel_id=1, source_target_pairs={{0,1},{1,0},{2,3},{3,2},{4,5},{5,4},{6,7},{7,6},{8,9},{9,8},{10,11... | collective-permute-start | bytes 1572872 | tf_op jit(solution)/shard_map/ppermute | solution.py:384
  56.8 0.0 collective-permute-done.4
  56.8 0.1 add.58
  56.8 1.5 %collective-permute-done.10 = f32[8,128,128]{2,1,0:T(8,128)S(1)} collective-permute-done((f32[8,128,128]{2,1,0:T(8,128)S(1)}, f32[8,128,128]{2,1,0:T(8,128)S(1)}, u32[]{:S(2)}, u32[]{:S(2)}) %collective-permute-start.10) | collective-permute-done | bytes 524320 | tf_op jit(solution)/shard_map/ppermute | solution.py:384
  58.3 0.9 add.66
  59.1 3.5 %all-to-all-start.2 = ((f32[8,128,128]{2,1,0:T(8,128)}), f32[8,128,128]{2,1,0:T(8,128)S(1)}, u32[]{:S(2)}, u32[]{:S(2)}) async-start(f32[8,128,128]{2,1,0:T(8,128)} %add.66), calls=%async_computation.2 | async-start | bytes 1048576 | tf_op jit(solution)/shard_map/all_to_all | solution.py:418
  62.7 0.1 collective-permute-start.5
  62.8 8.5 %collective-permute-done.5 = f32[2,128,256]{2,1,0:T(8,128)S(1)} collective-permute-done((f32[2,128,256]{2,1,0:T(8,128)S(1)}, f32[2,128,256]{2,1,0:T(8,128)S(1)}, u32[]{:S(2)}, u32[]{:S(2)}) %collective-permute-start.5) | collective-permute-done | bytes 262176 | tf_op jit(solution)/shard_map/ppermute | solution.py:407
  71.4 2.0 %collective-permute-start.6 = (f32[128,256]{1,0:T(8,128)S(1)}, f32[128,256]{1,0:T(8,128)S(1)}, u32[]{:S(2)}, u32[]{:S(2)}) collective-permute-start(f32[128,256]{1,0:T(8,128)S(1)} %slice_bitcast_fusion.2), channel_id=1, source_target_pairs={{0,4},{4,0},{1,5},{5,1},{2,6},{6,2},{3,7},{7,3},{8,12},{12,8},{9,1... | collective-permute-start | bytes 393224 | tf_op jit(solution)/shard_map/ppermute | solution.py:408
  73.4 0.0 all-to-all-done.2
  73.4 0.1 copy.16
  73.5 3.1 %collective-permute-start.11 = (f32[128,128]{1,0:T(8,128)S(1)}, f32[128,128]{1,0:T(8,128)S(1)}, u32[]{:S(2)}, u32[]{:S(2)}) collective-permute-start(f32[128,128]{1,0:T(8,128)S(1)} %get-tuple-element.57), channel_id=1, source_target_pairs={{8,16},{9,24},{10,2},{11,3},{12,6},{13,7},{14,20},{15,28},{16,17},... | collective-permute-start | bytes 196616 | tf_op jit(solution)/shard_map/ppermute | solution.py:424
  76.6 1.3 %collective-permute-start.12 = (f32[128,128]{1,0:T(8,128)S(1)}, f32[128,128]{1,0:T(8,128)S(1)}, u32[]{:S(2)}, u32[]{:S(2)}) collective-permute-start(f32[128,128]{1,0:T(8,128)S(1)} %get-tuple-element.58), channel_id=1, source_target_pairs={{8,2},{9,3},{10,20},{11,28},{12,16},{13,24},{14,6},{15,7},{16,10},... | collective-permute-start | bytes 196616 | tf_op jit(solution)/shard_map/ppermute | solution.py:423
  77.9 0.0 collective-permute-done.6
  78.0 1.3 %collective-permute-start.7 = (f32[128,256]{1,0:T(8,128)S(1)}, f32[128,256]{1,0:T(8,128)S(1)}, u32[]{:S(2)}, u32[]{:S(2)}) collective-permute-start(f32[128,256]{1,0:T(8,128)S(1)} %fusion.3), channel_id=1, source_target_pairs={{2,0},{3,1},{6,4},{7,5},{10,8},{11,9},{14,12},{15,13},{16,18},{17,... | collective-permute-start | bytes 393224 | tf_op jit(solution)/shard_map/ppermute | solution.py:416
  79.3 0.0 collective-permute-done.11
  79.3 0.5 collective-permute-done.12
  79.8 5.9 %collective-permute-done.7 = f32[128,256]{1,0:T(8,128)S(1)} collective-permute-done((f32[128,256]{1,0:T(8,128)S(1)}, f32[128,256]{1,0:T(8,128)S(1)}, u32[]{:S(2)}, u32[]{:S(2)}) %collective-permute-start.7) | collective-permute-done | bytes 131104 | tf_op jit(solution)/shard_map/ppermute | solution.py:416
  85.7 0.7 maximum_select_fusion
  (30 shorter events, 0.3 us)
Async XLA Ops:
  2.1 5.1 %copy-start.2 = (f32[3072,128]{1,0:T(8,128)S(1)}, f32[3072,128]{1,0:T(8,128)}, u32[]{:S(2)}) copy-start(f32[3072,128]{1,0:T(8,128)} %param.4) | copy-start | bytes 4718596
  3.0 12.0 %all-to-all-start = ((f32[4,272,128]{2,1,0:T(8,128)}), f32[4,272,128]{2,1,0:T(8,128)S(1)}, u32[]{:S(2)}, u32[]{:S(2)}) async-start(f32[4,272,128]{2,1,0:T(8,128)} %pad_maximum_fusion.4), calls=%async_computation | async-start | bytes 1114112 | tf_op jit(solution)/shard_map/all_to_all | solution.py:335
  7.3 4.1 %copy-start.3 = (f32[3072,128]{1,0:T(8,128)S(1)}, f32[3072,128]{1,0:T(8,128)}, u32[]{:S(2)}) copy-start(f32[3072,128]{1,0:T(8,128)} %param.4) | copy-start | bytes 4718596
  7.4 4.2 %copy-start.5 = (s32[6,512]{1,0:T(8,128)S(1)}, s32[6,512]{1,0:T(8,128)}, u32[]{:S(2)}) copy-start(s32[6,512]{1,0:T(8,128)} %param.5) | copy-start | bytes 36868
  7.4 4.2 %copy-start.6 = (f32[8]{0:T(128)S(1)}, f32[8]{0:T(128)}, u32[]{:S(2)}) copy-start(f32[8]{0:T(128)} %param.6) | copy-start | bytes 100
  8.4 3.6 %copy-start.4 = (f32[784,128]{1,0:T(8,128)}, f32[784,128]{1,0:T(8,128)S(1)}, u32[]{:S(2)}) copy-start(f32[784,128]{1,0:T(8,128)S(1)} %get-tuple-element.31) | copy-start | bytes 1204228
  8.4 19.6 %collective-permute-start.2 = (f32[784,128]{1,0:T(8,128)S(1)}, f32[784,128]{1,0:T(8,128)S(1)}, u32[]{:S(2)}, u32[]{:S(2)}) collective-permute-start(f32[784,128]{1,0:T(8,128)S(1)} %get-tuple-element.31), channel_id=1, source_target_pairs={{8,16},{9,17},{10,18},{11,19},{12,20},{13,21},{14,22},{15,23},{16,... | collective-permute-start | bytes 1204232 | tf_op jit(solution)/shard_map/ppermute | solution.py:324
  15.0 29.9 %all-to-all-start.1 = ((f32[4,512,128]{2,1,0:T(8,128)}), f32[4,512,128]{2,1,0:T(8,128)S(1)}, u32[]{:S(2)}, u32[]{:S(2)}) async-start(f32[4,512,128]{2,1,0:T(8,128)} %pad_maximum_fusion), calls=%async_computation.1 | async-start | bytes 2097152 | tf_op jit(solution)/shard_map/all_to_all | solution.py:336
  19.1 17.0 %copy-start.7 = (f32[2]{0:T(128)S(1)}, f32[2]{0:T(128)}, u32[]{:S(2)}) copy-start(f32[2]{0:T(128)} %constant.57.clone) | copy-start | bytes 28
  19.1 15.6 %collective-permute-start = (f32[784,128]{1,0:T(8,128)}, f32[784,128]{1,0:T(8,128)S(1)}, u32[]{:S(2)}, u32[]{:S(2)}) collective-permute-start(f32[784,128]{1,0:T(8,128)} %get-tuple-element.34), channel_id=1, source_target_pairs={{8,20},{9,21},{10,22},{11,23},{12,16},{13,17},{14,18},{15,19},{16,... | collective-permute-start | bytes 1204232 | tf_op jit(solution)/shard_map/ppermute | solution.py:338
  25.4 8.0 %collective-permute-start.1 = (f32[688,128]{1,0:T(8,128)}, f32[688,128]{1,0:T(8,128)S(1)}, u32[]{:S(2)}, u32[]{:S(2)}) collective-permute-start(f32[688,128]{1,0:T(8,128)} %pad_maximum_fusion.5), channel_id=1, source_target_pairs={{0,1},{1,2},{2,3},{4,5},{5,6},{6,7},{8,9},{9,10},{10,11},{12,13},{... | collective-permute-start | bytes 1056776 | tf_op jit(solution)/shard_map/ppermute | solution.py:359
  26.7 5.4 %collective-permute-start.3 = (f32[544,128]{1,0:T(8,128)}, f32[544,128]{1,0:T(8,128)S(1)}, u32[]{:S(2)}, u32[]{:S(2)}) collective-permute-start(f32[544,128]{1,0:T(8,128)} %bitcast.23), channel_id=1, source_target_pairs={{1,0},{2,1},{3,2},{5,4},{6,5},{7,6},{9,8},{10,9},{11,10},{13,12},{... | collective-permute-start | bytes 835592 | tf_op jit(solution)/shard_map/ppermute | solution.py:360
  32.1 17.9 %collective-permute-start.9 = (f32[784,128]{1,0:T(8,128)}, f32[784,128]{1,0:T(8,128)S(1)}, u32[]{:S(2)}, u32[]{:S(2)}) collective-permute-start(f32[784,128]{1,0:T(8,128)} %get-tuple-element.34), channel_id=1, source_target_pairs={{0,20},{1,21},{2,22},{3,23},{4,16},{5,17},{6,18},{7,19},{24,12},{2... | collective-permute-start | bytes 1204232 | tf_op jit(solution)/shard_map/ppermute | solution.py:362
  33.4 0.7 copy-start
  34.7 17.0 %collective-permute-start.8 = (f32[784,128]{1,0:T(8,128)}, f32[784,128]{1,0:T(8,128)S(1)}, u32[]{:S(2)}, u32[]{:S(2)}) collective-permute-start(f32[784,128]{1,0:T(8,128)} %copy-done.4), channel_id=1, source_target_pairs={{0,16},{1,17},{2,18},{3,19},{4,20},{5,21},{6,22},{7,23},{24,8},{25... | collective-permute-start | bytes 1204232 | tf_op jit(solution)/shard_map/ppermute | solution.py:364
  45.1 1.0 %copy-start.1 = (f32[688,128]{1,0:T(8,128)S(1)}, f32[688,128]{1,0:T(8,128)}, u32[]{:S(2)}) copy-start(f32[688,128]{1,0:T(8,128)} %copy-done) | copy-start | bytes 1056772
  49.9 6.9 %collective-permute-start.4 = (f32[2,2,128,256]{3,2,1,0:T(8,128)S(1)}, f32[2,2,128,256]{3,2,1,0:T(8,128)S(1)}, u32[]{:S(2)}, u32[]{:S(2)}) collective-permute-start(f32[2,2,128,256]{3,2,1,0:T(8,128)S(1)} %get-tuple-element.28), channel_id=1, source_target_pairs={{0,1},{1,0},{2,3},{3,2},{4,5},{5,4},{6,7},{7,6},{8,9},{9,8},{10,11... | collective-permute-start | bytes 1572872 | tf_op jit(solution)/shard_map/ppermute | solution.py:384
  53.2 5.1 %collective-permute-start.10 = (f32[8,128,128]{2,1,0:T(8,128)S(1)}, f32[8,128,128]{2,1,0:T(8,128)S(1)}, u32[]{:S(2)}, u32[]{:S(2)}) collective-permute-start(f32[8,128,128]{2,1,0:T(8,128)S(1)} %get-tuple-element.38), channel_id=1, source_target_pairs={{0,1},{1,0},{2,3},{3,2},{4,5},{5,4},{6,7},{7,6},{8,9},{9,8},{10,11... | collective-permute-start | bytes 1572872 | tf_op jit(solution)/shard_map/ppermute | solution.py:384
  59.1 14.2 %all-to-all-start.2 = ((f32[8,128,128]{2,1,0:T(8,128)}), f32[8,128,128]{2,1,0:T(8,128)S(1)}, u32[]{:S(2)}, u32[]{:S(2)}) async-start(f32[8,128,128]{2,1,0:T(8,128)} %add.66), calls=%async_computation.2 | async-start | bytes 1048576 | tf_op jit(solution)/shard_map/all_to_all | solution.py:418
  62.7 8.6 %collective-permute-start.5 = (f32[2,128,256]{2,1,0:T(8,128)S(1)}, f32[2,128,256]{2,1,0:T(8,128)S(1)}, u32[]{:S(2)}, u32[]{:S(2)}) collective-permute-start(f32[2,128,256]{2,1,0:T(8,128)S(1)} %slice_bitcast_fusion), channel_id=1, source_target_pairs={{0,8},{8,0},{1,9},{9,1},{2,10},{10,2},{3,11},{11,3},{4,12},{12,4},... | collective-permute-start | bytes 786440 | tf_op jit(solution)/shard_map/ppermute | solution.py:407
  71.4 6.6 %collective-permute-start.6 = (f32[128,256]{1,0:T(8,128)S(1)}, f32[128,256]{1,0:T(8,128)S(1)}, u32[]{:S(2)}, u32[]{:S(2)}) collective-permute-start(f32[128,256]{1,0:T(8,128)S(1)} %slice_bitcast_fusion.2), channel_id=1, source_target_pairs={{0,4},{4,0},{1,5},{5,1},{2,6},{6,2},{3,7},{7,3},{8,12},{12,8},{9,1... | collective-permute-start | bytes 393224 | tf_op jit(solution)/shard_map/ppermute | solution.py:408
  73.5 5.8 %collective-permute-start.11 = (f32[128,128]{1,0:T(8,128)S(1)}, f32[128,128]{1,0:T(8,128)S(1)}, u32[]{:S(2)}, u32[]{:S(2)}) collective-permute-start(f32[128,128]{1,0:T(8,128)S(1)} %get-tuple-element.57), channel_id=1, source_target_pairs={{8,16},{9,24},{10,2},{11,3},{12,6},{13,7},{14,20},{15,28},{16,17},... | collective-permute-start | bytes 196616 | tf_op jit(solution)/shard_map/ppermute | solution.py:424
  76.6 3.2 %collective-permute-start.12 = (f32[128,128]{1,0:T(8,128)S(1)}, f32[128,128]{1,0:T(8,128)S(1)}, u32[]{:S(2)}, u32[]{:S(2)}) collective-permute-start(f32[128,128]{1,0:T(8,128)S(1)} %get-tuple-element.58), channel_id=1, source_target_pairs={{8,2},{9,3},{10,20},{11,28},{12,16},{13,24},{14,6},{15,7},{16,10},... | collective-permute-start | bytes 196616 | tf_op jit(solution)/shard_map/ppermute | solution.py:423
  78.0 7.7 %collective-permute-start.7 = (f32[128,256]{1,0:T(8,128)S(1)}, f32[128,256]{1,0:T(8,128)S(1)}, u32[]{:S(2)}, u32[]{:S(2)}) collective-permute-start(f32[128,256]{1,0:T(8,128)S(1)} %fusion.3), channel_id=1, source_target_pairs={{2,0},{3,1},{6,4},{7,5},{10,8},{11,9},{14,12},{15,13},{16,18},{17,... | collective-permute-start | bytes 393224 | tf_op jit(solution)/shard_map/ppermute | solution.py:416
